TPU v7x, 32 devices: a whole 2x2x4 slice. The times are simulated.
32 devices in a mesh: seq: 8 (over z, x), head: 4 (over y, core).
Axes of the slice: x: 2, y: 2, z: 4, core: 2. Of those that a mesh axis runs over, the one named last changes fastest.
Arguments:
- hidden: bfloat16 [2, 4096, 1536], P(None, 'seq', 'head'), may hold values from -6 to 6
- output_grad: bfloat16 [2, 4096, 1536], P(None, 'seq', 'head'), may hold values from -6 to 6
- lengths: int32 [2, 4], replicated, may hold values from 1 to 3840, 4096 in all within a row
- seq_order: int32 [2, 4], replicated, may hold values from 0 to 3, each once within a row
- routes: int32 [2, 4096, 6], P(None, 'seq'), may hold values from 0 to 31, all different within a row; in each aligned block of 512 rows (0 to 511, 512 to 1023, ..., all dimensions but the last counted through in order) at most 192 rows name the same one
- mix_gain: float32 [1536], P('head'), may hold values from 0.5 to 1.5
- input_proj: bfloat16 [2, 1536, 3072], P(None, 'seq', 'head'), may hold values from -0.15309311 to 0.15309311
- state_proj: bfloat16 [1536, 256], P('seq'), may hold values from -0.15309311 to 0.15309311
- step_proj: bfloat16 [1536, 48], P('seq', 'head'), may hold values from -0.15309311 to 0.15309311
- conv_inner: float32 [4, 3072], P(None, 'head'), may hold values from -3 to 3
- conv_state: float32 [4, 256], replicated, may hold values from -3 to 3
- inner_bias: float32 [3072], P('head'), may hold values from -1.2 to 1.2
- state_bias: float32 [256], replicated, may hold values from -1.2 to 1.2
- step_bias: float32 [48], P('head'), may hold values from -2 to 0.5
- decay_rate: float32 [48], P('head'), may hold values from 6.1035156e-05 to 0.08
- skip_gain: float32 [48], P('head'), may hold values from 0.5 to 1.5
- gate_gain: float32 [3072], P('head'), may hold values from 0.5 to 1.5
- output_proj: bfloat16 [3072, 1536], P('head', 'seq'), may hold values from -0.108253175 to 0.108253175
- moe_gain: float32 [1536], P('head'), may hold values from 0.5 to 1.5
- router: bfloat16 [1536, 32], P('seq'), may hold values from -0.076546554 to 0.076546554
- expert_up: bfloat16 [32, 1536, 1024], P('head', 'seq'), may hold values from -0.15309311 to 0.15309311
- expert_down: bfloat16 [32, 512, 1536], P('head', None, 'seq'), may hold values from -0.53033009 to 0.53033009
- shared_up: bfloat16 [1536, 2, 1024], P('seq', None, 'head'), may hold values from -0.15309311 to 0.15309311
- shared_down: bfloat16 [1024, 1536], P('head', 'seq'), may hold values from -0.1875 to 0.1875
Outputs:
- output: bfloat16 [2, 4096, 1536], P(None, 'seq', 'head')
- hidden_grad: float32 [2, 4096, 1536], P(None, 'seq', 'head')
- mix_gain_grad: float32 [1536], P('head')
- input_proj_grad: float32 [2, 1536, 3072], P(None, 'seq', 'head')
- state_proj_grad: float32 [1536, 256], P('seq')
- step_proj_grad: float32 [1536, 48], P('seq', 'head')
- conv_inner_grad: float32 [4, 3072], P(None, 'head')
- conv_state_grad: float32 [4, 256], replicated
- inner_bias_grad: float32 [3072], P('head')
- state_bias_grad: float32 [256], replicated
- step_bias_grad: float32 [48], P('head')
- decay_rate_grad: float32 [48], P('head')
- skip_gain_grad: float32 [48], P('head')
- gate_gain_grad: float32 [3072], P('head')
- output_proj_grad: float32 [3072, 1536], P('head', 'seq')
- moe_gain_grad: float32 [1536], P('head')
- router_grad: float32 [1536, 32], P('seq')
- expert_up_grad: float32 [32, 1536, 1024], P('head', 'seq')
- expert_down_grad: float32 [32, 512, 1536], P('head', None, 'seq')
- shared_up_grad: float32 [1536, 2, 1024], P('seq', None, 'head')
- shared_down_grad: float32 [1024, 1536], P('head', 'seq')
Inputs may be any that keep to these rules, and one draw needn't show every extreme that they name: The 4 lengths of a micro-batch sum to 4096, and the largest is 3840. Each row names each of the 4 sequences once; seq_order[m, k] is the sequence packed k-th in micro-batch m. `routes`: A token's 6 experts are distinct. In each aligned block of 512 rows of a micro-batch (the rows of one index of seq) no expert is named by more than 192 rows, a bound that some block reaches.
All inputs are finite; a program needn't handle non-finite values.
Results may differ from a plain program's by a relative error of at most 0.03.
Values may be sent and summed in bfloat16 or wider, within the bound.
A program may use at most 320 MiB of HBM per device.

v0:
```python
from functools import partial

import jax
import jax.numpy as jnp
from jax import lax
from jax.sharding import PartitionSpec as P

D = 1536
HEAD_DIM = 64
STATE = 128
CONV = 4
TOPK = 6
EFF = 512
GROUP = 256
INNER = 3072


EPSILON = 1e-05
HIGHEST = lax.Precision.HIGHEST


def passed_along(value, axis, steps):
    count = lax.axis_size(axis)
    leading, last = (max(0, -steps), min(count, count - steps))
    return lax.ppermute(value, axis, [(source, source + steps) for source in range(leading, last)])


def carried_in(part, axis, combine, identity):
    place = lax.axis_index(axis)
    gathered = jax.tree.map(lambda a: lax.all_gather(a, axis), part)
    state = jax.tree.map(lambda a, e: jnp.zeros_like(a) + jnp.asarray(e, a.dtype), part, identity)

    def carried_one(step, state):
        return combine(
            state, jax.tree.map(lambda a: lax.dynamic_index_in_dim(a, step, 0, False), gathered)
        )

    return lax.fori_loop(0, place, carried_one, state)


def prefix(value, axis, join, neutral):
    count = lax.axis_size(axis)
    place = lax.axis_index(axis)
    ahead = count - 1 - place
    gathered = jax.tree.map(
        lambda a, kind: lax.all_gather(a.astype(kind), axis),
        value,
        jax.tree.map(lambda a: jnp.bfloat16 if a.dtype == jnp.float32 else a.dtype, value),
    )
    state = jax.tree.map(lambda a, e: jnp.zeros_like(a) + jnp.asarray(e, a.dtype), value, neutral)

    def prefix_one(step, state):
        source = count - 1 - step
        return join(
            state,
            jax.tree.map(
                lambda a, own: lax.dynamic_index_in_dim(a, source, 0, False).astype(own.dtype),
                gathered,
                value,
            ),
        )

    return lax.fori_loop(0, ahead, prefix_one, state)


def squash_slope(values):
    logistic = jax.nn.sigmoid(values)
    return logistic * (1.0 + values * (1.0 - logistic))


def segment_numbers(length_row, order_row, positions):
    seq_count = length_row.shape[0]
    seq_index = jnp.arange(seq_count, dtype=jnp.int32)
    picked = (order_row[:, None] == seq_index[None, :]).astype(jnp.int32)
    placed = jnp.sum(picked * length_row[None, :], axis=1)
    earlier = (seq_index[:, None] > seq_index[None, :]).astype(jnp.int32)
    begins = jnp.sum(earlier * placed[None, :], axis=1)
    return jnp.sum((begins[None, :] <= positions[:, None]).astype(jnp.int32), axis=1)


def conv_extended(padded, conv_weight, conv_offset, segment_padded):
    conv_taps = conv_weight.shape[0]
    length = padded.shape[0] - (conv_taps - 1)
    current = segment_padded[conv_taps - 1 :]
    summed = conv_offset + padded[conv_taps - 1 :] * conv_weight[0]
    for offset in range(1, conv_taps):
        begin_at = conv_taps - 1 - offset
        keep_mask = (segment_padded[begin_at : begin_at + length] == current).astype(jnp.float32)
        summed = (
            summed + padded[begin_at : begin_at + length] * conv_weight[offset] * keep_mask[:, None]
        )
    return summed


def prepare_inputs(
    padded, conv_weight, conv_offset, step_raw, step_bias, decay_rate, segment_padded
):
    activated = jax.nn.silu(conv_extended(padded, conv_weight, conv_offset, segment_padded))
    length = activated.shape[0]
    inner_width = activated.shape[1] - 2 * STATE
    head_number = step_raw.shape[1]
    signal = activated[:, :inner_width].reshape(length, head_number, inner_width // head_number)
    write_keys = activated[:, inner_width : inner_width + STATE]
    read_keys = activated[:, inner_width + STATE :]
    step_sizes = jax.nn.softplus(step_raw + step_bias)
    return (signal, write_keys, read_keys, step_sizes, -step_sizes * decay_rate)


def ssd_block(carry_state, block_in):
    signal, write_keys, read_keys, step_sizes, log_decay, segments, segment_before = block_in
    length = log_decay.shape[0]
    row_index = jnp.arange(length, dtype=jnp.int32)
    lower_ones = (row_index[:, None] >= row_index[None, :]).astype(jnp.float32)
    running = jnp.einsum("ij,jh->ih", lower_ones, log_decay, precision=HIGHEST)
    within = (row_index[:, None] >= row_index[None, :]) & (segments[:, None] == segments[None, :])
    spread = running[:, None, :] - running[None, :, :]
    decays = jnp.where(within[:, :, None], jnp.exp(jnp.where(within[:, :, None], spread, 0.0)), 0.0)
    scores = jnp.einsum("in,jn->ij", read_keys, write_keys, precision=HIGHEST)
    mixing = decays * scores[:, :, None] * step_sizes[None, :, :]
    local_out = jnp.einsum("ijh,jhp->ihp", mixing, signal, precision=HIGHEST)
    carried = jnp.where((segments == segment_before)[:, None], jnp.exp(running), 0.0)
    from_state = (
        jnp.einsum("in,hpn->ihp", read_keys, carry_state, precision=HIGHEST) * carried[:, :, None]
    )
    last_keep = (
        jnp.where((segments == segments[-1])[:, None], jnp.exp(running[-1][None, :] - running), 0.0)
        * step_sizes
    )
    through = jnp.where(segments[-1] == segment_before, jnp.exp(running[-1]), 0.0)
    new_state = carry_state * through[:, None, None] + jnp.einsum(
        "jh,jhp,jn->hpn", last_keep, signal, write_keys, precision=HIGHEST
    )
    return (new_state, local_out + from_state)


def scan_device(
    signal,
    write_keys,
    read_keys,
    step_sizes,
    log_decay,
    skip_gain,
    carry_in,
    segments,
    segment_before,
):
    length, head_number, head_width = signal.shape
    blocks = length // GROUP
    before = jnp.concatenate([segment_before[None], segments[:-1]]).reshape(blocks, GROUP)[:, 0]
    block_parts = (
        signal.reshape(blocks, GROUP, head_number, head_width),
        write_keys.reshape(blocks, GROUP, STATE),
        read_keys.reshape(blocks, GROUP, STATE),
        step_sizes.reshape(blocks, GROUP, head_number),
        log_decay.reshape(blocks, GROUP, head_number),
        segments.reshape(blocks, GROUP),
        before,
    )
    carry_out, mixed_out = lax.scan(jax.checkpoint(ssd_block), carry_in, block_parts)
    return (
        mixed_out.reshape(length, head_number, head_width) + skip_gain[None, :, None] * signal,
        carry_out,
    )


def prefix_rows(log_decay):
    length, head_number = log_decay.shape
    blocks = length // GROUP
    shaped = log_decay.reshape(blocks, GROUP, head_number)
    row_index = jnp.arange(GROUP, dtype=jnp.int32)
    lower_ones = (row_index[:, None] >= row_index[None, :]).astype(jnp.float32)
    within = jnp.einsum("ij,bjh->bih", lower_ones, shaped, precision=HIGHEST)
    block_ends = within[:, -1, :]
    before = jnp.cumsum(block_ends, axis=0) - block_ends
    return (within + before[:, None, :]).reshape(length, head_number)


def slot_table(route_rows, first_expert, expert_count, capacity):
    pair_count = route_rows.shape[0] * route_rows.shape[1]
    flat_local = route_rows.reshape(-1) - first_expert
    matches = (flat_local[:, None] == jnp.arange(expert_count, dtype=jnp.int32)[None, :]).astype(
        jnp.int32
    )
    slot_ranks = jnp.sum((jnp.cumsum(matches, axis=0) - 1) * matches, axis=1)
    inside = (flat_local >= 0) & (flat_local < expert_count)
    target = jnp.where(inside, flat_local * capacity + slot_ranks, expert_count * capacity)
    empty_table = jnp.full((expert_count * capacity,), pair_count, jnp.int32)
    return empty_table.at[target].set(jnp.arange(pair_count, dtype=jnp.int32), mode="drop")


def chain_step(earlier_part, later_part):
    return (
        earlier_part[0] * later_part[0],
        later_part[0][:, None, None] * earlier_part[1] + later_part[1],
    )


def head_total(values):
    return lax.psum(values, "head")


def rows_gather(shard_rows):
    return lax.all_gather(shard_rows, "head", axis=1, tiled=True)


def rows_reduce(partial_rows):
    return lax.psum_scatter(partial_rows, "head", scatter_dimension=1, tiled=True)


def grads_gather(shard_rows):
    return lax.all_gather(shard_rows, "head", axis=1, tiled=True)


def grads_reduce(partial_rows):
    return lax.psum_scatter(
        partial_rows.astype(jnp.bfloat16), "head", scatter_dimension=1, tiled=True
    ).astype(jnp.float32)


def fetch_weights(shards):
    return (
        lax.all_gather(shards[0], "seq", axis=1, tiled=True),
        lax.all_gather(shards[1], "seq", axis=0, tiled=True),
        lax.all_gather(shards[2], "seq", axis=0, tiled=True),
        lax.all_gather(shards[3], "seq", axis=1, tiled=True),
        lax.all_gather(shards[4], "seq", axis=0, tiled=True),
        lax.all_gather(shards[5], "seq", axis=1, tiled=True),
        lax.all_gather(shards[6], "seq", axis=2, tiled=True),
        lax.all_gather(shards[7], "seq", axis=0, tiled=True),
        lax.all_gather(shards[8], "seq", axis=1, tiled=True),
    )


def reduce_weights(matrices, smalls):
    summed = (
        lax.psum_scatter(
            matrices[0].astype(jnp.bfloat16), "seq", scatter_dimension=1, tiled=True
        ).astype(jnp.float32),
        lax.psum_scatter(
            matrices[1].astype(jnp.bfloat16), "seq", scatter_dimension=0, tiled=True
        ).astype(jnp.float32),
        lax.psum_scatter(
            matrices[2].astype(jnp.bfloat16), "seq", scatter_dimension=0, tiled=True
        ).astype(jnp.float32),
        lax.psum_scatter(
            matrices[3].astype(jnp.bfloat16), "seq", scatter_dimension=1, tiled=True
        ).astype(jnp.float32),
        lax.psum_scatter(
            matrices[4].astype(jnp.bfloat16), "seq", scatter_dimension=0, tiled=True
        ).astype(jnp.float32),
        lax.psum_scatter(
            matrices[5].astype(jnp.bfloat16), "seq", scatter_dimension=1, tiled=True
        ).astype(jnp.float32),
        lax.psum_scatter(
            matrices[6].astype(jnp.bfloat16), "seq", scatter_dimension=2, tiled=True
        ).astype(jnp.float32),
        lax.psum_scatter(
            matrices[7].astype(jnp.bfloat16), "seq", scatter_dimension=0, tiled=True
        ).astype(jnp.float32),
        lax.psum_scatter(
            matrices[8].astype(jnp.bfloat16), "seq", scatter_dimension=1, tiled=True
        ).astype(jnp.float32),
    )
    small_totals = lax.psum(
        (
            smalls[0],
            smalls[1],
            smalls[2],
            smalls[3],
            smalls[4],
            smalls[5],
            smalls[6],
            smalls[7],
            smalls[8],
            smalls[9],
        ),
        "seq",
    )
    return (summed, small_totals)


def norm_forward(shard_rows, norm_gain, feature_count):
    squares = head_total(jnp.sum(shard_rows * shard_rows, axis=1))
    norm_scale = lax.rsqrt(squares / feature_count + EPSILON)
    return ((shard_rows * norm_scale[:, None] * norm_gain).astype(jnp.bfloat16), norm_scale)


def norm_backward(grad_out, shard_rows, norm_gain, norm_scale, feature_count):
    weighted = grad_out * norm_gain
    products = head_total(jnp.sum(weighted * shard_rows, axis=1))
    cubed = norm_scale * norm_scale * norm_scale
    grad_in = (
        norm_scale[:, None] * weighted - shard_rows * (cubed * products / feature_count)[:, None]
    )
    gain_grad = jnp.sum(grad_out * shard_rows * norm_scale[:, None], axis=0)
    return (grad_in, gain_grad)


def body(
    hidden,
    output_grad,
    lengths,
    seq_order,
    routes,
    mix_gain,
    input_proj,
    state_proj,
    step_proj,
    conv_inner,
    conv_state,
    inner_bias,
    state_bias,
    step_bias,
    decay_rate,
    skip_gain,
    gate_gain,
    output_proj,
    moe_gain,
    router,
    expert_up,
    expert_down,
    shared_up,
    shared_down,
):
    seq_rank = lax.axis_index("seq")
    head_rank = lax.axis_index("head")
    head_count = lax.axis_size("head")
    micro_count, tokens, local_width = hidden.shape
    inner_local = conv_inner.shape[1]
    heads_local = step_bias.shape[0]
    experts_local = expert_up.shape[0]
    shared_local = shared_down.shape[0]
    capacity = 2 * tokens * TOPK // (experts_local * head_count)
    feature_start = head_rank * local_width
    positions = seq_rank * tokens + jnp.arange(1 - CONV, tokens, dtype=jnp.int32)
    conv_weight = jnp.concatenate([conv_inner, conv_state], axis=1)
    conv_offset = jnp.concatenate([inner_bias, state_bias])
    shard_list = (
        input_proj,
        step_proj,
        state_proj,
        output_proj,
        router,
        expert_up,
        expert_down,
        shared_up,
        shared_down,
    )
    outputs = []
    input_grads = []
    matrix_sums = None
    small_sums = None
    for micro_index in range(micro_count):
        full_weights = fetch_weights(shard_list)
        (
            proj_full,
            step_full,
            state_full,
            out_full,
            router_full,
            up_full,
            down_full,
            shared_up_full,
            shared_down_full,
        ) = full_weights
        segment_wide = segment_numbers(lengths[micro_index], seq_order[micro_index], positions)
        segments = segment_wide[CONV - 1 :]
        segment_before = segment_wide[CONV - 2]
        resid_in = hidden[micro_index].astype(jnp.float32)
        normed_shard, scale_mix = norm_forward(resid_in, mix_gain, D)
        normed = rows_gather(normed_shard)
        gate_pre = jnp.dot(normed, proj_full[0], preferred_element_type=jnp.float32)
        inner_pre = jnp.dot(normed, proj_full[1], preferred_element_type=jnp.float32)
        state_pre = jnp.dot(normed, state_full, preferred_element_type=jnp.float32)
        step_raw = jnp.dot(normed, step_full, preferred_element_type=jnp.float32)
        conv_in = jnp.concatenate([inner_pre, state_pre], axis=1)
        edge_rows = passed_along(conv_in[tokens - (CONV - 1) :], "seq", 1)
        padded = jnp.concatenate([edge_rows, conv_in], axis=0)
        prepared, prepare_back = jax.vjp(
            partial(prepare_inputs, segment_padded=segment_wide),
            padded,
            conv_weight,
            conv_offset,
            step_raw,
            step_bias,
            decay_rate,
        )
        signal, write_keys, read_keys, step_sizes, log_decay = prepared
        zero_state = jnp.zeros((heads_local, HEAD_DIM, STATE), jnp.float32)
        local_out, local_state = scan_device(
            signal,
            write_keys,
            read_keys,
            step_sizes,
            log_decay,
            skip_gain,
            zero_state,
            segments,
            segment_before,
        )
        running = prefix_rows(log_decay)
        entry_weight = jnp.where((segments == segment_before)[:, None], jnp.exp(running), 0.0)
        passing = jnp.where(segments[-1] == segment_before, jnp.exp(running[-1]), 0.0)
        incoming = carried_in(
            (passing, local_state),
            "seq",
            chain_step,
            (jnp.ones_like(passing), jnp.zeros_like(local_state)),
        )
        state_in = incoming[1]
        mixer_out = local_out + entry_weight[:, :, None] * jnp.einsum(
            "tn,hpn->thp", read_keys, state_in, precision=HIGHEST
        )
        gate_act = jax.nn.silu(gate_pre)
        mixer_flat = mixer_out.reshape(tokens, inner_local)
        gated_rows = mixer_flat * gate_act
        gate_normed, scale_gate = norm_forward(gated_rows, gate_gain, INNER)
        mix_shard = rows_reduce(jnp.dot(gate_normed, out_full, preferred_element_type=jnp.float32))
        resid_mid = resid_in + mix_shard
        moe_shard, scale_moe = norm_forward(resid_mid, moe_gain, D)
        moe_normed = rows_gather(moe_shard)
        logits = jnp.dot(moe_normed, router_full, preferred_element_type=jnp.float32)
        route_rows = routes[micro_index]
        expert_ids = jnp.arange(router_full.shape[1], dtype=jnp.int32)
        choose = (route_rows[:, :, None] == expert_ids[None, None, :]).astype(jnp.float32)
        gate_weights = jax.nn.softmax(jnp.sum(choose * logits[:, None, :], axis=2), axis=1)
        slot_pairs = slot_table(route_rows, head_rank * experts_local, experts_local, capacity)
        filled = slot_pairs < tokens * TOPK
        safe_pair = jnp.where(filled, slot_pairs, 0)
        token_ids = safe_pair // TOPK
        slot_gate = jnp.where(filled, jnp.take(gate_weights.reshape(-1), safe_pair), 0.0).reshape(
            experts_local, capacity
        )
        slot_rows = jnp.take(moe_normed, token_ids, axis=0).reshape(experts_local, capacity, D)
        gate_up = jnp.einsum("ecd,edf->ecf", slot_rows, up_full, preferred_element_type=jnp.float32)
        up_gate = gate_up[:, :, :EFF]
        up_linear = gate_up[:, :, EFF:]
        hidden_act = (jax.nn.silu(up_gate) * up_linear).astype(jnp.bfloat16)
        expert_out = jnp.einsum(
            "ecf,efd->ecd", hidden_act, down_full, preferred_element_type=jnp.float32
        )
        combined = (
            jnp.zeros((tokens, D), jnp.float32)
            .at[token_ids]
            .add((expert_out * slot_gate[:, :, None]).reshape(-1, D))
        )
        shared_flat = shared_up_full.reshape(D, 2 * shared_local)
        shared_both = jnp.dot(moe_normed, shared_flat, preferred_element_type=jnp.float32)
        shared_gate = shared_both[:, :shared_local]
        shared_linear = shared_both[:, shared_local:]
        shared_act = (jax.nn.silu(shared_gate) * shared_linear).astype(jnp.bfloat16)
        combined = combined + jnp.dot(
            shared_act, shared_down_full, preferred_element_type=jnp.float32
        )
        ffn_shard = rows_reduce(combined)
        outputs.append((resid_mid + ffn_shard).astype(jnp.bfloat16))
        held_shards = lax.optimization_barrier((shard_list, outputs[-1]))[0]
        full_weights = fetch_weights(held_shards)
        (
            proj_full,
            step_full,
            state_full,
            out_full,
            router_full,
            up_full,
            down_full,
            shared_up_full,
            shared_down_full,
        ) = full_weights
        shared_flat = shared_up_full.reshape(D, 2 * shared_local)
        grad_ffn = grads_gather(output_grad[micro_index])
        shared_grad_act = jnp.einsum(
            "td,fd->tf", grad_ffn, shared_down_full, preferred_element_type=jnp.float32
        )
        shared_grad_both = jnp.concatenate(
            [
                shared_grad_act * shared_linear * squash_slope(shared_gate),
                shared_grad_act * jax.nn.silu(shared_gate),
            ],
            axis=1,
        ).astype(jnp.bfloat16)
        grad_shared_down = jnp.einsum(
            "tf,td->fd", shared_act, grad_ffn, preferred_element_type=jnp.float32
        )
        grad_shared_up = jnp.einsum(
            "td,tf->df", moe_normed, shared_grad_both, preferred_element_type=jnp.float32
        ).reshape(D, 2, shared_local)
        grad_normed = jnp.einsum(
            "tf,df->td", shared_grad_both, shared_flat, preferred_element_type=jnp.float32
        )
        slot_grad = jnp.take(grad_ffn, token_ids, axis=0).reshape(experts_local, capacity, D)
        slot_gate_grad = jnp.sum(slot_grad.astype(jnp.float32) * expert_out, axis=2)
        grad_expert_out = (slot_gate[:, :, None] * slot_grad).astype(jnp.bfloat16)
        grad_hidden = jnp.einsum(
            "ecd,efd->ecf", grad_expert_out, down_full, preferred_element_type=jnp.float32
        )
        grad_down = jnp.einsum(
            "ecf,ecd->efd", hidden_act, grad_expert_out, preferred_element_type=jnp.float32
        )
        grad_gate_up = jnp.concatenate(
            [grad_hidden * up_linear * squash_slope(up_gate), grad_hidden * jax.nn.silu(up_gate)],
            axis=2,
        ).astype(jnp.bfloat16)
        grad_up = jnp.einsum(
            "ecd,ecf->edf", slot_rows, grad_gate_up, preferred_element_type=jnp.float32
        )
        grad_rows = jnp.einsum(
            "ecf,edf->ecd", grad_gate_up, up_full, preferred_element_type=jnp.float32
        )
        grad_normed = grad_normed.at[token_ids].add(grad_rows.reshape(-1, D))
        pair_grad = (
            jnp.zeros((tokens * TOPK,), jnp.float32)
            .at[slot_pairs]
            .add(slot_gate_grad.reshape(-1), mode="drop")
        )
        gate_grad = lax.psum(pair_grad.reshape(tokens, TOPK), "head")
        pick_grad = gate_weights * (
            gate_grad - jnp.sum(gate_weights * gate_grad, axis=1, keepdims=True)
        )
        logit_grad = jnp.sum(pick_grad[:, :, None] * choose, axis=1).astype(jnp.bfloat16)
        grad_router = jnp.einsum(
            "td,te->de", moe_normed, logit_grad, preferred_element_type=jnp.float32
        )
        router_rows = lax.dynamic_slice_in_dim(router_full, feature_start, local_width, 0)
        moe_grad_shard = grads_reduce(grad_normed) + jnp.einsum(
            "te,de->td", logit_grad, router_rows, preferred_element_type=jnp.float32
        )
        grad_mid, grad_moe_gain = norm_backward(moe_grad_shard, resid_mid, moe_gain, scale_moe, D)
        grad_mid = grad_mid + output_grad[micro_index].astype(jnp.float32)
        grad_mix = grads_gather(grad_mid.astype(jnp.bfloat16))
        grad_out_proj = jnp.einsum(
            "tc,td->cd", gate_normed, grad_mix, preferred_element_type=jnp.float32
        )
        grad_gate_normed = jnp.einsum(
            "td,cd->tc", grad_mix, out_full, preferred_element_type=jnp.float32
        )
        grad_gated, grad_gate_gain = norm_backward(
            grad_gate_normed, gated_rows, gate_gain, scale_gate, INNER
        )
        grad_mixer = (grad_gated * gate_act).reshape(tokens, heads_local, HEAD_DIM)
        grad_gate_pre = grad_gated * mixer_flat * squash_slope(gate_pre)
        entry_grad = jnp.einsum(
            "th,thp,tn->hpn", entry_weight, grad_mixer, read_keys, precision=HIGHEST
        )
        outgoing = prefix(
            (passing, entry_grad),
            "seq",
            chain_step,
            (jnp.ones_like(passing), jnp.zeros_like(entry_grad)),
        )
        scan_local = partial(scan_device, segments=segments, segment_before=segment_before)
        unused, scan_back = jax.vjp(
            scan_local, signal, write_keys, read_keys, step_sizes, log_decay, skip_gain, state_in
        )
        grad_signal, grad_write, grad_read, grad_steps, grad_log, grad_skip, unused_state = (
            scan_back((grad_mixer, outgoing[1]))
        )
        (
            grad_padded,
            grad_conv_weight,
            grad_conv_offset,
            grad_step_raw,
            grad_step_bias,
            grad_decay,
        ) = prepare_back((grad_signal, grad_write, grad_read, grad_steps, grad_log))
        head_summed = (
            lax.psum(grad_padded[:, inner_local:].astype(jnp.bfloat16), "head").astype(jnp.float32),
            lax.psum(grad_conv_weight[:, inner_local:].astype(jnp.bfloat16), "head").astype(
                jnp.float32
            ),
            lax.psum(grad_conv_offset[inner_local:].astype(jnp.bfloat16), "head").astype(
                jnp.float32
            ),
        )
        grad_padded = jnp.concatenate([grad_padded[:, :inner_local], head_summed[0]], axis=1)
        edge_back = passed_along(grad_padded[: CONV - 1], "seq", -1)
        grad_conv_in = grad_padded[CONV - 1 :]
        grad_conv_in = grad_conv_in.at[tokens - (CONV - 1) :].add(edge_back)
        grad_inner_low = grad_conv_in[:, :inner_local].astype(jnp.bfloat16)
        grad_state_low = grad_conv_in[:, inner_local:].astype(jnp.bfloat16)
        grad_gate_low = grad_gate_pre.astype(jnp.bfloat16)
        grad_step_low = grad_step_raw.astype(jnp.bfloat16)
        grad_proj = jnp.stack(
            [
                jnp.einsum("td,tc->dc", normed, grad_gate_low, preferred_element_type=jnp.float32),
                jnp.einsum("td,tc->dc", normed, grad_inner_low, preferred_element_type=jnp.float32),
            ]
        )
        grad_state_proj = jnp.einsum(
            "td,tc->dc", normed, grad_state_low, preferred_element_type=jnp.float32
        )
        grad_step_proj = jnp.einsum(
            "td,tc->dc", normed, grad_step_low, preferred_element_type=jnp.float32
        )
        grad_first = jnp.einsum(
            "tc,dc->td", grad_gate_low, proj_full[0], preferred_element_type=jnp.float32
        )
        grad_first = grad_first + jnp.einsum(
            "tc,dc->td", grad_inner_low, proj_full[1], preferred_element_type=jnp.float32
        )
        grad_first = grad_first + jnp.einsum(
            "tc,dc->td", grad_step_low, step_full, preferred_element_type=jnp.float32
        )
        state_rows = lax.dynamic_slice_in_dim(state_full, feature_start, local_width, 0)
        first_grad_shard = grads_reduce(grad_first) + jnp.einsum(
            "tc,dc->td", grad_state_low, state_rows, preferred_element_type=jnp.float32
        )
        grad_in, grad_mix_gain = norm_backward(first_grad_shard, resid_in, mix_gain, scale_mix, D)
        input_grads.append(grad_in + grad_mid)
        matrix_grads = (
            grad_proj,
            grad_step_proj,
            grad_state_proj,
            grad_out_proj,
            grad_router,
            grad_up,
            grad_down,
            grad_shared_up,
            grad_shared_down,
        )
        small_grads = (
            grad_mix_gain,
            grad_conv_weight[:, :inner_local],
            head_summed[1],
            grad_conv_offset[:inner_local],
            head_summed[2],
            grad_step_bias,
            grad_decay,
            grad_skip,
            grad_gate_gain,
            grad_moe_gain,
        )
        reduced = reduce_weights(matrix_grads, small_grads)
        matrix_sums = (
            reduced[0] if matrix_sums is None else jax.tree.map(jnp.add, matrix_sums, reduced[0])
        )
        small_sums = (
            reduced[1] if small_sums is None else jax.tree.map(jnp.add, small_sums, reduced[1])
        )
    return (
        jnp.stack(outputs),
        jnp.stack(input_grads),
        small_sums[0],
        matrix_sums[0],
        matrix_sums[2],
        matrix_sums[1],
        small_sums[1],
        small_sums[2],
        small_sums[3],
        small_sums[4],
        small_sums[5],
        small_sums[6],
        small_sums[7],
        small_sums[8],
        matrix_sums[3],
        small_sums[9],
        matrix_sums[4],
        matrix_sums[5],
        matrix_sums[6],
        matrix_sums[7],
        matrix_sums[8],
    )


def solution(mesh):
    return jax.shard_map(
        body,
        mesh=mesh,
        in_specs=(
            P(None, "seq", "head"),
            P(None, "seq", "head"),
            P(),
            P(),
            P(None, "seq", None),
            P("head"),
            P(None, "seq", "head"),
            P("seq", None),
            P("seq", "head"),
            P(None, "head"),
            P(),
            P("head"),
            P(),
            P("head"),
            P("head"),
            P("head"),
            P("head"),
            P("head", "seq"),
            P("head"),
            P("seq", None),
            P("head", "seq", None),
            P("head", None, "seq"),
            P("seq", None, "head"),
            P("head", "seq"),
        ),
        out_specs=(
            P(None, "seq", "head"),
            P(None, "seq", "head"),
            P("head"),
            P(None, "seq", "head"),
            P("seq", None),
            P("seq", "head"),
            P(None, "head"),
            P(),
            P("head"),
            P(),
            P("head"),
            P("head"),
            P("head"),
            P("head"),
            P("head", "seq"),
            P("head"),
            P("seq", None),
            P("head", "seq", None),
            P("head", None, "seq"),
            P("seq", None, "head"),
            P("head", "seq"),
        ),
        check_vma=False,
    )
```

profile of v0, /device:TPU:0, one launch (start us, length us, event | category | flops | bytes accessed | tf_op | source)
XLA Modules:
  0.0 5987.4 jit_solution(15890383101522802778)
XLA Ops:
  101.4 44.6 all-gather.46.cloned.1.call-done
  169.2 63.5 %while.165 = (s32[]{:T(128)}, f32[12,64,128]{2,1,0:T(8,128)S(1)}, f32[2,256,12,64]{1,0,3,2:T(2,128)}, s32[2,256]{1,0:T(2,128)}, s32[2]{0:T(128)}, /*index=5*/f32...) while((s32[]{:T(128)}, f32[12,64,128]{2,1,0:T(8,128)S(1)}, ...), condition=%wide.region_30.34_spmd.clone, body=%wide.region_29.33_spmd.clone.sunk | while | flops 1323250176 | bytes 9614202 | solution.py:159
  256.7 55.8 while.164
  468.7 41.2 reduce-scatter.41.cloned.1.call-done
  685.9 444.0 %all-gather.54.cloned.1.call-done = bf16[8,1536,1024]{2,1,0:T(8,128)(2,1)} async-done(((bf16[8,192,1024]{2,1,0:T(8,128)(2,1)}), bf16[8,1536,1024]{2,1,0:T(8,128)(2,1)}) %all-gather.54.cloned.1.call-update) | async-done | bytes 25165840 | tf_op jit(solution)/shard_map/all_gather | solution.py:227
  1147.5 160.9 %all-gather.56.cloned.1.call-done = bf16[8,512,1536]{1,2,0:T(8,128)(2,1)} async-done(((bf16[8,512,192]{1,2,0:T(8,128)(2,1)}), bf16[8,512,1536]{1,2,0:T(8,128)(2,1)}) %all-gather.56.cloned.1.call-update) | async-done | bytes 12582928 | tf_op jit(solution)/shard_map/all_gather | solution.py:228
  1609.3 171.8 %all-gather.64.cloned.1.call-done = bf16[8,512,1536]{1,2,0:T(8,128)(2,1)} async-done(((bf16[8,512,192]{1,2,0:T(8,128)(2,1)}), bf16[8,512,1536]{1,2,0:T(8,128)(2,1)}) %all-gather.64.cloned.1.call-update) | async-done | bytes 12582928 | tf_op jit(solution)/shard_map/all_gather | solution.py:228
  1794.5 466.8 %all-gather.66.cloned.1.call-done = bf16[8,1536,1024]{2,1,0:T(8,128)(2,1)} async-done(((bf16[8,192,1024]{2,1,0:T(8,128)(2,1)}), bf16[8,1536,1024]{2,1,0:T(8,128)(2,1)}) %all-gather.66.cloned.1.call-update) | async-done | bytes 25165840 | tf_op jit(solution)/shard_map/all_gather | solution.py:227
  2306.0 133.9 %all-gather.76.cloned.1.call-done = bf16[8,512,1536]{1,2,0:T(8,128)(2,1)} async-done(((bf16[8,512,192]{1,2,0:T(8,128)(2,1)}), bf16[8,512,1536]{1,2,0:T(8,128)(2,1)}) %all-gather.76.cloned.1.call-update) | async-done | bytes 12582928 | tf_op jit(solution)/shard_map/all_gather | solution.py:228
  2453.3 466.8 %all-gather.78.cloned.1.call-done = bf16[8,1536,1024]{2,1,0:T(8,128)(2,1)} async-done(((bf16[8,192,1024]{2,1,0:T(8,128)(2,1)}), bf16[8,1536,1024]{2,1,0:T(8,128)(2,1)}) %all-gather.78.cloned.1.call-update) | async-done | bytes 25165840 | tf_op jit(solution)/shard_map/all_gather | solution.py:227
  3222.0 109.9 %while.161 = (s32[]{:T(128)}, f32[12,64,128]{2,1,0:T(8,128)S(1)}, f32[2,256,12,64]{1,0,3,2:T(2,128)}, f32[2,256,128]{2,1,0:T(8,128)}, f32[2,256,128]{2,1,0:T(8,1...) while((s32[]{:T(128)}, f32[12,64,128]{2,1,0:T(8,128)S(1)}, ...), condition=%wide.region_99.103_spmd, body=%wide.region_91.102_spmd.sunk | while | flops 3057048064 | bytes 36261276 | solution.py:159
  3348.9 111.0 %while.159 = (s32[]{:T(128)}, f32[12,64,128]{2,1,0:T(8,128)S(1)}, f32[2,256,12,64]{1,0,3,2:T(2,128)}, f32[2,256,128]{2,1,0:T(8,128)}, f32[2,256,128]{2,1,0:T(8,1...) while((s32[]{:T(128)}, f32[12,64,128]{2,1,0:T(8,128)S(1)}, ...), condition=%wide.region_71.75_spmd, body=%wide.region_63.74_spmd.sunk | while | flops 3057048064 | bytes 35786180 | solution.py:159
  3635.7 43.0 all-gather.84.cloned.1.call-done
  3743.0 64.6 %reduce-scatter.71.cloned.1.call-done = bf16[256,192]{0,1:T(8,128)(2,1)} async-done(((bf16[256,1536]{0,1:T(8,128)(2,1)}), bf16[256,192]{0,1:T(8,128)(2,1)}) %reduce-scatter.71.cloned.1.call-update) | async-done | bytes 98320 | tf_op jit(solution)/shard_map/reduce_scatter | solution.py:260
  3809.2 62.2 %reduce-scatter.85.cloned.1.call-done = bf16[192,32]{1,0:T(8,128)(2,1)} async-done(((bf16[1536,32]{1,0:T(8,128)(2,1)}), bf16[192,32]{1,0:T(8,128)(2,1)}) %reduce-scatter.85.cloned.1.call-update) | async-done | bytes 12304
  3872.3 63.2 %reduce-scatter.87.cloned.1.call-done = bf16[192,32]{1,0:T(8,128)(2,1)} async-done(((bf16[1536,32]{1,0:T(8,128)(2,1)}), bf16[192,32]{1,0:T(8,128)(2,1)}) %reduce-scatter.87.cloned.1.call-update) | async-done | bytes 12304
  3938.0 35.3 all_gather.200
  3973.3 36.0 all_gather.186
  4009.3 70.7 %all-reduce.42.cloned.1.call-done = (bf16[1536,2,256]{2,1,0:T(2,128)(2,1)}, bf16[1536,2,256]{2,1,0:T(2,128)(2,1)}) async-done(((bf16[1536,2,256]{2,1,0:T(2,128)(2,1)}, bf16[1536,2,256]{2,1,0:T(2,128)(2,1)}), (bf16[1536,2,256]{2,1,0:T(2,128)(2,1)}, bf16[1536,2,256]{2,1,0:T(2,128)(2,1)})) %all-reduce.42.cloned.1.call-update) | async-done | bytes 3145744
  4082.0 208.0 %reduce-scatter.65.cloned.1.call-done = bf16[8,512,192]{1,2,0:T(8,128)(2,1)} async-done(((bf16[8,512,1536]{1,2,0:T(8,128)(2,1)}), bf16[8,512,192]{1,2,0:T(8,128)(2,1)}) %reduce-scatter.65.cloned.1.call-update) | async-done | bytes 1572880 | tf_op jit(solution)/shard_map/reduce_scatter | solution.py:254
  4289.9 210.1 %reduce-scatter.67.cloned.1.call-done = bf16[8,512,192]{1,2,0:T(8,128)(2,1)} async-done(((bf16[8,512,1536]{1,2,0:T(8,128)(2,1)}), bf16[8,512,192]{1,2,0:T(8,128)(2,1)}) %reduce-scatter.67.cloned.1.call-update) | async-done | bytes 1572880 | tf_op jit(solution)/shard_map/reduce_scatter | solution.py:254
  4516.6 47.2 reduce-scatter.81.cloned.1.call-done
  4564.7 63.2 %reduce-scatter.83.cloned.1.call-done = bf16[192,12]{1,0:T(8,128)(2,1)} async-done(((bf16[1536,12]{1,0:T(8,128)(2,1)}), bf16[192,12]{1,0:T(8,128)(2,1)}) %reduce-scatter.83.cloned.1.call-update) | async-done | bytes 4624
  4629.4 63.3 %reduce-scatter.53.cloned.1.call-done = bf16[192,256]{1,0:T(8,128)(2,1)} async-done(((bf16[1536,256]{1,0:T(8,128)(2,1)}), bf16[192,256]{1,0:T(8,128)(2,1)}) %reduce-scatter.53.cloned.1.call-update) | async-done | bytes 98320 | tf_op jit(solution)/shard_map/reduce_scatter | solution.py:242
  4692.7 64.9 %reduce-scatter.55.cloned.1.call-done = bf16[192,256]{1,0:T(8,128)(2,1)} async-done(((bf16[1536,256]{1,0:T(8,128)(2,1)}), bf16[192,256]{1,0:T(8,128)(2,1)}) %reduce-scatter.55.cloned.1.call-update) | async-done | bytes 98320 | tf_op jit(solution)/shard_map/reduce_scatter | solution.py:242
  4759.2 69.9 %reduce-scatter.59.cloned.1.call-done = bf16[768,192]{0,1:T(8,128)(2,1)} async-done(((bf16[768,1536]{0,1:T(8,128)(2,1)}), bf16[768,192]{0,1:T(8,128)(2,1)}) %reduce-scatter.59.cloned.1.call-update) | async-done | bytes 294928 | tf_op jit(solution)/shard_map/reduce_scatter | solution.py:245
  4829.1 71.4 %reduce-scatter.57.cloned.1.call-done = bf16[768,192]{0,1:T(8,128)(2,1)} async-done(((bf16[768,1536]{0,1:T(8,128)(2,1)}), bf16[768,192]{0,1:T(8,128)(2,1)}) %reduce-scatter.57.cloned.1.call-update) | async-done | bytes 294928 | tf_op jit(solution)/shard_map/reduce_scatter | solution.py:245
  4967.4 40.3 all-reduce.28
  5019.2 41.1 reduce-scatter.49.cloned.1.call-done
  5060.4 99.1 %reduce-scatter.51.cloned.1.call-done = bf16[2,192,768]{2,1,0:T(8,128)(2,1)} async-done(((bf16[2,1536,768]{2,1,0:T(8,128)(2,1)}), bf16[2,192,768]{2,1,0:T(8,128)(2,1)}) %reduce-scatter.51.cloned.1.call-update) | async-done | bytes 589840 | tf_op jit(solution)/shard_map/reduce_scatter | solution.py:236
  5161.9 404.8 %reduce-scatter.61.cloned.1.call-done = bf16[8,192,1024]{2,1,0:T(8,128)(2,1)} async-done(((bf16[8,1536,1024]{2,1,0:T(8,128)(2,1)}), bf16[8,192,1024]{2,1,0:T(8,128)(2,1)}) %reduce-scatter.61.cloned.1.call-update) | async-done | bytes 3145744 | tf_op jit(solution)/shard_map/reduce_scatter | solution.py:251
  5566.7 406.6 %reduce-scatter.63.cloned.1.call-done = bf16[8,192,1024]{2,1,0:T(8,128)(2,1)} async-done(((bf16[8,1536,1024]{2,1,0:T(8,128)(2,1)}), bf16[8,192,1024]{2,1,0:T(8,128)(2,1)}) %reduce-scatter.63.cloned.1.call-update) | async-done | bytes 3145744 | tf_op jit(solution)/shard_map/reduce_scatter | solution.py:251
  (1479 shorter events, 1905.1 us)
Async XLA Ops:
  20.9 340.5 %all-gather.88.cloned.1.call-start = ((), (), s32[]{:S(2)}) async-start(), calls=%async_computation.62 | async-start | bytes 3538944 | tf_op jit(solution)/shard_map/all_gather | solution.py:30
  440.4 205.6 %all-gather.52.cloned.1.call-start = ((), (), s32[]{:S(2)}) async-start(), calls=%async_computation.29 | async-start | bytes 1769472 | tf_op jit(solution)/shard_map/all_gather | solution.py:229
  441.2 206.7 %all-gather.50.cloned.1.call-start = ((), (), s32[]{:S(2)}) async-start(), calls=%async_computation.28 | async-start | bytes 1966080 | tf_op jit(solution)/shard_map/all_gather | solution.py:203
  519.9 610.0 %all-gather.54.cloned.1.call-start = ((), (), s32[]{:S(2)}) async-start(), calls=%async_computation.30 | async-start | bytes 28311552 | tf_op jit(solution)/shard_map/all_gather | solution.py:227
  520.5 787.9 %all-gather.56.cloned.1.call-start = ((), (), s32[]{:S(2)}) async-start(), calls=%async_computation.31 | async-start | bytes 14155776 | tf_op jit(solution)/shard_map/all_gather | solution.py:228
  521.1 944.7 %reduce-scatter.43.cloned.1.call-start = ((), (), s32[]{:S(2)}) async-start(), calls=%async_computation.32 | async-start | bytes 3932160 | tf_op jit(solution)/shard_map/reduce_scatter | solution.py:207
  1504.7 276.3 %all-gather.64.cloned.1.call-start = ((), (), s32[]{:S(2)}) async-start(), calls=%async_computation.38 | async-start | bytes 14155776 | tf_op jit(solution)/shard_map/all_gather | solution.py:228
  1505.3 755.9 %all-gather.66.cloned.1.call-start = ((), (), s32[]{:S(2)}) async-start(), calls=%async_computation.39 | async-start | bytes 28311552 | tf_op jit(solution)/shard_map/all_gather | solution.py:227
  1506.1 933.8 %all-gather.76.cloned.1.call-start = ((), (), s32[]{:S(2)}) async-start(), calls=%async_computation.44 | async-start | bytes 14155776 | tf_op jit(solution)/shard_map/all_gather | solution.py:228
  1506.8 1413.3 %all-gather.78.cloned.1.call-start = ((), (), s32[]{:S(2)}) async-start(), calls=%async_computation.45 | async-start | bytes 28311552 | tf_op jit(solution)/shard_map/all_gather | solution.py:227
  1507.6 1517.1 %reduce-scatter.73.cloned.1.call-start = ((), (), s32[]{:S(2)}) async-start(), calls=%async_computation.67 | async-start | bytes 1966080
  2305.9 719.9 %reduce-scatter.77.cloned.1.call-start = ((), (), s32[]{:S(2)}) async-start(), calls=%async_computation.69 | async-start | bytes 1966080
  3209.4 324.3 %all-reduce.44.cloned.1.call-start = ((), (), s32[]{:S(2)}) async-start(), calls=%async_computation.76 | async-start | bytes 1064960 | tf_op jit(solution)/shard_map/psum | solution.py:567
  3484.9 258.1 %reduce-scatter.69.cloned.1.call-start = ((), (), s32[]{:S(2)}) async-start(), calls=%async_computation.59 | async-start | bytes 884736 | tf_op jit(solution)/shard_map/reduce_scatter | solution.py:260
  3486.6 321.0 %reduce-scatter.71.cloned.1.call-start = ((), (), s32[]{:S(2)}) async-start(), calls=%async_computation.60 | async-start | bytes 884736 | tf_op jit(solution)/shard_map/reduce_scatter | solution.py:260
  3489.4 382.1 %reduce-scatter.85.cloned.1.call-start = ((), (), s32[]{:S(2)}) async-start(), calls=%async_computation.73 | async-start | bytes 442368
  3490.8 444.7 %reduce-scatter.87.cloned.1.call-start = ((), (), s32[]{:S(2)}) async-start(), calls=%async_computation.74 | async-start | bytes 442368
  3492.2 587.8 %all-reduce.42.cloned.1.call-start = ((), (), s32[]{:S(2)}) async-start(), calls=%async_computation.75 | async-start | bytes 6291456
  3505.2 784.7 %reduce-scatter.65.cloned.1.call-start = ((), (), s32[]{:S(2)}) async-start(), calls=%async_computation.57 | async-start | bytes 14155776 | tf_op jit(solution)/shard_map/reduce_scatter | solution.py:254
  3516.6 983.4 %reduce-scatter.67.cloned.1.call-start = ((), (), s32[]{:S(2)}) async-start(), calls=%async_computation.58 | async-start | bytes 14155776 | tf_op jit(solution)/shard_map/reduce_scatter | solution.py:254
  3528.0 1035.8 %reduce-scatter.81.cloned.1.call-start = ((), (), s32[]{:S(2)}) async-start(), calls=%async_computation.71 | async-start | bytes 442368
  3530.7 1097.1 %reduce-scatter.83.cloned.1.call-start = ((), (), s32[]{:S(2)}) async-start(), calls=%async_computation.72 | async-start | bytes 442368
  3533.7 1159.0 %reduce-scatter.53.cloned.1.call-start = ((), (), s32[]{:S(2)}) async-start(), calls=%async_computation.51 | async-start | bytes 884736 | tf_op jit(solution)/shard_map/reduce_scatter | solution.py:242
  3544.7 1212.9 %reduce-scatter.55.cloned.1.call-start = ((), (), s32[]{:S(2)}) async-start(), calls=%async_computation.52 | async-start | bytes 884736 | tf_op jit(solution)/shard_map/reduce_scatter | solution.py:242
  3553.7 1275.4 %reduce-scatter.59.cloned.1.call-start = ((), (), s32[]{:S(2)}) async-start(), calls=%async_computation.54 | async-start | bytes 2654208 | tf_op jit(solution)/shard_map/reduce_scatter | solution.py:245
  3558.6 1341.9 %reduce-scatter.57.cloned.1.call-start = ((), (), s32[]{:S(2)}) async-start(), calls=%async_computation.53 | async-start | bytes 2654208 | tf_op jit(solution)/shard_map/reduce_scatter | solution.py:245
  3564.5 1365.6 %reduce-scatter.75.cloned.1.call-start = ((), (), s32[]{:S(2)}) async-start(), calls=%async_computation.68 | async-start | bytes 1966080
  3604.5 1356.3 %reduce-scatter.79.cloned.1.call-start = ((), (), s32[]{:S(2)}) async-start(), calls=%async_computation.70 | async-start | bytes 1966080
  3688.2 1372.2 %reduce-scatter.49.cloned.1.call-start = ((), (), s32[]{:S(2)}) async-start(), calls=%async_computation.49 | async-start | bytes 5308416 | tf_op jit(solution)/shard_map/reduce_scatter | solution.py:236
  3695.1 1464.4 %reduce-scatter.51.cloned.1.call-start = ((), (), s32[]{:S(2)}) async-start(), calls=%async_computation.50 | async-start | bytes 5308416 | tf_op jit(solution)/shard_map/reduce_scatter | solution.py:236
  3702.0 1864.6 %reduce-scatter.61.cloned.1.call-start = ((), (), s32[]{:S(2)}) async-start(), calls=%async_computation.55 | async-start | bytes 28311552 | tf_op jit(solution)/shard_map/reduce_scatter | solution.py:251
  3718.7 2254.6 %reduce-scatter.63.cloned.1.call-start = ((), (), s32[]{:S(2)}) async-start(), calls=%async_computation.56 | async-start | bytes 28311552 | tf_op jit(solution)/shard_map/reduce_scatter | solution.py:251
  (358 other events, 13184.6 us)
Sparse Core Ops, SparseCore 0:
  63.5 82.3 all-gather.45
  233.6 59.8 all-gather.87
  313.4 61.0 all-gather.85
  376.5 50.6 all-gather.47
  649.4 480.4 all-gather.53
  1131.9 176.3 all-gather.55
  1504.8 52.8 all-gather.61
  1605.8 175.2 all-gather.63
  1782.6 478.6 all-gather.65
  2263.5 176.4 all-gather.75
  2441.4 478.6 all-gather.77
  2990.6 52.1 all-gather.81
  3065.4 52.0 all-gather.69
  3516.3 81.1 all-gather.71
  3599.9 78.6 all-gather.83
  3682.3 60.6 reduce-scatter.68
  3746.1 61.4 reduce-scatter.70
  3811.1 60.3 reduce-scatter.84
  3875.0 60.3 reduce-scatter.86
  3939.4 140.4 all-reduce.41
  4083.6 206.3 reduce-scatter.64
  4293.5 206.4 reduce-scatter.66
  4503.3 60.4 reduce-scatter.80
  4567.5 60.3 reduce-scatter.82
  4631.2 61.4 reduce-scatter.52
  4696.2 61.3 reduce-scatter.54
  4760.9 68.1 reduce-scatter.58
  4832.4 68.0 reduce-scatter.56
  4964.5 95.8 reduce-scatter.48
  5064.5 94.9 reduce-scatter.50
  5163.4 403.2 reduce-scatter.60
  5570.4 402.8 reduce-scatter.62
  (21 shorter events, 625.2 us)
where the time goes:
time: 6010 us; the launch traced here: 5990 us
  waiting for transfers between devices  4240 us (71%)
  blocking collectives  561 us (9%)
  local copies, waits for them, and re-layouts  443 us (7%)
  matrix products  408 us (7%)
  other arithmetic  283 us (5%)
    all_gather x3, waiting for transfers between devices, fetch_weights(): lax.all_gather(shards[5], 'seq', axis=1, tiled=True)  1380 us
    reduce_scatter x2, waiting for transfers between devices, reduce_weights(): lax.psum_scatter(matrices[5].astype(jnp.bfloat16), 'seq', scatter_dimensi...  811 us
    all_gather x3, waiting for transfers between devices, fetch_weights(): lax.all_gather(shards[6], 'seq', axis=2, tiled=True)  467 us
    reduce_scatter x2, waiting for transfers between devices, reduce_weights(): lax.psum_scatter(matrices[6].astype(jnp.bfloat16), 'seq', scatter_dimensi...  418 us
    unnamed x62, waiting for transfers between devices  375 us
    dynamic_update_slice x36, local copies, waits for them, and re-layouts, scan_device(): lax.scan(jax.checkpoint(ssd_block), carry_in, block_parts)  149 us
    reduce_scatter x2, waiting for transfers between devices, reduce_weights(): lax.psum_scatter(matrices[3].astype(jnp.bfloat16), 'seq', scatter_dimensi...  141 us
    reduce_scatter x2, waiting for transfers between devices, reduce_weights(): lax.psum_scatter(matrices[0].astype(jnp.bfloat16), 'seq', scatter_dimensi...  140 us
  transfers between devices with their start and end apart: 57, of which 39 were waited for; matrix products, arithmetic and copies ran while one was open for 12% of the time, Pallas kernels for 0%

commit v1 on v0

v1 whole, which is shorter than its diff:
```python
import functools
from functools import partial

import jax
import jax.numpy as jnp
from jax import lax
from jax.experimental import pallas as pl
from jax.experimental.pallas import tpu as pltpu
from jax.sharding import PartitionSpec as P

D = 1536
HEAD_DIM = 64
STATE = 128
CONV = 4
TOPK = 6
EFF = 512
INNER = 3072
MEMBERS = 4
EDGE = 8
CHUNK = 128

EPSILON = 1e-05
HIGHEST = lax.Precision.HIGHEST
BF = jnp.bfloat16
F32 = jnp.float32
MESH = pl.DeviceIdType.MESH

def flips(bits):
    found = [(0, 0)]
    for axis, mask in bits:
        found += [(a ^ (mask * (axis == "seq")), b ^ (mask * (axis == "head"))) for a, b in found]
    return found


def joined(left, right):
    return (left[0] ^ right[0], left[1] ^ right[1])


def flip_of(bit):
    axis, mask = bit
    return (mask, 0) if axis == "seq" else (0, mask)


def toggled(place, mask):
    found, bit = place, 1
    while bit <= mask:
        if mask & bit:
            found = found + bit * (1 - 2 * lax.rem(lax.div(place, bit), 2))
        bit = 2 * bit
    return found


def across(me, masks):
    return (toggled(me[0], masks[0]), toggled(me[1], masks[1]))


def greet(jobs, me):
    bits = sorted({bit for job in jobs for bit in job.parts[0][2]})
    barrier = pltpu.get_barrier_semaphore()
    for bit in bits:
        pl.semaphore_signal(
            barrier, inc=1, device_id=across(me, flip_of(bit)), device_id_type=MESH
        )
    pl.semaphore_wait(barrier, len(bits))


class Job:
    def __init__(self, parts, slot_of, wide=False):
        self.parts, self.slot_of, self.wide = parts, slot_of, wide
        self.depth = len(parts[0][2])
        self.count = 1 << self.depth

    def view(self, ref, place, rows, columns, width):
        slot = self.slot_of(*place)
        if self.wide:
            at = columns[0] + slot * width
            if columns[0] % 128 == 0 and width % 128 == 0:
                at = pl.multiple_of(at, 128)
            return ref.at[:, pl.ds(*rows), pl.ds(at, columns[1])]
        return ref.at[:, slot, pl.ds(*rows), pl.ds(*columns)]

    def whole_shape(self, shape):
        lead, rows, columns = shape
        if self.wide:
            return (lead, rows, self.count * columns)
        return (lead, self.count, rows, columns)


def gather_kernel(jobs, *refs):
    me = (lax.axis_index("seq"), lax.axis_index("head"))
    number = len(jobs)
    x_refs, o_refs, sems = refs[:number], refs[number : 2 * number], refs[2 * number :]
    greet(jobs, me)
    owns, copies, waited = [], {}, set()
    for step in range(max(job.depth for job in jobs)):
        for j, job in enumerate(jobs):
            if step >= job.depth:
                continue
            send_sem, recv_sem, own_sem = sems[3 * j : 3 * j + 3]
            x_ref, o_ref = x_refs[j], o_refs[j]
            width = x_ref.shape[2]
            for p, (rows, columns, order) in enumerate(job.parts):
                other = flip_of(order[step])
                for place, held in enumerate(flips(order[:step])):
                    if place and (j, p, place) not in waited:
                        copies[j, p, place].wait_recv()
                        waited.add((j, p, place))
                    dst = job.view(o_ref, across(me, held), rows, columns, width)
                    src = dst if place else x_ref.at[:, pl.ds(*rows), pl.ds(*columns)]
                    arriving = place + (1 << step)
                    copy = pltpu.make_async_remote_copy(
                        src_ref=src,
                        dst_ref=dst,
                        send_sem=send_sem.at[p, arriving],
                        recv_sem=recv_sem.at[p, arriving],
                        device_id=across(me, other),
                        device_id_type=MESH,
                    )
                    copy.start()
                    copies[j, p, arriving] = copy
            if step == 0:
                whole = ((0, x_ref.shape[1]), (0, width))
                own = pltpu.make_async_copy(x_ref, job.view(o_ref, me, *whole, width), own_sem)
                own.start()
                owns.append(own)
    for key, copy in copies.items():
        if key not in waited:
            copy.wait_recv()
    for copy in copies.values():
        copy.wait_send()
    for own in owns:
        own.wait()


def cube_gather(jobs, arrays, collective_id, weight=100 << 20):
    anywhere = pl.BlockSpec(memory_space=pl.ANY)
    scratch = []
    for job in jobs:
        for shape in ((len(job.parts), job.count),) * 2 + ((),):
            scratch.append(pltpu.SemaphoreType.DMA(shape) if shape else pltpu.SemaphoreType.DMA)
    return pl.pallas_call(
        functools.partial(gather_kernel, jobs),
        out_shape=tuple(
            jax.ShapeDtypeStruct(job.whole_shape(x.shape), x.dtype)
            for job, x in zip(jobs, arrays, strict=True)
        ),
        in_specs=[anywhere] * len(jobs),
        out_specs=(anywhere,) * len(jobs),
        scratch_shapes=scratch,
        compiler_params=pltpu.CompilerParams(collective_id=collective_id, has_side_effects=True),
        cost_estimate=pl.CostEstimate(flops=0, bytes_accessed=weight, transcendentals=0),
    )(*arrays)


def reduce_kernel(jobs, *refs):
    me = (lax.axis_index("seq"), lax.axis_index("head"))
    number = len(jobs)
    x_refs, o_refs, scratch = refs[:number], refs[number : 2 * number], refs[2 * number :]
    greet(jobs, me)
    loads, flying = {}, {}

    def base(job, step):
        return sum(1 << (job.depth - 1 - i) for i in range(step))

    def send(j, p, step, place):
        job, x_ref = jobs[j], x_refs[j]
        kept, stage, send_sem, recv_sem, own_sem = scratch[5 * j : 5 * j + 5]
        rows, columns, order = job.parts[p]
        other = flip_of(order[step])
        gone = joined(flips(order[step + 1 :])[place], other)
        if step == 0:
            src = job.view(x_ref, across(me, gone), rows, columns, stage.shape[3])
        else:
            source = base(job, step - 1) + flips(order[step:]).index(gone)
            src = stage.at[source, :, pl.ds(*rows), pl.ds(*columns)]
        target = base(job, step) + place
        copy = pltpu.make_async_remote_copy(
            src_ref=src,
            dst_ref=stage.at[target, :, pl.ds(*rows), pl.ds(*columns)],
            send_sem=send_sem.at[p, target],
            recv_sem=recv_sem.at[p, target],
            device_id=across(me, other),
            device_id_type=MESH,
        )
        copy.start()
        flying[j, p, step, place] = copy

    def add(j, p, step, place):
        job, o_ref = jobs[j], o_refs[j]
        kept, stage = scratch[5 * j : 5 * j + 2]
        rows, columns, order = job.parts[p]
        tile = 16 if rows[1] % 16 == 0 else 8
        target = base(job, step) + place
        left = flips(order[step + 1 :])[place]
        source = base(job, step - 1) + flips(order[step:]).index(left) if step else 0

        def one(i, carry):
            here = pl.ds(pl.multiple_of(rows[0] + i * tile, tile), tile)
            for m in range(stage.shape[1]):
                got = stage[target, m, here, pl.ds(*columns)].astype(F32)
                if step == 0:
                    mine = kept[place, m, here, pl.ds(*columns)]
                else:
                    mine = stage[source, m, here, pl.ds(*columns)]
                total = got + mine.astype(F32)
                if step + 1 == job.depth:
                    o_ref[m, here, pl.ds(*columns)] = total
                else:
                    stage[target, m, here, pl.ds(*columns)] = total.astype(stage.dtype)
            return carry

        lax.fori_loop(0, rows[1] // tile, one, 0)

    def sequence(job, p, step):
        order = job.parts[p][2]
        found = flips(order[step + 1 :])
        if step + 1 == job.depth:
            return [0]
        other, later = flip_of(order[step + 1]), flips(order[step + 2 :])
        return [found.index(joined(left, other)) for left in later] + [
            found.index(left) for left in later
        ]

    for j, job in enumerate(jobs):
        for p in range(len(job.parts)):
            for place in sequence(job, p, 0):
                send(j, p, 0, place)
    for j, job in enumerate(jobs):
        kept, stage, send_sem, recv_sem, own_sem = scratch[5 * j : 5 * j + 5]
        for p, (rows, columns, order) in enumerate(job.parts):
            for place, held in enumerate(flips(order[1:])):
                load = pltpu.make_async_copy(
                    job.view(x_refs[j], across(me, held), rows, columns, stage.shape[3]),
                    kept.at[place, :, pl.ds(*rows), pl.ds(*columns)],
                    own_sem.at[p, place],
                )
                load.start()
                loads[j, p, place] = load
    for step in range(max(job.depth for job in jobs)):
        for j, job in enumerate(jobs):
            if step >= job.depth:
                continue
            for p, (rows, columns, order) in enumerate(job.parts):
                places = sequence(job, p, step)
                for at, place in enumerate(places):
                    if step == 0:
                        loads[j, p, place].wait()
                    flying[j, p, step, place].wait_recv()
                    add(j, p, step, place)
                    if step + 1 < job.depth and at < len(places) // 2:
                        send(j, p, step + 1, at)
    for copy in flying.values():
        copy.wait_send()


def cube_reduce(jobs, arrays, collective_id, weight=100 << 20):
    out_shape, scratch = [], []
    for job, x in zip(jobs, arrays, strict=True):
        if job.wide:
            lead, rows, columns = x.shape[0], x.shape[1], x.shape[2] // job.count
        else:
            lead, _, rows, columns = x.shape
        out_shape.append(jax.ShapeDtypeStruct((lead, rows, columns), F32))
        scratch += [
            pltpu.VMEM((job.count // 2, lead, rows, columns), x.dtype),
            pltpu.VMEM((job.count - 1, lead, rows, columns), x.dtype),
            pltpu.SemaphoreType.DMA((len(job.parts), job.count - 1)),
            pltpu.SemaphoreType.DMA((len(job.parts), job.count - 1)),
            pltpu.SemaphoreType.DMA((len(job.parts), job.count // 2)),
        ]
    return pl.pallas_call(
        functools.partial(reduce_kernel, jobs),
        out_shape=tuple(out_shape),
        in_specs=[pl.BlockSpec(memory_space=pl.ANY)] * len(jobs),
        out_specs=(pl.BlockSpec(memory_space=pltpu.VMEM),) * len(jobs),
        scratch_shapes=scratch,
        compiler_params=pltpu.CompilerParams(
            collective_id=collective_id, has_side_effects=True, vmem_limit_bytes=52 << 20
        ),
        cost_estimate=pl.CostEstimate(flops=0, bytes_accessed=weight, transcendentals=0),
    )(*arrays)


def bits_in(axis, size):
    return [(axis, 1 << i) for i in range(size.bit_length() - 1)]


def thirds(rows, columns):
    if columns % 384:
        return [((0, rows), (0, columns))]
    third = columns // 3
    return [((0, rows), (i * third, third)) for i in range(3)]


def slot_in_head(s, h):
    return h


def slot_in_seq(s, h):
    return s


def slot_in_members(s, h):
    return lax.rem(s, MEMBERS)


def slot_in_group(s, h):
    return lax.rem(s, MEMBERS) * lax.axis_size("head") + h


def group_job(rows, columns, way):
    core = ("head", 1)
    links = bits_in("head", lax.axis_size("head"))[1:] + bits_in("seq", MEMBERS)
    parts = []
    for i, (r, c) in enumerate(thirds(rows, columns)):
        turned = links[i:] + links[:i]
        parts.append((r, c, (turned + [core])[::way]))
    return Job(parts, slot_in_group)


def head_job(rows, columns, way, wide=False):
    bits = bits_in("head", lax.axis_size("head"))
    order = (bits[1:] + bits[:1])[::way]
    return Job([(r, c, order) for r, c in thirds(rows, columns)], slot_in_head, wide)


def seq_job(rows, columns, way):
    bits = bits_in("seq", lax.axis_size("seq"))
    cut = rows * 5 // 6 // 16 * 16
    parts = [
        ((0, cut), (0, columns), bits[::-1][::way]),
        ((cut, rows - cut), (0, columns), (bits[:1] + bits[:0:-1])[::way]),
    ]
    return Job(parts, slot_in_seq)


def members_job(rows, columns):
    return Job([((0, rows), (0, columns), bits_in("seq", MEMBERS))], slot_in_members)


RUN, STEP, SEG = 0, 2, 4


def dot(a, b, dims):
    return lax.dot_general(
        a.astype(BF), b.astype(BF), (dims, ((), ())), preferred_element_type=F32
    )


def split_low(a):
    high = a.astype(BF)
    return high, (a - high.astype(F32)).astype(BF)


def dot_fine(a, b, dims):
    (a_high, a_low), (b_high, b_low) = split_low(a), split_low(b)
    return dot(a_high, b_high, dims) + (dot(a_high, b_low, dims) + dot(a_low, b_high, dims))


NN = ((1,), (0,))
NT = ((1,), (1,))
TN = ((0,), (0,))


def chunk_parts(cols_ref, rows_ref, begin):
    here = pl.ds(begin, CHUNK)
    cols, rows = cols_ref[0, 0, here, :], rows_ref[0, 0, :, here]
    last = slice(CHUNK - 1, CHUNK)
    seg_c, seg_r, seg_end = cols[:, SEG : SEG + 1], rows[SEG : SEG + 1], cols[last, SEG : SEG + 1]
    if begin:
        before = cols_ref[0, 0, pl.ds(begin - 8, 8), :][7:8]
        seg_before, run_before = before[:, SEG : SEG + 1], [before[:, RUN + k : RUN + k + 1] for k in range(2)]
    else:
        seg_before, run_before = cols[:1, SEG + 1 : SEG + 2], [jnp.zeros((1, 1), F32)] * 2
    row = lax.broadcasted_iota(jnp.int32, (CHUNK, CHUNK), 0)
    column = lax.broadcasted_iota(jnp.int32, (CHUNK, CHUNK), 1)
    within = (row >= column) & (seg_c == seg_r)
    heads = []
    for k in range(2):
        run_c, run_r = cols[:, RUN + k : RUN + k + 1], rows[RUN + k : RUN + k + 1]
        run_end = run_c[CHUNK - 1 :]
        decay = jnp.where(within, jnp.exp(jnp.where(within, run_c - run_r, 0.0)), 0.0)
        enter = jnp.where(seg_c == seg_before, jnp.exp(run_c - run_before[k]), 0.0)
        leave = jnp.where(seg_c == seg_end, jnp.exp(run_end - run_c), 0.0)
        through = jnp.where(seg_end == seg_before, jnp.exp(run_end - run_before[k]), 0.0)
        heads.append((decay, enter, leave, through, cols[:, STEP + k : STEP + k + 1], rows[STEP + k : STEP + k + 1]))
    return heads


def of_pair(first, second, axis):
    shape = (first.shape[0], 2 * HEAD_DIM) if axis == 1 else (2 * HEAD_DIM, first.shape[1])
    return jnp.where(
        lax.broadcasted_iota(jnp.int32, shape, axis) < HEAD_DIM,
        jnp.broadcast_to(first, shape),
        jnp.broadcast_to(second, shape),
    )


def halves(value):
    low = lax.broadcasted_iota(jnp.int32, value.shape, 1) < HEAD_DIM
    return jnp.where(low, value, 0.0), jnp.where(low, 0.0, value)


def forward_kernel(x_ref, keys_ref, cols_ref, rows_ref, y_ref):
    state = jnp.zeros((2 * HEAD_DIM, STATE), F32)
    tokens = x_ref.shape[1]
    for begin in range(0, tokens, CHUNK):
        here = pl.ds(begin, CHUNK)
        x, write, read = x_ref[0, here, :], keys_ref[0, here, :STATE], keys_ref[0, here, STATE:]
        heads = chunk_parts(cols_ref, rows_ref, begin)
        scores = dot_fine(read, write, NT)
        split = halves(x)
        y = 0.0
        for k, (decay, enter, leave, through, step_c, step_r) in enumerate(heads):
            y = y + dot_fine(scores * decay * step_r, split[k], NN)
        if begin:
            y = y + of_pair(heads[0][1], heads[1][1], 1) * dot_fine(read, state, NT)
        y_ref[0, here, :] = y
        if begin + CHUNK < tokens:
            keep = of_pair(heads[0][2] * heads[0][4], heads[1][2] * heads[1][4], 1)
            state = of_pair(heads[0][3], heads[1][3], 0) * state + dot_fine(
                keep * x, write, TN
            )


def scan_forward(x, keys, cols, rows):
    micro, tokens, width = x.shape
    pairs = width // (2 * HEAD_DIM)
    wide = pl.BlockSpec((1, tokens, 2 * HEAD_DIM), lambda m, p: (m, 0, p))
    return pl.pallas_call(
        forward_kernel,
        grid=(micro, pairs),
        out_shape=jax.ShapeDtypeStruct((micro, tokens, width), F32),
        in_specs=[
            wide,
            pl.BlockSpec((1, tokens, 2 * STATE), lambda m, p: (m, 0, 0)),
            pl.BlockSpec((1, 1, tokens, 8), lambda m, p: (m, p, 0, 0)),
            pl.BlockSpec((1, 1, 8, tokens), lambda m, p: (m, p, 0, 0)),
        ],
        out_specs=wide,
        compiler_params=pltpu.CompilerParams(vmem_limit_bytes=32 << 20),
        cost_estimate=pl.CostEstimate(
            flops=micro * pairs * tokens * CHUNK * 2 * 700, bytes_accessed=micro * tokens * width * 12, transcendentals=0
        ),
    )(x, keys, cols, rows)


def backward_kernel(
    x_ref, keys_ref, cols_ref, rows_ref, dy_ref, state_ref, next_ref,
    dx_ref, dkeys_ref, dcols_ref, drows_ref, states
):
    tokens = x_ref.shape[1]
    chunks = tokens // CHUNK
    pair = pl.program_id(1)

    @pl.when(pair == 0)
    def _():
        dkeys_ref[...] = jnp.zeros_like(dkeys_ref)

    state = state_ref[0]
    for c in range(chunks):
        states[c] = state
        if c + 1 < chunks:
            here = pl.ds(c * CHUNK, CHUNK)
            heads = chunk_parts(cols_ref, rows_ref, c * CHUNK)
            keep = of_pair(heads[0][2] * heads[0][4], heads[1][2] * heads[1][4], 1)
            state = of_pair(heads[0][3], heads[1][3], 0) * state + dot_fine(
                keep * x_ref[0, here, :], keys_ref[0, here, :STATE], TN
            )
    later = next_ref[0]
    pending = [jnp.zeros((1, 1), F32)] * 2
    end_row = lax.broadcasted_iota(jnp.int32, (CHUNK, 1), 0) == CHUNK - 1
    lane8 = lax.broadcasted_iota(jnp.int32, (CHUNK, 8), 1)
    sub8 = lax.broadcasted_iota(jnp.int32, (8, CHUNK), 0)
    for c in reversed(range(chunks)):
        begin = c * CHUNK
        here = pl.ds(begin, CHUNK)
        x, write, read = x_ref[0, here, :], keys_ref[0, here, :STATE], keys_ref[0, here, STATE:]
        dy = dy_ref[0, here, :]
        state = states[c]
        heads = chunk_parts(cols_ref, rows_ref, begin)
        scores = dot_fine(read, write, NT)
        x_split, dy_split = halves(x), halves(dy)
        enter = of_pair(heads[0][1], heads[1][1], 1)
        leave = of_pair(heads[0][2], heads[1][2], 1)
        step = of_pair(heads[0][4], heads[1][4], 1)
        through = of_pair(heads[0][3], heads[1][3], 0)
        entered = enter * dy
        kept = leave * step * x
        from_later = dot_fine(write, later, NT)
        dx = leave * step * from_later
        dread = dot_fine(entered, state, NN)
        dwrite = dot_fine(kept, later, NN)
        weight_grad = halves(from_later * x)
        entry_grad = halves(entered * dot_fine(read, state, NT))
        kept_state = later * state * through
        dscores = 0.0
        dcols = jnp.zeros((CHUNK, 8), F32)
        drows = jnp.zeros((8, CHUNK), F32)
        for k, (decay, _, leave_k, through_k, step_c, step_r) in enumerate(heads):
            products = dot_fine(dy, x_split[k], NT)
            weighted = products * decay
            dx = dx + dot(scores * decay * step_r, dy_split[k], TN)
            dscores = dscores + weighted * step_r
            q = weighted * scores
            r = q * step_r
            dw = jnp.sum(weight_grad[k], axis=1, keepdims=True) * leave_k
            de = jnp.sum(entry_grad[k], axis=1, keepdims=True)
            drun = jnp.sum(r, axis=1, keepdims=True) + de - dw * step_c
            half = slice(k * HEAD_DIM, (k + 1) * HEAD_DIM)
            passed = jnp.sum(jnp.sum(kept_state[half], axis=1, keepdims=True), axis=0, keepdims=True)
            at_end = passed + jnp.sum(dw * step_c, axis=0, keepdims=True) + pending[k]
            pending[k] = -passed - jnp.sum(de, axis=0, keepdims=True)
            drun = drun + jnp.where(end_row, at_end, 0.0)
            dcols = dcols + jnp.where(lane8 == RUN + k, drun, 0.0) + jnp.where(lane8 == STEP + k, dw, 0.0)
            q_sum = jnp.sum(q, axis=0, keepdims=True)
            drows = drows + jnp.where(sub8 == STEP + k, q_sum, 0.0)
            drows = drows + jnp.where(sub8 == RUN + k, -q_sum * step_r, 0.0)
        dread = dread + dot_fine(dscores, write, NN)
        dwrite = dwrite + dot_fine(dscores, read, TN)
        later = through * later + dot_fine(entered, read, TN)
        dx_ref[0, here, :] = dx
        dkeys_ref[0, here, :STATE] += dwrite
        dkeys_ref[0, here, STATE:] += dread
        dcols_ref[0, 0, here, :] = dcols
        drows_ref[0, 0, :, here] = drows


def scan_backward(x, keys, cols, rows, dy, state, later):
    micro, tokens, width = x.shape
    pairs = width // (2 * HEAD_DIM)
    wide = pl.BlockSpec((1, tokens, 2 * HEAD_DIM), lambda m, p: (m, 0, p))
    key = pl.BlockSpec((1, tokens, 2 * STATE), lambda m, p: (m, 0, 0))
    col = pl.BlockSpec((1, 1, tokens, 8), lambda m, p: (m, p, 0, 0))
    row = pl.BlockSpec((1, 1, 8, tokens), lambda m, p: (m, p, 0, 0))
    hold = pl.BlockSpec((1, 2 * HEAD_DIM, STATE), lambda m, p: (m, p, 0))
    return pl.pallas_call(
        backward_kernel,
        grid=(micro, pairs),
        out_shape=(
            jax.ShapeDtypeStruct(x.shape, F32),
            jax.ShapeDtypeStruct(keys.shape, F32),
            jax.ShapeDtypeStruct(cols.shape, F32),
            jax.ShapeDtypeStruct(rows.shape, F32),
        ),
        in_specs=[wide, key, col, row, wide, hold, hold],
        out_specs=(wide, key, col, row),
        scratch_shapes=[pltpu.VMEM((tokens // CHUNK, 2 * HEAD_DIM, STATE), F32)],
        compiler_params=pltpu.CompilerParams(vmem_limit_bytes=32 << 20),
    )(x, keys, cols, rows, dy, state, later)


def mm(a, b, dims, out=F32):
    return lax.dot_general(a, b, (dims, ((), ())), preferred_element_type=out)


def squash_slope(values):
    logistic = jax.nn.sigmoid(values)
    return logistic * (1.0 + values * (1.0 - logistic))


def segment_numbers(lengths, seq_order, positions):
    seq_index = jnp.arange(lengths.shape[1], dtype=jnp.int32)
    picked = (seq_order[:, :, None] == seq_index).astype(jnp.int32)
    placed = jnp.sum(picked * lengths[:, None, :], axis=2)
    earlier = (seq_index[:, None] > seq_index[None, :]).astype(jnp.int32)
    begins = jnp.sum(earlier[None] * placed[:, None, :], axis=2)
    return jnp.sum((begins[:, None, :] <= positions[None, :, None]).astype(jnp.int32), axis=2)


def spread(values):
    return jnp.repeat(values, HEAD_DIM, axis=-1)


def chain(passing, state, axis, way, beside=()):
    count = lax.axis_size(axis)
    heads = passing.shape[1]
    beside = list(beside)
    done = []

    def pull(passing, state, steps):
        pairs = [(i, i + way * steps) for i in range(count) if 0 <= i + way * steps < count]
        far = lax.ppermute(state.astype(BF), axis, pairs)
        rows = jnp.pad(passing[:, None], ((0, 0), (0, 7), (0, STATE - heads)))
        passing = lax.ppermute(rows, axis, pairs)[:, 0, :heads]
        if beside:
            far, value = lax.optimization_barrier((far, beside.pop(0)))
            done.append(value)
        return passing, far.astype(F32)

    passing, state = pull(passing, state, 1)
    covered = 1
    while covered < count - 1:
        far_passing, far_state = pull(passing, state, covered)
        state = spread(passing)[..., None] * far_state + state
        passing = passing * far_passing
        covered = 2 * covered
    return state, done + beside


def groups_of(seq_count, head_count):
    return [
        [s * head_count + h for s in range(g, g + MEMBERS) for h in range(head_count)]
        for g in range(0, seq_count, MEMBERS)
    ]


def rms_scale(rows):
    return lax.rsqrt(jnp.mean(rows * rows, axis=-1, keepdims=True) + EPSILON)


def norm_back(grad_out, rows, gain, scale):
    weighted = grad_out * gain
    products = jnp.mean(weighted * rows, axis=-1, keepdims=True)
    return scale * weighted - rows * (scale * scale * scale * products)


def to_rows(features):
    count = lax.axis_size("head")
    lead, tokens, width = features.shape
    split = features.reshape(lead, count, tokens // count, width)
    return lax.all_to_all(split, "head", 1, 3, tiled=True)[:, 0]


def to_features(rows):
    count = lax.axis_size("head")
    lead, number, width = rows.shape
    split = rows.reshape(lead, 1, number, width)
    return lax.all_to_all(split, "head", 3, 1, tiled=True).reshape(
        lead, count * number, width // count
    )


def gather_features(features, jobs, arrays, collective_id):
    count = lax.axis_size("head")
    wide = features[0].shape[2] % 128 == 0
    own = [head_job(f.shape[1], f.shape[2], 1, wide) for f in features]
    found = cube_gather(own + jobs, list(features) + arrays, collective_id)
    whole = list(found[: len(own)])
    if not wide:
        whole = [
            w.transpose(0, 2, 1, 3).reshape(w.shape[0], w.shape[2], count * w.shape[3])
            for w in whole
        ]
    return whole, found[len(own) :]


def reduce_rows(partial_rows, collective_id):
    lead, tokens, width = partial_rows.shape
    count = lax.axis_size("head")
    number = tokens // count
    split = partial_rows.reshape(lead, count, number, width)
    return cube_reduce([head_job(number, width, -1)], [split], collective_id)[0]


def gather_group(rows, collective_id):
    lead, number, width = rows.shape
    count = lax.axis_size("head")
    whole = cube_gather([group_job(number, width, 1)], [rows], collective_id)[0]
    return whole.reshape(lead, MEMBERS, count * number, width)


def reduce_group(partial_rows, collective_id):
    lead, members, tokens, width = partial_rows.shape
    count = lax.axis_size("head")
    number = tokens // count
    split = partial_rows.reshape(lead, members * count, number, width)
    return cube_reduce([group_job(number, width, -1)], [split], collective_id)[0]


def slot_in_mesh(s, h):
    return s * lax.axis_size("head") + h


def in_rows(values):
    line = jnp.concatenate([v.reshape(-1) for v in values])
    return jnp.pad(line, (0, -line.shape[0] % 1024)).reshape(1, -1, 128)


def tied(value, *others):
    return lax.optimization_barrier((value, *others))[0]


def lane_padded(matrix):
    return jnp.pad(matrix, ((0, 0), (0, -matrix.shape[1] % 128)))


def body(
    hidden,
    output_grad,
    lengths,
    seq_order,
    routes,
    mix_gain,
    input_proj,
    state_proj,
    step_proj,
    conv_inner,
    conv_state,
    inner_bias,
    state_bias,
    step_bias,
    decay_rate,
    skip_gain,
    gate_gain,
    output_proj,
    moe_gain,
    router,
    expert_up,
    expert_down,
    shared_up,
    shared_down,
):
    seq_count, head_count = lax.axis_size("seq"), lax.axis_size("head")
    seq_rank, head_rank = lax.axis_index("seq"), lax.axis_index("head")
    micro, tokens, local_width = hidden.shape
    inner_local = conv_inner.shape[1]
    heads_local = step_bias.shape[0]
    pairs = heads_local // 2
    experts_local = expert_up.shape[0]
    shared_local = shared_down.shape[0]
    slice_rows = input_proj.shape[1]
    expert_total = experts_local * head_count
    capacity = 2 * tokens * TOPK // expert_total
    own_experts = experts_local // MEMBERS
    member = lax.rem(seq_rank, MEMBERS)
    row_count = tokens // head_count
    channels = inner_local + 2 * STATE
    groups = groups_of(seq_count, head_count)
    seq_groups = [list(range(g, g + MEMBERS)) for g in range(0, seq_count, MEMBERS)]

    first_shard = lane_padded(jnp.concatenate([input_proj[1], state_proj, step_proj], axis=1))
    gain_rows = jnp.pad(jnp.stack([mix_gain, moe_gain])[None], ((0, 0), (0, 6), (0, 0)))
    route_shard = jnp.pad(routes.transpose(0, 2, 1), ((0, 0), (0, 8 - TOPK), (0, 0)))
    (hidden_full, grad_full, gains), (first_full, route_group) = gather_features(
        [hidden, output_grad, gain_rows],
        [seq_job(slice_rows, first_shard.shape[1], 1), members_job(8, tokens)],
        [first_shard[None], route_shard],
        0,
    )
    first_full = first_full.reshape(D, -1)
    gains = gains[0, :2]
    conv_proj, step_full = first_full[:, :channels], first_full[:, channels : channels + heads_local]
    own_rows = partial(
        lax.dynamic_slice_in_dim, start_index=head_rank * row_count, slice_size=row_count, axis=1
    )
    resid_in = own_rows(hidden_full).astype(F32)
    grad_rows = own_rows(grad_full)

    second_shard = jnp.concatenate(
        [
            input_proj[0],
            output_proj.T,
            router,
            shared_up.reshape(slice_rows, 2 * shared_local),
            shared_down.T,
        ],
        axis=1,
    )
    second_full = lax.all_gather(tied(second_shard, first_full), "seq", axis=0, tiled=True)
    cuts = [inner_local, inner_local, expert_total, 2 * shared_local, shared_local]
    cuts = [sum(cuts[: i + 1]) for i in range(4)]
    proj_gate, out_t, router_full, shared_flat, shared_down_t = jnp.split(second_full, cuts, axis=1)
    expert_shard = jnp.concatenate([expert_up, expert_down.transpose(0, 2, 1)], axis=2)
    expert_shard = expert_shard.reshape(MEMBERS, own_experts, slice_rows, 3 * EFF)

    def return_expert(grads, *after):
        send = grads.reshape(seq_count, slice_rows, 3 * EFF)
        return lax.all_to_all(tied(send, *after), "seq", 0, 0, tiled=True)

    def fetch_expert(own, *after):
        send = jnp.tile(expert_shard[:, own], (seq_count // MEMBERS, 1, 1))
        return lax.all_to_all(tied(send, *after), "seq", 0, 0, tiled=True).reshape(D, 3 * EFF)

    experts = [fetch_expert(0, first_full)]
    hidden_wide = hidden_full.astype(F32)
    scale_mix = rms_scale(hidden_wide)
    normed = (hidden_wide * scale_mix * gains[0]).astype(BF)
    ahead = [(i, i + 1) for i in range(seq_count - 1)]
    behind = [(i + 1, i) for i in range(seq_count - 1)]
    edge = lax.ppermute(normed[:, tokens - EDGE :], "seq", ahead)

    conv_in = mm(normed, conv_proj, ((2,), (0,)))
    edge, conv_in = lax.optimization_barrier((edge, conv_in))
    conv_in = jnp.concatenate([mm(edge, conv_proj, ((2,), (0,))), conv_in], axis=1)
    step_raw = mm(normed, step_full, ((2,), (0,))) + step_bias
    gate_pre = mm(normed, proj_gate, ((2,), (0,)))
    conv_weight = jnp.concatenate([conv_inner, conv_state], axis=1)
    conv_offset = jnp.concatenate([inner_bias, state_bias])
    positions = seq_rank * tokens + jnp.arange(-EDGE, tokens + EDGE, dtype=jnp.int32)
    segment_wide = segment_numbers(lengths, seq_order, positions)
    segments = segment_wide[:, EDGE : EDGE + tokens]
    segment_before = segment_wide[:, EDGE - 1 : EDGE]

    def keep(offset, begin, count):
        now = segment_wide[:, EDGE + begin : EDGE + begin + count]
        return (now == segment_wide[:, EDGE + begin - offset : EDGE + begin - offset + count])[
            :, :, None
        ]

    conv_out = conv_offset + conv_in[:, EDGE:] * conv_weight[0]
    for offset in range(1, CONV):
        shifted = conv_in[:, EDGE - offset : EDGE - offset + tokens]
        conv_out = conv_out + jnp.where(keep(offset, 0, tokens), shifted * conv_weight[offset], 0.0)
    act = jax.nn.silu(conv_out)
    signal, keys = act[:, :, :inner_local], act[:, :, inner_local:]
    step_sizes = jax.nn.softplus(step_raw)
    log_decay = -step_sizes * decay_rate
    row_index = jnp.arange(tokens, dtype=jnp.int32)
    until = (row_index[:, None] <= row_index[None, :]).astype(F32)
    running = jnp.einsum("ji,mjh->mih", until, log_decay, precision=HIGHEST)
    same_start = segments == segment_before
    same_end = segments == segments[:, -1:]
    entry_weight = jnp.where(same_start[:, :, None], jnp.exp(running), 0.0)
    passing = entry_weight[:, -1]
    leave_weight = (
        jnp.where(same_end[:, :, None], jnp.exp(running[:, -1:] - running), 0.0) * step_sizes
    )
    local_state = jnp.einsum(
        "mtc,mtn->mcn", spread(leave_weight) * signal, keys[:, :, :STATE], precision=HIGHEST
    )
    def by_pair(values):
        return values.reshape(micro, tokens, pairs, 2).transpose(0, 2, 1, 3)

    def flag(values):
        return jnp.broadcast_to(
            values.astype(F32)[:, None, :, None], (micro, pairs, tokens, 1)
        )

    cols = jnp.concatenate(
        [
            by_pair(running),
            by_pair(step_sizes),
            flag(segments),
            flag(segment_before),
            jnp.zeros((micro, pairs, tokens, 2), F32),
        ],
        axis=3,
    )
    rows = cols.transpose(0, 1, 3, 2)
    state_in, (local_out,) = chain(
        passing, tied(local_state, experts[0]), "seq", 1, (scan_forward(signal, keys, cols, rows),)
    )
    grad_group = lax.all_gather(
        tied(grad_rows, state_in), ("seq", "head"), axis=1, tiled=True, axis_index_groups=groups
    ).reshape(micro, MEMBERS, tokens, D)
    skip_wide, entry_wide = spread(skip_gain), spread(entry_weight)
    from_state = jnp.einsum(
        "mtn,mcn->mtc", keys[:, :, STATE:], state_in, precision=HIGHEST
    )
    mixer_out = local_out + entry_wide * from_state + skip_wide * signal
    gate_act = jax.nn.silu(gate_pre)
    gated = mixer_out * gate_act
    squares = lax.psum(jnp.sum(gated * gated, axis=2), "head")
    scale_gate = lax.rsqrt(squares / INNER + EPSILON)[:, :, None]
    gate_normed = (gated * scale_gate * gate_gain).astype(BF)
    mix_rows = reduce_rows(mm(gate_normed, out_t, ((2,), (1,)), BF), 1)
    resid_mid = resid_in + mix_rows
    scale_moe = rms_scale(resid_mid)
    moe_rows = (resid_mid * scale_moe * gains[1]).astype(BF)
    moe_group = gather_group(moe_rows, 2)

    expert_ids = jnp.arange(expert_total, dtype=jnp.int32)
    experts += [fetch_expert(own, moe_group) for own in range(1, own_experts)]

    def dense_weights(route_lines, rows):
        logits = mm(rows, router_full, ((rows.ndim - 1,), (0,)))
        named = jnp.any(route_lines[..., None] == expert_ids, axis=-3)
        top = jnp.max(jnp.where(named, logits, -jnp.inf), axis=-1, keepdims=True)
        raised = jnp.where(named, jnp.exp(logits - top), 0.0)
        return named, raised / jnp.sum(raised, axis=-1, keepdims=True)

    named_group, weight_group = dense_weights(route_group[:, :, :TOPK], moe_group)
    first_own = head_rank * experts_local + member * own_experts
    slot_index = jnp.arange(capacity, dtype=jnp.int32)
    ffn_parts, back_parts, expert_grads, weight_grads = [], [], [], []
    block = (((3,), (2,)), ((0, 1), (0, 1)))
    block_t = (((2,), (2,)), ((0, 1), (0, 1)))

    def flat(a):
        return a.reshape(-1, a.shape[-1])

    moe_own = lax.dynamic_index_in_dim(moe_group, member, 1, False)
    grad_own = lax.dynamic_index_in_dim(grad_group, member, 1, False)
    shared_both = mm(moe_own, shared_flat, ((2,), (0,)))
    shared_gate, shared_linear = shared_both[..., :shared_local], shared_both[..., shared_local:]
    shared_act = (jax.nn.silu(shared_gate) * shared_linear).astype(BF)
    shared_out = mm(shared_act, shared_down_t, ((2,), (1,)))
    shared_grad_act = mm(grad_own, shared_down_t, ((2,), (0,)))
    shared_grad = jnp.concatenate(
        [
            shared_grad_act * shared_linear * squash_slope(shared_gate),
            shared_grad_act * jax.nn.silu(shared_gate),
        ],
        axis=-1,
    ).astype(BF)
    shared_back = mm(shared_grad, shared_flat, ((2,), (1,)))
    grad_shared_up = mm(moe_own, shared_grad, ((0, 1), (0, 1)), BF)
    grad_shared_down_t = mm(grad_own, shared_act, ((0, 1), (0, 1)), BF)

    expert_backs, slot_parts = [], []
    for own in range(own_experts):
        weights = tied(experts[own], *((expert_grads[-1], shared_out) if own else ()))
        chosen = (expert_ids == first_own + own).astype(F32)
        named = jnp.sum(named_group * chosen, axis=-1)
        weight = jnp.sum(weight_group * chosen, axis=-1)
        rank = mm(named.astype(BF), until.astype(BF), ((2,), (0,))).astype(jnp.int32) - 1
        pick = (rank[:, :, None, :] == slot_index[:, None]) & (named[:, :, None, :] > 0.0)
        slots = pick.astype(BF)
        slot_weight = jnp.sum(pick * weight[:, :, None, :], axis=-1, keepdims=True)
        slot_rows = lax.dot_general(slots, moe_group, block, preferred_element_type=BF)
        slot_grads = lax.dot_general(slots, grad_group, block, preferred_element_type=BF)
        up_own, down_t = weights[:, : 2 * EFF], weights[:, 2 * EFF :]
        both = mm(slot_rows, up_own, ((3,), (0,)))
        up_gate, up_linear = both[..., :EFF], both[..., EFF:]
        hidden_act = (jax.nn.silu(up_gate) * up_linear).astype(BF)
        made = mm(hidden_act, down_t, ((3,), (1,)))
        slot_dot = jnp.sum(slot_grads.astype(F32) * made, axis=-1, keepdims=True)
        weight_grads.append(jnp.sum(pick * slot_dot, axis=2))
        made_low = (made * slot_weight).astype(BF)
        slot_parts.append(slots)
        ffn_parts.append(made_low)
        grads_low = (slot_grads * slot_weight).astype(BF)
        act_grad = mm(grads_low, down_t, ((3,), (0,)))
        both_grad = jnp.concatenate(
            [act_grad * up_linear * squash_slope(up_gate), act_grad * jax.nn.silu(up_gate)], axis=-1
        ).astype(BF)
        back = mm(both_grad, up_own, ((3,), (1,)), BF)
        back_parts.append(back)
        expert_grads.append(
            jnp.concatenate(
                [
                    mm(flat(slot_rows), flat(both_grad), ((0,), (0,)), BF),
                    mm(flat(grads_low), flat(hidden_act), ((0,), (0,)), BF),
                ],
                axis=1,
            )
        )

    def group_partial(parts, own_part):
        total = lax.dot_general(
            jnp.concatenate(slot_parts, axis=2),
            jnp.concatenate(parts, axis=2),
            block_t,
            preferred_element_type=BF,
        )
        mine = lax.dynamic_slice_in_dim(total, member, 1, 1).astype(F32) + own_part[:, None]
        return lax.dynamic_update_slice_in_dim(total, mine.astype(BF), member, 1)

    weight_grad = lax.all_to_all(
        jnp.stack(weight_grads, axis=-1)
        .reshape(micro, MEMBERS * head_count, row_count, own_experts)
        .transpose(1, 0, 2, 3),
        ("seq", "head"),
        0,
        0,
        tiled=True,
        axis_index_groups=groups,
    )
    weight_grad = (
        weight_grad.reshape(MEMBERS, head_count, micro, row_count, own_experts)
        .transpose(2, 3, 1, 0, 4)
        .reshape(micro, row_count, expert_total)
    )
    expert_backs = [return_expert(grads) for grads in expert_grads[:-1]]
    back_parts[-1] = tied(back_parts[-1], *expert_backs)
    back_partial = group_partial(back_parts, shared_back)
    back_rows = reduce_group(back_partial, 3)
    ffn_partial = group_partial(ffn_parts, shared_out)
    route_rows = own_rows(routes).transpose(0, 2, 1)
    named_rows, weight_rows = dense_weights(route_rows, moe_rows)
    weight_grad = jnp.where(named_rows, weight_grad, 0.0)
    logit_grad = weight_rows * (
        weight_grad - jnp.sum(weight_rows * weight_grad, axis=-1, keepdims=True)
    )
    logit_grad = logit_grad.astype(BF)
    grad_router = mm(moe_rows, logit_grad, ((0, 1), (0, 1)))
    back_rows = back_rows + mm(logit_grad, router_full, ((2,), (1,)))
    grad_mid = norm_back(back_rows, resid_mid, gains[1], scale_moe) + grad_rows.astype(F32)
    grad_moe_gain = jnp.sum(back_rows * resid_mid * scale_moe, axis=(0, 1))

    grad_mid_low = grad_mid.astype(BF)
    row_dots = jnp.sum(grad_mid_low.astype(F32) * mix_rows, axis=2)
    grad_mix, row_dots = cube_gather(
        [head_job(row_count, D, 1), head_job(8, row_count, 1)],
        [grad_mid_low, jnp.broadcast_to(row_dots[:, None], (micro, 8, row_count))],
        4,
    )
    grad_mix = grad_mix.reshape(micro, tokens, D)
    grad_mid_features = to_features(grad_mid)
    grad_gate_normed = mm(grad_mix, out_t, ((2,), (0,)))
    weighted = grad_gate_normed * gate_gain
    products = row_dots[:, :, 0].reshape(micro, tokens, 1) / scale_gate
    grad_gated = scale_gate * weighted - gated * (
        scale_gate * scale_gate * scale_gate * products / INNER
    )
    grad_gate_gain = jnp.sum(grad_gate_normed * gated * scale_gate, axis=(0, 1))
    grad_mixer = grad_gated * gate_act
    grad_gate_low = (grad_gated * mixer_out * squash_slope(gate_pre)).astype(BF)
    entry_grad = jnp.einsum(
        "mtc,mtn->mcn", entry_wide * grad_mixer, keys[:, :, STATE:], precision=HIGHEST
    )
    grad_out_t = mm(grad_mix, gate_normed, ((0, 1), (0, 1)), BF)
    grad_gate_proj = mm(normed, grad_gate_low, ((0, 1), (0, 1)), BF)
    second_grads = lane_padded(
        jnp.concatenate([grad_gate_proj, grad_out_t, grad_shared_up, grad_shared_down_t], axis=1)
    ).reshape(1, seq_count, slice_rows, -1)
    ffn_partial = ffn_partial.reshape(micro, MEMBERS * head_count, row_count, D)
    ffn_rows, grad_second = cube_reduce(
        [group_job(row_count, D, -1), seq_job(slice_rows, second_grads.shape[3], -1)],
        [tied(ffn_partial, entry_grad), second_grads],
        5,
    )
    grad_gate_in = mm(tied(grad_gate_low, entry_grad), proj_gate, ((2,), (1,)))
    state_grad, (ffn_rows, grad_gate_in) = chain(
        passing, entry_grad, "seq", -1, (ffn_rows, grad_gate_in)
    )
    output = to_features((resid_mid + ffn_rows).astype(BF))
    expert_backs.append(return_expert(expert_grads[-1], state_grad))
    grad_signal, grad_keys, grad_cols, grad_rows_part = scan_backward(
        signal, keys, cols, rows, grad_mixer, state_in, state_grad
    )
    grad_skip = jnp.sum(
        jnp.sum(grad_mixer * signal, axis=(0, 1)).reshape(heads_local, HEAD_DIM), axis=1
    )
    grad_act = jnp.concatenate([grad_signal + skip_wide * grad_mixer, grad_keys], axis=2)
    small = grad_cols[..., : SEG] + grad_rows_part[:, :, :SEG].transpose(0, 1, 3, 2)

    def by_head(values):
        return values.transpose(0, 2, 1, 3).reshape(micro, tokens, heads_local)

    grad_running, grad_steps = by_head(small[..., RUN:STEP]), by_head(small[..., STEP:SEG])
    grad_log = jnp.einsum("ij,mjh->mih", until, grad_running, precision=HIGHEST)
    grad_decay = -jnp.sum(grad_log * step_sizes, axis=(0, 1))
    grad_step_raw = (grad_steps - grad_log * decay_rate) * jax.nn.sigmoid(step_raw)
    grad_step_bias = jnp.sum(grad_step_raw, axis=(0, 1))
    grad_step_low = grad_step_raw.astype(BF)
    grad_conv = grad_act * squash_slope(conv_out)
    grad_next = jnp.concatenate(
        [grad_conv, lax.ppermute(grad_conv[:, :EDGE], "seq", behind)], axis=1
    )
    grad_conv_offset = jnp.sum(grad_conv, axis=(0, 1))
    grad_pre = grad_conv * conv_weight[0]
    taps = [jnp.sum(grad_conv * conv_in[:, EDGE:], axis=(0, 1))]
    for offset in range(1, CONV):
        shifted = conv_in[:, EDGE - offset : EDGE - offset + tokens]
        taps.append(
            jnp.sum(jnp.where(keep(offset, 0, tokens), grad_conv * shifted, 0.0), axis=(0, 1))
        )
        grad_pre = grad_pre + jnp.where(
            keep(offset, offset, tokens),
            grad_next[:, offset : offset + tokens] * conv_weight[offset],
            0.0,
        )
    grad_conv_weight = jnp.stack(taps)
    grad_pre = grad_pre.astype(BF)

    grad_first = (
        grad_gate_in
        + mm(grad_pre, conv_proj, ((2,), (1,)))
        + mm(grad_step_low, step_full, ((2,), (1,)))
    )
    grad_first_sums = lax.psum(jnp.sum(grad_first * gains[0] * hidden_wide, axis=2), "head")
    grad_conv_proj = mm(normed, grad_pre, ((0, 1), (0, 1)), BF)
    grad_step_proj = mm(normed, grad_step_low, ((0, 1), (0, 1)), BF)
    first_grads = lane_padded(
        jnp.concatenate([grad_conv_proj, grad_step_proj, grad_router.astype(BF)], axis=1)
    ).reshape(1, seq_count, slice_rows, -1)
    wide = local_width % 128 == 0
    grad_first = grad_first.astype(BF)
    if not wide:
        grad_first = grad_first.reshape(micro, tokens, head_count, local_width)
        grad_first = grad_first.transpose(0, 2, 1, 3)
    first_grads = tied(first_grads, expert_backs[-1])
    first_features, grad_first_w = cube_reduce(
        [
            head_job(tokens, local_width, -1, wide),
            seq_job(slice_rows, first_grads.shape[3], -1),
        ],
        [grad_first, first_grads],
        6,
    )
    resid_features = hidden.astype(F32)
    grad_in = scale_mix * (first_features * mix_gain) - resid_features * (
        scale_mix * scale_mix * scale_mix * grad_first_sums[:, :, None] / D
    )
    input_grad = grad_in + grad_mid_features
    cuts = [inner_local, inner_local, 2 * shared_local]
    cuts = [sum(cuts[: i + 1]) for i in range(3)]
    gate_w, out_w, shared_up_w, shared_down_w = jnp.split(grad_second[0], cuts + [sum(cuts[-1:]) + shared_local], axis=1)[:4]
    grad_first_w = grad_first_w[0]
    inner_w, step_w = grad_first_w[:, :inner_local], grad_first_w[:, channels : channels + heads_local]
    over_heads = jnp.concatenate(
        [
            grad_first_w[:, inner_local:channels],
            grad_first_w[:, channels + heads_local : channels + heads_local + expert_total],
        ],
        axis=1,
    )
    expert_w = jnp.stack(
        [
            jnp.sum(
                back.reshape(seq_count // MEMBERS, MEMBERS, slice_rows, 3 * EFF).astype(F32), axis=0
            )
            for back in expert_backs
        ],
        axis=1,
    ).reshape(experts_local, slice_rows, 3 * EFF)
    own_sizes = [CONV * inner_local, inner_local, inner_local, heads_local, heads_local, heads_local]
    own_small = in_rows(
        [
            grad_conv_weight[:, :inner_local],
            grad_conv_offset[:inner_local],
            grad_gate_gain,
            grad_step_bias,
            grad_decay,
            grad_skip,
            jnp.sum(first_features * resid_features * scale_mix, axis=(0, 1)),
        ]
    )
    all_sizes = [CONV * 2 * STATE, 2 * STATE, D]
    all_small = in_rows(
        [grad_conv_weight[:, inner_local:], grad_conv_offset[inner_local:], grad_moe_gain]
    )
    seq_bits, head_bits = bits_in("seq", seq_count), bits_in("head", head_count)
    over_heads = lane_padded(over_heads)[None]

    def plain_job(array, bits, slot_of):
        return Job([((0, array.shape[1]), (0, array.shape[2]), bits)], slot_of)

    heads_found, own_found, all_found = cube_gather(
        [
            plain_job(over_heads, head_bits, slot_in_head),
            plain_job(own_small, seq_bits, slot_in_seq),
            plain_job(all_small, seq_bits + head_bits, slot_in_mesh),
        ],
        [over_heads, own_small, all_small],
        7,
    )
    over_heads = jnp.sum(heads_found[0], axis=0)
    state_w, router_w = over_heads[:, : 2 * STATE], over_heads[:, 2 * STATE : 2 * STATE + expert_total]

    def taken(found, sizes):
        return jnp.split(jnp.sum(found[0], axis=0).reshape(-1), [sum(sizes[: i + 1]) for i in range(len(sizes))])

    conv_inner_w, inner_bias_w, gate_gain_w, step_bias_w, decay_w, skip_w, mix_gain_w = taken(
        own_found, own_sizes
    )
    conv_state_w, state_bias_w, moe_gain_w, _ = taken(all_found, all_sizes)
    return (
        output,
        input_grad,
        mix_gain_w[:local_width],
        jnp.stack([gate_w, inner_w]),
        state_w,
        step_w,
        conv_inner_w.reshape(CONV, inner_local),
        conv_state_w.reshape(CONV, 2 * STATE),
        inner_bias_w,
        state_bias_w,
        step_bias_w,
        decay_w,
        skip_w,
        gate_gain_w,
        out_w.T,
        lax.dynamic_slice_in_dim(moe_gain_w, head_rank * local_width, local_width, 0),
        router_w,
        expert_w[:, :, : 2 * EFF],
        expert_w[:, :, 2 * EFF :].transpose(0, 2, 1),
        shared_up_w.reshape(slice_rows, 2, shared_local),
        shared_down_w.T,
    )


def solution(mesh):
    return jax.shard_map(
        body,
        mesh=mesh,
        in_specs=(
            P(None, "seq", "head"),
            P(None, "seq", "head"),
            P(),
            P(),
            P(None, "seq", None),
            P("head"),
            P(None, "seq", "head"),
            P("seq", None),
            P("seq", "head"),
            P(None, "head"),
            P(),
            P("head"),
            P(),
            P("head"),
            P("head"),
            P("head"),
            P("head"),
            P("head", "seq"),
            P("head"),
            P("seq", None),
            P("head", "seq", None),
            P("head", None, "seq"),
            P("seq", None, "head"),
            P("head", "seq"),
        ),
        out_specs=(
            P(None, "seq", "head"),
            P(None, "seq", "head"),
            P("head"),
            P(None, "seq", "head"),
            P("seq", None),
            P("seq", "head"),
            P(None, "head"),
            P(),
            P("head"),
            P(),
            P("head"),
            P("head"),
            P("head"),
            P("head"),
            P("head", "seq"),
            P("head"),
            P("seq", None),
            P("head", "seq", None),
            P("head", None, "seq"),
            P("seq", None, "head"),
            P("head", "seq"),
        ),
        check_vma=False,
    )
```

time: 6010 us -> 1450 us (0.24)
  waiting for transfers between devices: 4240 us -> 238 us
  blocking collectives: 561 us -> 12.3 us
  Pallas kernels: 0 us -> 526 us
  local copies, waits for them, and re-layouts: 443 us -> 156 us
  other arithmetic: 283 us -> 128 us
  matrix products: 408 us -> 259 us
  starting transfers between devices: 11.6 us -> 105 us
    all_gather x27 -> x2, waiting for transfers between devices: 2040 us -> 0.01 us  [the longest x1 0.01 us: body(): lax.all_gather(tied(second_shard, first_full), 'seq', axis=0, tiled=True)]
    reduce_scatter x16 -> x0, waiting for transfers between devices: 1810 us -> none  [the longest x2 811 us: reduce_weights(): lax.psum_scatter(matrices[5].astype(jnp.bfloat16), 'seq', scatter_dimensi...]
    pallas_call x0 -> x10, Pallas kernels: none -> 526 us  [the longest x4 266 us: cube_reduce(): pl.pallas_call(functools.partial(reduce_kernel, jobs), out_shape=tuple(ou...]
    all_gather x16 -> x0, blocking collectives: 464 us -> none  [the longest x3 105 us: fetch_weights(): lax.all_gather(shards[2], 'seq', axis=0, tiled=True)]
    unnamed x62 -> x2, waiting for transfers between devices: 375 us -> 0.03 us
    all_to_all x0 -> x7, waiting for transfers between devices: none -> 178 us  [the longest x2 129 us: fetch_expert(): lax.all_to_all(tied(send, *after), 'seq', 0, 0, tiled=True)]
    dot_general x142 -> x48, matrix products: 408 us -> 259 us  [the longest x37 190 us: mm(): return lax.dot_general(a, b, (dims, ((), ())), preferred_element_type=out)]
    dynamic_update_slice x36 -> x0, local copies, waits for them, and re-layouts: 149 us -> none  [scan_device(): lax.scan(jax.checkpoint(ssd_block), carry_in, block_parts)]
  transfers between devices with their start and end apart: 57 -> 25, of which waited for: 39 -> 12; matrix products, arithmetic and copies ran while one was open for 12% -> 28% of each run, Pallas kernels for 0% -> 20%
where the time goes in v1:
time: 1450 us; the launch traced here: 1440 us
  Pallas kernels  526 us (36%)
  matrix products  259 us (18%)
  waiting for transfers between devices  238 us (16%)
  local copies, waits for them, and re-layouts  156 us (11%)
  other arithmetic  128 us (9%)
  starting transfers between devices  105 us (7%)
  between operations  17.1 us (1%)
    pallas_call x4, Pallas kernels, cube_reduce(): pl.pallas_call(functools.partial(reduce_kernel, jobs), out_shape=tuple(ou...  266 us
    dot_general x37, matrix products, mm(): return lax.dot_general(a, b, (dims, ((), ())), preferred_element_type=out)  190 us
    pallas_call x4, Pallas kernels, cube_gather(): pl.pallas_call(functools.partial(gather_kernel, jobs), out_shape=tuple((j...  180 us
    all_to_all x2, waiting for transfers between devices, fetch_expert(): lax.all_to_all(tied(send, *after), 'seq', 0, 0, tiled=True)  129 us
    pallas_call x1, Pallas kernels, scan_backward(): pl.pallas_call(backward_kernel, grid=(micro, pairs), out_shape=(jax.Shape...  60.6 us
    all_to_all x2, waiting for transfers between devices, return_expert(): return lax.all_to_all(tied(send, *after), 'seq', 0, 0, tiled=True)  48.4 us
    ppermute x6, starting transfers between devices, pull(): passing = lax.ppermute(rows, axis, pairs)[:, 0, :heads]  40.5 us
    unnamed x327, local copies, waits for them, and re-layouts  38.5 us
  transfers between devices with their start and end apart: 25, of which 12 were waited for; matrix products, arithmetic and copies ran while one was open for 28% of the time, Pallas kernels for 20%

profile of v1, /device:TPU:0, one launch (start us, length us, event | category | flops | bytes accessed | tf_op | source)
XLA Modules:
  0.0 1441.7 jit_solution(11583577667901050098)
XLA Ops:
  19.0 74.6 %shard_map.391 = (bf16[2,512,1536]{2,1,0:T(8,128)(2,1)}, bf16[2,512,1536]{2,1,0:T(8,128)(2,1)}, f32[1,8,1536]{2,1,0:T(8,128)}, bf16[1,8,192,1152]{3,2,1,0:T(8,128)(2,1)}, s32[2,4,8,512]{3,2,1,0:T(8,128)}) custom-call(bf16[2,512,384]{2,1,0:T(8,128)(2,1)} %refs_0_.1, bf16[2,512,384]{2,1,0:T(8,128)(2,1)} %refs_1_.1, f32[1,8,384]{2,1,0:T(8,128)} %pad.45.refs_2_, ...), custom_call_target="tpu_custom_call" | custom-call | bytes 104857600 | tf_op jit(solution)/shard_map/pallas_call | solution.py:141
  126.1 15.4 %collective-permute-done = bf16[2,8,1536]{2,1,0:T(8,128)(2,1)} collective-permute-done((bf16[2,8,1536]{2,1,0:T(8,128)(2,1)S(1)}, bf16[2,8,1536]{2,1,0:T(8,128)(2,1)}, u32[]{:S(2)}, u32[]{:S(2)}) %collective-permute-start) | collective-permute-done | bytes 49184 | tf_op jit(solution)/shard_map/ppermute | solution.py:781
  144.0 10.1 fusion.35
  162.0 129.2 %all-to-all-done = bf16[8,192,1536]{2,1,0:T(8,128)(2,1)} async-done(((bf16[8,192,1536]{2,1,0:T(8,128)(2,1)}), bf16[8,192,1536]{2,1,0:T(8,128)(2,1)}, u32[]{:S(2)}, u32[]{:S(2)}) %all-to-all-start) | async-done | bytes 4718624 | tf_op jit(solution)/shard_map/all_to_all | solution.py:773
  301.0 19.6 %shard_map.392 = f32[2,512,768]{2,1,0:T(8,128)S(1)} custom-call(f32[2,512,768]{2,1,0:T(8,128)S(1)} %slice.334.x_ref, f32[2,512,256]{2,1,0:T(8,128)S(1)} %slice.337.keys_ref, f32[2,6,512,8]{3,2,1,0:T(8,128)S(1)} %copy.319.cols_ref, f32[2,6,8,512]{3,2,1,0:T(8,128)S(1)} %bitcast.320), custom_call_target="tpu_custom_call" | custom-call | flops 1101004800 | bytes 9437184 | tf_op jit(solution)/shard_map/pallas_call | solution.py:430
  323.7 23.8 %collective-permute-start.2 = (f32[2,8,128]{1,2,0:T(8,128)S(1)}, f32[2,8,128]{1,2,0:T(8,128)S(1)}, u32[]{:S(2)}, u32[]{:S(2)}) collective-permute-start(f32[2,8,128]{1,2,0:T(8,128)S(1)} %pad.48), channel_id=1, source_target_pairs={{0,4},{4,8},{8,12},{12,16},{16,20},{20,24},{24,28},{1,5},{5,9},{9,... | collective-permute-start | bytes 24584 | tf_op jit(solution)/shard_map/ppermute | solution.py:585
  350.0 8.7 collective-permute-start.3
  362.3 7.4 collective-permute-start.6
  401.6 15.1 %collective-permute-done.11 = f32[2,8,128]{1,2,0:T(8,128)S(1)} collective-permute-done((f32[2,8,128]{1,2,0:T(8,128)S(1)}, f32[2,8,128]{1,2,0:T(8,128)S(1)}, u32[]{:S(2)}, u32[]{:S(2)}) %collective-permute-start.11) | collective-permute-done | bytes 8224 | tf_op jit(solution)/shard_map/ppermute | solution.py:585
  457.8 21.8 %shard_map.393 = f32[2,128,1536]{2,1,0:T(8,128)S(1)} custom-call(bf16[2,4,128,1536]{3,2,1,0:T(8,128)(2,1)} %bitcast.376), custom_call_target="tpu_custom_call" | custom-call | bytes 104857600 | tf_op jit(solution)/shard_map/pallas_call | solution.py:271
  484.4 58.3 %shard_map.394 = bf16[2,16,128,1536]{3,2,1,0:T(8,128)(2,1)} custom-call(bf16[2,128,1536]{2,1,0:T(8,128)(2,1)} %multiply_convert_fusion.10.refs_0_), custom_call_target="tpu_custom_call" | custom-call | bytes 104857600 | tf_op jit(solution)/shard_map/pallas_call | solution.py:141
  550.7 8.4 fusion.145
  573.2 7.9 fusion.202
  581.1 9.0 fusion.88
  606.2 7.8 fusion.4
  646.5 7.2 multiply_convert_fusion.1
  659.3 7.8 fusion.51
  671.8 7.1 fusion.6
  715.9 12.1 fusion.11
  735.8 8.8 fusion.87
  750.1 8.6 fusion.49
  765.7 48.4 %all-to-all-done.2 = bf16[8,192,1536]{2,1,0:T(8,128)(2,1)} async-done(((bf16[8,192,1536]{2,1,0:T(8,128)(2,1)}), bf16[8,192,1536]{2,1,0:T(8,128)(2,1)}, u32[]{:S(2)}, u32[]{:S(2)}) %all-to-all-start.2) | async-done | bytes 4718624 | tf_op jit(solution)/shard_map/all_to_all | solution.py:769
  814.1 12.0 fusion.7
  832.7 53.9 %shard_map.395 = f32[2,128,1536]{2,1,0:T(8,128)S(1)} custom-call(bf16[2,16,128,1536]{3,2,1,0:T(8,128)(2,1)} %bitcast.357), custom_call_target="tpu_custom_call" | custom-call | bytes 104857600 | tf_op jit(solution)/shard_map/pallas_call | solution.py:271
  892.9 26.0 %shard_map.396 = (bf16[2,4,128,1536]{3,2,1,0:T(8,128)(2,1)}, f32[2,4,8,128]{3,2,1,0:T(8,128)}) custom-call(bf16[2,128,1536]{2,1,0:T(8,128)(2,1)} %get-tuple-element.250.refs_0_, f32[2,8,128]{2,1,0:T(8,128)} %broadcast_in_dim.229.refs_1_), custom_call_target="tpu_custom_call" | custom-call | bytes 104857600 | tf_op jit(solution)/shard_map/pallas_call | solution.py:141
  948.3 10.3 copy.344
  958.6 127.1 %shard_map.397 = (f32[2,128,1536]{2,1,0:T(8,128)S(1)}, f32[1,192,2304]{2,1,0:T(8,128)}) custom-call(bf16[2,16,128,1536]{3,2,1,0:T(8,128)(2,1)} %bitcast.344, bf16[1,8,192,2304]{3,2,1,0:T(8,128)(2,1)} %bitcast.341), custom_call_target="tpu_custom_call" | custom-call | bytes 104857600 | tf_op jit(solution)/shard_map/pallas_call | solution.py:271
  1137.8 10.2 collective-permute-done.14
  1185.8 60.6 %shard_map.398 = (f32[2,512,768]{2,1,0:T(8,128)S(1)}, f32[2,512,256]{2,1,0:T(8,128)S(1)}, f32[2,6,512,8]{3,2,1,0:T(8,128)S(1)}, f32[2,6,8,512]{3,2,1,0:T(8,128)S(1)}) custom-call(f32[2,512,768]{2,1,0:T(8,128)S(1)} %copy-done.3, f32[2,512,256]{2,1,0:T(8,128)S(1)} %copy-done.9, f32[2,6,512,8]{3,2,1,0:T(8,128)S(1)} %copy-done.1, ...), custom_call_target="tpu_custom_call" | custom-call | tf_op jit(solution)/shard_map/pallas_call | solution.py:537
  1284.7 11.5 concatenate.92
  1319.9 63.4 %shard_map.399 = (f32[2,512,384]{2,1,0:T(8,128)}, f32[1,192,1152]{2,1,0:T(8,128)S(1)}) custom-call(bf16[2,512,1536]{2,1,0:T(8,128)(2,1)} %get-tuple-element.261.refs_0_, bf16[1,8,192,1152]{3,2,1,0:T(8,128)(2,1)} %bitcast.356), custom_call_target="tpu_custom_call" | custom-call | bytes 104857600 | tf_op jit(solution)/shard_map/pallas_call | solution.py:271
  1388.0 20.9 %shard_map.400 = (f32[1,4,192,384]{3,2,1,0:T(8,128)}, f32[1,8,40,128]{3,2,1,0:T(8,128)}, f32[1,32,24,128]{3,2,1,0:T(8,128)}) custom-call(f32[1,192,384]{2,1,0:T(8,128)} %fusion.151.refs_0_, f32[1,40,128]{2,1,0:T(8,128)} %pad_bitcast_fusion.refs_1_, f32[1,24,128]{2,1,0:T(8,128)} %fusion.166.refs_2_), custom_call_target="tpu_custom_call" | custom-call | bytes 104857600 | tf_op jit(solution)/shard_map/pallas_call | solution.py:141
  (605 shorter events, 511.4 us)
Async XLA Ops:
  7.2 426.7 %all-gather.3.cloned.1.call-start = ((), (), s32[]{:S(2)}) async-start(), calls=%async_computation.7 | async-start | bytes 8404992 | tf_op jit(solution)/shard_map/all_gather | solution.py:760
  12.0 81.7 %copy-start.50 = (bf16[8,192,1024]{2,1,0:T(8,128)(2,1)S(1)}, bf16[8,192,1024]{2,1,0:T(8,128)(2,1)}, u32[]{:S(2)}) copy-start(bf16[8,192,1024]{2,1,0:T(8,128)(2,1)} %param.44) | copy-start | bytes 9437188
  99.8 191.4 %all-to-all-start = ((bf16[8,192,1536]{2,1,0:T(8,128)(2,1)}), bf16[8,192,1536]{2,1,0:T(8,128)(2,1)}, u32[]{:S(2)}, u32[]{:S(2)}) async-start(bf16[8,192,1536]{2,1,0:T(8,128)(2,1)} %bitcast.348), calls=%async_computation | async-start | bytes 9437184 | tf_op jit(solution)/shard_map/all_to_all | solution.py:773
  104.7 495.0 %all-gather.5.cloned.1.call-start = ((), (), s32[]{:S(2)}) async-start(), calls=%async_computation.8 | async-start | bytes 13369344 | tf_op jit(solution)/shard_map/all_gather | solution.py:844
  105.7 376.5 %copy-start.67 = (f32[1536]{0:T(1024)}, f32[1536]{0:T(1024)S(1)}, u32[]{:S(2)}) copy-start(f32[1536]{0:T(1024)S(1)} %get-tuple-element.232) | copy-start | bytes 18436
  107.5 34.0 %collective-permute-start = (bf16[2,8,1536]{2,1,0:T(8,128)(2,1)S(1)}, bf16[2,8,1536]{2,1,0:T(8,128)(2,1)}, u32[]{:S(2)}, u32[]{:S(2)}) collective-permute-start(bf16[2,8,1536]{2,1,0:T(8,128)(2,1)S(1)} %slice.321), channel_id=1, source_target_pairs={{0,4},{4,8},{8,12},{12,16},{16,20},{20,24},{24,28},{1,5},{5,9},{9,... | collective-permute-start | bytes 147464 | tf_op jit(solution)/shard_map/ppermute | solution.py:781
  291.2 31.1 %collective-permute-start.1 = (bf16[2,768,128]{2,1,0:T(8,128)(2,1)}, bf16[2,768,128]{2,1,0:T(8,128)(2,1)}, u32[]{:S(2)}, u32[]{:S(2)}) collective-permute-start(bf16[2,768,128]{2,1,0:T(8,128)(2,1)} %fusion.66), channel_id=1, source_target_pairs={{0,4},{4,8},{8,12},{12,16},{16,20},{20,24},{24,28},{1,5},{5,9},{9,... | collective-permute-start | bytes 1179656 | tf_op jit(solution)/shard_map/ppermute | solution.py:583
  322.3 38.7 %collective-permute-start.5 = (bf16[2,768,128]{2,1,0:T(8,128)(2,1)}, bf16[2,768,128]{2,1,0:T(8,128)(2,1)S(1)}, u32[]{:S(2)}, u32[]{:S(2)}) collective-permute-start(bf16[2,768,128]{2,1,0:T(8,128)(2,1)} %collective-permute-done.1), channel_id=1, source_target_pairs={{0,4},{4,8},{8,12},{12,16},{16,20},{20,24},{24,28},{1,5},{5,9},{9,... | collective-permute-start | bytes 1179656 | tf_op jit(solution)/shard_map/ppermute | solution.py:583
  323.7 26.3 %collective-permute-start.2 = (f32[2,8,128]{1,2,0:T(8,128)S(1)}, f32[2,8,128]{1,2,0:T(8,128)S(1)}, u32[]{:S(2)}, u32[]{:S(2)}) collective-permute-start(f32[2,8,128]{1,2,0:T(8,128)S(1)} %pad.48), channel_id=1, source_target_pairs={{0,4},{4,8},{8,12},{12,16},{16,20},{20,24},{24,28},{1,5},{5,9},{9,... | collective-permute-start | bytes 24584 | tf_op jit(solution)/shard_map/ppermute | solution.py:585
  350.0 10.8 collective-permute-start.3
  362.3 16.3 %collective-permute-start.6 = (bf16[2,768,128]{2,1,0:T(8,128)(2,1)S(1)}, bf16[2,768,128]{2,1,0:T(8,128)(2,1)S(1)}, u32[]{:S(2)}, u32[]{:S(2)}) collective-permute-start(bf16[2,768,128]{2,1,0:T(8,128)(2,1)S(1)} %fusion.125), channel_id=1, source_target_pairs={{0,8},{4,12},{8,16},{12,20},{16,24},{20,28},{1,9},{5,13},{9,17},{1... | collective-permute-start | bytes 1179656 | tf_op jit(solution)/shard_map/ppermute | solution.py:583
  369.7 8.5 collective-permute-start.4
  380.0 11.6 collective-permute-start.7
  393.4 6.9 collective-permute-start.10
  400.3 16.5 %collective-permute-start.11 = (f32[2,8,128]{1,2,0:T(8,128)S(1)}, f32[2,8,128]{1,2,0:T(8,128)S(1)}, u32[]{:S(2)}, u32[]{:S(2)}) collective-permute-start(f32[2,8,128]{1,2,0:T(8,128)S(1)} %pad.51), channel_id=1, source_target_pairs={{4,0},{8,4},{12,8},{16,12},{20,16},{24,20},{28,24},{5,1},{9,5},{13... | collective-permute-start | bytes 24584 | tf_op jit(solution)/shard_map/ppermute | solution.py:585
  401.6 160.4 %copy-start.72 = (pred[2,128,32]{1,2,0:T(8,128)(4,1)}, pred[2,128,32]{1,2,0:T(8,128)(4,1)S(1)}, u32[]{:S(2)}) copy-start(pred[2,128,32]{1,2,0:T(8,128)(4,1)S(1)} %fusion.153) | copy-start | bytes 24580
  416.9 10.1 collective-permute-start.12
  545.4 113.9 %all-to-all-start.1 = ((bf16[8,192,1536]{2,1,0:T(8,128)(2,1)}), bf16[8,192,1536]{2,1,0:T(8,128)(2,1)}, u32[]{:S(2)}, u32[]{:S(2)}) async-start(bf16[8,192,1536]{2,1,0:T(8,128)(2,1)} %bitcast.349), calls=%async_computation.1 | async-start | bytes 9437184 | tf_op jit(solution)/shard_map/all_to_all | solution.py:773
  682.5 20.6 %all-to-all-start.3 = ((f32[16,2,128,2]{2,3,1,0:T(2,128)}), f32[16,2,128,2]{2,3,1,0:T(2,128)S(1)}, u32[]{:S(2)}, u32[]{:S(2)}) async-start(f32[16,2,128,2]{2,3,1,0:T(2,128)} %copy.334), calls=%async_computation.3 | async-start | bytes 65536 | tf_op jit(solution)/shard_map/all_to_all | solution.py:950
  703.2 110.9 %all-to-all-start.2 = ((bf16[8,192,1536]{2,1,0:T(8,128)(2,1)}), bf16[8,192,1536]{2,1,0:T(8,128)(2,1)}, u32[]{:S(2)}, u32[]{:S(2)}) async-start(bf16[8,192,1536]{2,1,0:T(8,128)(2,1)} %bitcast.350), calls=%async_computation.2 | async-start | bytes 9437184 | tf_op jit(solution)/shard_map/all_to_all | solution.py:769
  940.1 152.0 %collective-permute-start.8 = (bf16[2,768,128]{2,1,0:T(8,128)(2,1)}, bf16[2,768,128]{2,1,0:T(8,128)(2,1)}, u32[]{:S(2)}, u32[]{:S(2)}) collective-permute-start(bf16[2,768,128]{2,1,0:T(8,128)(2,1)} %fusion.61), channel_id=1, source_target_pairs={{4,0},{8,4},{12,8},{16,12},{20,16},{24,20},{28,24},{5,1},{9,5},{13... | collective-permute-start | bytes 1179656 | tf_op jit(solution)/shard_map/ppermute | solution.py:583
  958.6 127.2 %copy-start.55 = (bf16[2,512,768]{2,1,0:T(8,128)(2,1)S(1)}, bf16[2,512,768]{2,1,0:T(8,128)(2,1)}, u32[]{:S(2)}) copy-start(bf16[2,512,768]{2,1,0:T(8,128)(2,1)} %copy-done.54) | copy-start | bytes 4718596
  1092.0 12.1 collective-permute-start.9
  1097.6 20.6 %all-to-all-start.4 = ((bf16[2,1,128,1536]{2,0,1,3:T(2,128)(2,1)}), bf16[2,1,128,1536]{2,0,1,3:T(2,128)(2,1)}, u32[]{:S(2)}, u32[]{:S(2)}) async-start(bf16[2,1,128,1536]{2,0,1,3:T(2,128)(2,1)} %copy.345), calls=%async_computation.4 | async-start | bytes 1572864 | tf_op jit(solution)/shard_map/all_to_all | solution.py:629
  1106.3 16.2 %collective-permute-start.13 = (bf16[2,768,128]{2,1,0:T(8,128)(2,1)}, bf16[2,768,128]{2,1,0:T(8,128)(2,1)}, u32[]{:S(2)}, u32[]{:S(2)}) collective-permute-start(bf16[2,768,128]{2,1,0:T(8,128)(2,1)} %fusion.126), channel_id=1, source_target_pairs={{8,0},{12,4},{16,8},{20,12},{24,16},{28,20},{9,1},{13,5},{17,9},{2... | collective-permute-start | bytes 1179656 | tf_op jit(solution)/shard_map/ppermute | solution.py:583
  1118.2 32.6 %all-to-all-start.6 = ((f32[2,1,128,1536]{2,0,1,3:T(2,128)}), f32[2,1,128,1536]{2,0,1,3:T(2,128)}, u32[]{:S(2)}, u32[]{:S(2)}) async-start(f32[2,1,128,1536]{2,0,1,3:T(2,128)} %copy.356), calls=%async_computation.6 | async-start | bytes 3145728 | tf_op jit(solution)/shard_map/all_to_all | solution.py:629
  1125.0 23.0 %collective-permute-start.14 = (bf16[2,768,128]{2,1,0:T(8,128)(2,1)}, bf16[2,768,128]{2,1,0:T(8,128)(2,1)}, u32[]{:S(2)}, u32[]{:S(2)}) collective-permute-start(bf16[2,768,128]{2,1,0:T(8,128)(2,1)} %fusion.141), channel_id=1, source_target_pairs={{16,0},{20,4},{24,8},{28,12},{17,1},{21,5},{25,9},{29,13},{18,2},{... | collective-permute-start | bytes 1179656 | tf_op jit(solution)/shard_map/ppermute | solution.py:583
  1150.8 169.1 %all-to-all-start.5 = ((bf16[8,192,1536]{2,1,0:T(8,128)(2,1)}), bf16[8,192,1536]{2,1,0:T(8,128)(2,1)}, u32[]{:S(2)}, u32[]{:S(2)}) async-start(bf16[8,192,1536]{2,1,0:T(8,128)(2,1)} %bitcast.347), calls=%async_computation.5 | async-start | bytes 9437184 | tf_op jit(solution)/shard_map/all_to_all | solution.py:769
  1258.9 13.9 collective-permute-start.15
  1319.8 63.6 %copy-start.43 = (f32[2,1,128,4,384]{4,2,3,0,1:T(8,128)S(1)}, f32[2,1,128,4,384]{4,2,3,0,1:T(8,128)}, u32[]{:S(2)}) copy-start(f32[2,1,128,4,384]{4,2,3,0,1:T(8,128)} %copy.357) | copy-start | bytes 4718596
  1319.8 63.6 %copy-start.49 = (bf16[2,512,384]{2,1,0:T(8,128)(2,1)S(1)}, bf16[2,512,384]{2,1,0:T(8,128)(2,1)}, u32[]{:S(2)}) copy-start(bf16[2,512,384]{2,1,0:T(8,128)(2,1)} %refs_0_.1) | copy-start | bytes 2359300
  1319.8 63.6 %copy-start.91 = (f32[2,512]{1,0:T(2,128)S(1)}, f32[2,512]{1,0:T(2,128)}, u32[]{:S(2)}) copy-start(f32[2,512]{1,0:T(2,128)} %copy-done.90) | copy-start | bytes 12292
  (154 other events, 1756.6 us)
Sparse Core Ops, SparseCore 0:
  93.7 203.0 all-gather.2
  393.5 82.3 all-gather.4

commit v2 on v1

--- a/solution.py
+++ b/solution.py
@@ -90,39 +90,46 @@
     me = (lax.axis_index("seq"), lax.axis_index("head"))
     number = len(jobs)
     x_refs, o_refs, sems = refs[:number], refs[number : 2 * number], refs[2 * number :]
+    owns, copies, waited = [], {}, set()
+    for j in range(number):
+        load = pltpu.make_async_copy(x_refs[j], sems[4 * j + 3], sems[4 * j + 2].at[0])
+        load.start()
+        owns.append(load)
     greet(jobs, me)
-    owns, copies, waited = [], {}, set()
-    for step in range(max(job.depth for job in jobs)):
-        for j, job in enumerate(jobs):
-            if step >= job.depth:
-                continue
-            send_sem, recv_sem, own_sem = sems[3 * j : 3 * j + 3]
-            x_ref, o_ref = x_refs[j], o_refs[j]
-            width = x_ref.shape[2]
-            for p, (rows, columns, order) in enumerate(job.parts):
-                other = flip_of(order[step])
-                for place, held in enumerate(flips(order[:step])):
-                    if place and (j, p, place) not in waited:
-                        copies[j, p, place].wait_recv()
-                        waited.add((j, p, place))
-                    dst = job.view(o_ref, across(me, held), rows, columns, width)
-                    src = dst if place else x_ref.at[:, pl.ds(*rows), pl.ds(*columns)]
-                    arriving = place + (1 << step)
-                    copy = pltpu.make_async_remote_copy(
-                        src_ref=src,
-                        dst_ref=dst,
-                        send_sem=send_sem.at[p, arriving],
-                        recv_sem=recv_sem.at[p, arriving],
-                        device_id=across(me, other),
-                        device_id_type=MESH,
-                    )
-                    copy.start()
-                    copies[j, p, arriving] = copy
-            if step == 0:
-                whole = ((0, x_ref.shape[1]), (0, width))
-                own = pltpu.make_async_copy(x_ref, job.view(o_ref, me, *whole, width), own_sem)
-                own.start()
-                owns.append(own)
+    deepest_first = sorted(range(number), key=lambda j: -jobs[j].depth)
+    turns = [(0, j) for j in range(number)]
+    turns += [(step, j) for j in deepest_first for step in range(1, jobs[j].depth)]
+    for step, j in turns:
+        job = jobs[j]
+        send_sem, recv_sem, own_sem, own_block = sems[4 * j : 4 * j + 4]
+        x_ref, o_ref = x_refs[j], o_refs[j]
+        width = x_ref.shape[2]
+        for p, (rows, columns, order) in enumerate(job.parts):
+            other = flip_of(order[step])
+            for place, held in enumerate(flips(order[:step])):
+                if place and (j, p, place) not in waited:
+                    copies[j, p, place].wait_recv()
+                    waited.add((j, p, place))
+                dst = job.view(o_ref, across(me, held), rows, columns, width)
+                src = dst if place else x_ref.at[:, pl.ds(*rows), pl.ds(*columns)]
+                arriving = place + (1 << step)
+                copy = pltpu.make_async_remote_copy(
+                    src_ref=src,
+                    dst_ref=dst,
+                    send_sem=send_sem.at[p, arriving],
+                    recv_sem=recv_sem.at[p, arriving],
+                    device_id=across(me, other),
+                    device_id_type=MESH,
+                )
+                copy.start()
+                copies[j, p, arriving] = copy
+        if step == 0:
+            whole = ((0, x_ref.shape[1]), (0, width))
+            owns[j].wait()
+            owns[j] = pltpu.make_async_copy(
+                own_block, job.view(o_ref, me, *whole, width), own_sem.at[1]
+            )
+            owns[j].start()
     for key, copy in copies.items():
         if key not in waited:
             copy.wait_recv()
@@ -135,9 +142,10 @@
 def cube_gather(jobs, arrays, collective_id, weight=100 << 20):
     anywhere = pl.BlockSpec(memory_space=pl.ANY)
     scratch = []
-    for job in jobs:
-        for shape in ((len(job.parts), job.count),) * 2 + ((),):
-            scratch.append(pltpu.SemaphoreType.DMA(shape) if shape else pltpu.SemaphoreType.DMA)
+    for job, x in zip(jobs, arrays, strict=True):
+        for shape in ((len(job.parts), job.count),) * 2 + ((2,),):
+            scratch.append(pltpu.SemaphoreType.DMA(shape))
+        scratch.append(pltpu.VMEM(x.shape, x.dtype))
     return pl.pallas_call(
         functools.partial(gather_kernel, jobs),
         out_shape=tuple(
@@ -147,7 +155,9 @@
         in_specs=[anywhere] * len(jobs),
         out_specs=(anywhere,) * len(jobs),
         scratch_shapes=scratch,
-        compiler_params=pltpu.CompilerParams(collective_id=collective_id, has_side_effects=True),
+        compiler_params=pltpu.CompilerParams(
+            collective_id=collective_id, has_side_effects=True, vmem_limit_bytes=32 << 20
+        ),
         cost_estimate=pl.CostEstimate(flops=0, bytes_accessed=weight, transcendentals=0),
     )(*arrays)
 
@@ -326,16 +336,118 @@
 
 def seq_job(rows, columns, way):
     bits = bits_in("seq", lax.axis_size("seq"))
-    cut = rows * 5 // 6 // 16 * 16
-    parts = [
-        ((0, cut), (0, columns), bits[::-1][::way]),
-        ((cut, rows - cut), (0, columns), (bits[:1] + bits[:0:-1])[::way]),
-    ]
+    cut = rows * 7 // 12 // 16 * 16
+    parts = []
+    for _, some in thirds(rows, columns):
+        parts.append(((0, cut), some, bits[::-1][::way]))
+        parts.append(((cut, rows - cut), some, (bits[:1] + bits[:0:-1])[::way]))
     return Job(parts, slot_in_seq)
 
 
 def members_job(rows, columns):
     return Job([((0, rows), (0, columns), bits_in("seq", MEMBERS))], slot_in_members)
+
+
+def chain_kernel(way, widths, state_ref, pass_ref, out_ref, far, far_pass, low, near_pass, sems):
+    count = lax.axis_size("seq")
+    me, head = lax.axis_index("seq"), lax.axis_index("head")
+    micro, heads = pass_ref.shape[0], pass_ref.shape[1]
+    place = me if way == 1 else count - 1 - me
+    barrier = pltpu.get_barrier_semaphore()
+    expected = 0
+    for width in sorted(set(widths)):
+        for there, steps in ((place + width < count, width), (place >= width, -width)):
+            expected = expected + there.astype(jnp.int32)
+
+            @pl.when(there)
+            def _():
+                pl.semaphore_signal(
+                    barrier, inc=1, device_id=(me + way * steps, head), device_id_type=MESH
+                )
+
+    pl.semaphore_wait(barrier, expected)
+
+    def rows_of(h):
+        return pl.ds(h * HEAD_DIM, HEAD_DIM)
+
+    low[0] = state_ref[...].astype(BF)
+    near_pass[0] = pass_ref[...]
+    for hop, width in enumerate(widths):
+        sends, gets = place + width < count, place >= width
+        copies = [
+            pltpu.make_async_remote_copy(
+                src_ref=src.at[hop],
+                dst_ref=dst.at[hop],
+                send_sem=sems.at[0, i, hop],
+                recv_sem=sems.at[1, i, hop],
+                device_id=(me + way * width, head),
+                device_id_type=MESH,
+            )
+            for i, (src, dst) in enumerate(((low, far), (near_pass, far_pass)))
+        ]
+
+        @pl.when(sends)
+        def _():
+            for copy in copies:
+                copy.start()
+
+        @pl.when(gets)
+        def _():
+            for copy in copies:
+                copy.wait_recv()
+            for m in range(micro):
+                for h in range(heads):
+                    got = far[hop, m, rows_of(h), :].astype(F32)
+                    if hop:
+                        near = near_pass[hop, m, h : h + 1, :]
+                        got = out_ref[m, rows_of(h), :] + near * got
+                    out_ref[m, rows_of(h), :] = got
+                    if hop + 1 < len(widths):
+                        low[hop + 1, m, rows_of(h), :] = got.astype(BF)
+            if hop + 1 < len(widths):
+                passed = far_pass[hop]
+                near_pass[hop + 1] = passed * near_pass[hop] if hop else passed
+
+        @pl.when(jnp.logical_not(gets))
+        def _():
+            if hop == 0:
+                out_ref[...] = jnp.zeros_like(out_ref)
+            if hop + 1 < len(widths):
+                low[hop + 1] = out_ref[...].astype(BF)
+                near_pass[hop + 1] = jnp.zeros_like(pass_ref)
+
+        @pl.when(sends)
+        def _():
+            for copy in copies:
+                copy.wait_send()
+
+
+def chain(passing, state, way, collective_id):
+    count = lax.axis_size("seq")
+    widths, covered = [1], 1
+    while covered < count - 1:
+        widths.append(covered)
+        covered = 2 * covered
+    hops = len(widths)
+    lines = jnp.broadcast_to(passing[:, :, None], passing.shape + (STATE,))
+    vmem = pl.BlockSpec(memory_space=pltpu.VMEM)
+    return pl.pallas_call(
+        functools.partial(chain_kernel, way, widths),
+        out_shape=jax.ShapeDtypeStruct(state.shape, F32),
+        in_specs=[vmem, vmem],
+        out_specs=vmem,
+        scratch_shapes=[
+            pltpu.VMEM((hops,) + state.shape, BF),
+            pltpu.VMEM((hops,) + lines.shape, F32),
+            pltpu.VMEM((hops,) + state.shape, BF),
+            pltpu.VMEM((hops,) + lines.shape, F32),
+            pltpu.SemaphoreType.DMA((2, 2, hops)),
+        ],
+        compiler_params=pltpu.CompilerParams(
+            collective_id=collective_id, has_side_effects=True, vmem_limit_bytes=32 << 20
+        ),
+        cost_estimate=pl.CostEstimate(flops=0, bytes_accessed=100 << 20, transcendentals=0),
+    )(state, lines)
 
 
 RUN, STEP, SEG = 0, 2, 4
@@ -572,32 +684,6 @@
     return jnp.repeat(values, HEAD_DIM, axis=-1)
 
 
-def chain(passing, state, axis, way, beside=()):
-    count = lax.axis_size(axis)
-    heads = passing.shape[1]
-    beside = list(beside)
-    done = []
-
-    def pull(passing, state, steps):
-        pairs = [(i, i + way * steps) for i in range(count) if 0 <= i + way * steps < count]
-        far = lax.ppermute(state.astype(BF), axis, pairs)
-        rows = jnp.pad(passing[:, None], ((0, 0), (0, 7), (0, STATE - heads)))
-        passing = lax.ppermute(rows, axis, pairs)[:, 0, :heads]
-        if beside:
-            far, value = lax.optimization_barrier((far, beside.pop(0)))
-            done.append(value)
-        return passing, far.astype(F32)
-
-    passing, state = pull(passing, state, 1)
-    covered = 1
-    while covered < count - 1:
-        far_passing, far_state = pull(passing, state, covered)
-        state = spread(passing)[..., None] * far_state + state
-        passing = passing * far_passing
-        covered = 2 * covered
-    return state, done + beside
-
-
 def groups_of(seq_count, head_count):
     return [
         [s * head_count + h for s in range(g, g + MEMBERS) for h in range(head_count)]
@@ -772,7 +858,6 @@
         send = jnp.tile(expert_shard[:, own], (seq_count // MEMBERS, 1, 1))
         return lax.all_to_all(tied(send, *after), "seq", 0, 0, tiled=True).reshape(D, 3 * EFF)
 
-    experts = [fetch_expert(0, first_full)]
     hidden_wide = hidden_full.astype(F32)
     scale_mix = rms_scale(hidden_wide)
     normed = (hidden_wide * scale_mix * gains[0]).astype(BF)
@@ -838,9 +923,9 @@
         axis=3,
     )
     rows = cols.transpose(0, 1, 3, 2)
-    state_in, (local_out,) = chain(
-        passing, tied(local_state, experts[0]), "seq", 1, (scan_forward(signal, keys, cols, rows),)
-    )
+    state_in = chain(passing, local_state, 1, 8)
+    experts = [fetch_expert(0, state_in)]
+    local_out = scan_forward(signal, keys, cols, rows)
     grad_group = lax.all_gather(
         tied(grad_rows, state_in), ("seq", "head"), axis=1, tiled=True, axis_index_groups=groups
     ).reshape(micro, MEMBERS, tokens, D)
@@ -880,27 +965,9 @@
     def flat(a):
         return a.reshape(-1, a.shape[-1])
 
-    moe_own = lax.dynamic_index_in_dim(moe_group, member, 1, False)
-    grad_own = lax.dynamic_index_in_dim(grad_group, member, 1, False)
-    shared_both = mm(moe_own, shared_flat, ((2,), (0,)))
-    shared_gate, shared_linear = shared_both[..., :shared_local], shared_both[..., shared_local:]
-    shared_act = (jax.nn.silu(shared_gate) * shared_linear).astype(BF)
-    shared_out = mm(shared_act, shared_down_t, ((2,), (1,)))
-    shared_grad_act = mm(grad_own, shared_down_t, ((2,), (0,)))
-    shared_grad = jnp.concatenate(
-        [
-            shared_grad_act * shared_linear * squash_slope(shared_gate),
-            shared_grad_act * jax.nn.silu(shared_gate),
-        ],
-        axis=-1,
-    ).astype(BF)
-    shared_back = mm(shared_grad, shared_flat, ((2,), (1,)))
-    grad_shared_up = mm(moe_own, shared_grad, ((0, 1), (0, 1)), BF)
-    grad_shared_down_t = mm(grad_own, shared_act, ((0, 1), (0, 1)), BF)
-
     expert_backs, slot_parts = [], []
     for own in range(own_experts):
-        weights = tied(experts[own], *((expert_grads[-1], shared_out) if own else ()))
+        weights = tied(experts[own], *((expert_grads[-1],) if own else (moe_group,)))
         chosen = (expert_ids == first_own + own).astype(F32)
         named = jnp.sum(named_group * chosen, axis=-1)
         weight = jnp.sum(weight_group * chosen, axis=-1)
@@ -937,6 +1004,24 @@
             )
         )
 
+    moe_own = lax.dynamic_index_in_dim(tied(moe_group, back_parts[-1]), member, 1, False)
+    grad_own = lax.dynamic_index_in_dim(grad_group, member, 1, False)
+    shared_both = mm(moe_own, shared_flat, ((2,), (0,)))
+    shared_gate, shared_linear = shared_both[..., :shared_local], shared_both[..., shared_local:]
+    shared_act = (jax.nn.silu(shared_gate) * shared_linear).astype(BF)
+    shared_out = mm(shared_act, shared_down_t, ((2,), (1,)))
+    shared_grad_act = mm(grad_own, shared_down_t, ((2,), (0,)))
+    shared_grad = jnp.concatenate(
+        [
+            shared_grad_act * shared_linear * squash_slope(shared_gate),
+            shared_grad_act * jax.nn.silu(shared_gate),
+        ],
+        axis=-1,
+    ).astype(BF)
+    shared_back = mm(shared_grad, shared_flat, ((2,), (1,)))
+    grad_shared_up = mm(moe_own, shared_grad, ((0, 1), (0, 1)), BF)
+    grad_shared_down_t = mm(grad_own, shared_act, ((0, 1), (0, 1)), BF)
+
     def group_partial(parts, own_part):
         total = lax.dot_general(
             jnp.concatenate(slot_parts, axis=2),
@@ -1011,10 +1096,8 @@
         [tied(ffn_partial, entry_grad), second_grads],
         5,
     )
-    grad_gate_in = mm(tied(grad_gate_low, entry_grad), proj_gate, ((2,), (1,)))
-    state_grad, (ffn_rows, grad_gate_in) = chain(
-        passing, entry_grad, "seq", -1, (ffn_rows, grad_gate_in)
-    )
+    grad_gate_in = mm(grad_gate_low, proj_gate, ((2,), (1,)))
+    state_grad = chain(passing, tied(entry_grad, ffn_rows), -1, 9)
     output = to_features((resid_mid + ffn_rows).astype(BF))
     expert_backs.append(return_expert(expert_grads[-1], state_grad))
     grad_signal, grad_keys, grad_cols, grad_rows_part = scan_backward(
@@ -1055,29 +1138,28 @@
     grad_conv_weight = jnp.stack(taps)
     grad_pre = grad_pre.astype(BF)
 
-    grad_first = (
-        grad_gate_in
-        + mm(grad_pre, conv_proj, ((2,), (1,)))
-        + mm(grad_step_low, step_full, ((2,), (1,)))
-    )
+    columns = first_full.shape[1]
+    grad_all = jnp.concatenate([grad_pre, grad_step_low], axis=2)
+    grad_all = jnp.pad(grad_all, ((0, 0), (0, 0), (0, columns - grad_all.shape[2])))
+    grad_first = grad_gate_in + mm(grad_all, first_full, ((2,), (1,)))
     grad_first_sums = lax.psum(jnp.sum(grad_first * gains[0] * hidden_wide, axis=2), "head")
-    grad_conv_proj = mm(normed, grad_pre, ((0, 1), (0, 1)), BF)
-    grad_step_proj = mm(normed, grad_step_low, ((0, 1), (0, 1)), BF)
-    first_grads = lane_padded(
-        jnp.concatenate([grad_conv_proj, grad_step_proj, grad_router.astype(BF)], axis=1)
-    ).reshape(1, seq_count, slice_rows, -1)
+    first_grads = mm(normed, grad_all, ((0, 1), (0, 1)), BF).reshape(
+        1, seq_count, slice_rows, columns
+    )
+    router_grads = lane_padded(grad_router.astype(BF)).reshape(1, seq_count, slice_rows, -1)
     wide = local_width % 128 == 0
     grad_first = grad_first.astype(BF)
     if not wide:
         grad_first = grad_first.reshape(micro, tokens, head_count, local_width)
         grad_first = grad_first.transpose(0, 2, 1, 3)
     first_grads = tied(first_grads, expert_backs[-1])
-    first_features, grad_first_w = cube_reduce(
+    first_features, grad_first_w, grad_router_w = cube_reduce(
         [
             head_job(tokens, local_width, -1, wide),
-            seq_job(slice_rows, first_grads.shape[3], -1),
+            seq_job(slice_rows, columns, -1),
+            seq_job(slice_rows, router_grads.shape[3], -1),
         ],
-        [grad_first, first_grads],
+        [grad_first, first_grads, router_grads],
         6,
     )
     resid_features = hidden.astype(F32)
@@ -1093,7 +1175,7 @@
     over_heads = jnp.concatenate(
         [
             grad_first_w[:, inner_local:channels],
-            grad_first_w[:, channels + heads_local : channels + heads_local + expert_total],
+            grad_router_w[0, :, :expert_total],
         ],
         axis=1,
     )

time: 1450 us -> 1310 us (0.903)
  waiting for transfers between devices: 238 us -> 59 us
  Pallas kernels: 526 us -> 654 us
  other arithmetic: 128 us -> 89.4 us
  starting transfers between devices: 105 us -> 66.6 us
    pallas_call x0 -> x2, Pallas kernels: none -> 123 us  [chain(): pl.pallas_call(functools.partial(chain_kernel, way, widths), out_shape=ja...]
    all_to_all x2, waiting for transfers between devices: 129 us -> 20.2 us  [fetch_expert(): lax.all_to_all(tied(send, *after), 'seq', 0, 0, tiled=True)]
    ppermute x14 -> x0, starting transfers between devices: 64.5 us -> none  [the longest x6 40.5 us: pull(): passing = lax.ppermute(rows, axis, pairs)[:, 0, :heads]]
    ppermute x14 -> x0, waiting for transfers between devices: 45.1 us -> none  [the longest x6 29.5 us: pull(): passing = lax.ppermute(rows, axis, pairs)[:, 0, :heads]]
    all_to_all x2, starting transfers between devices: 10.1 us -> 38.6 us  [fetch_expert(): lax.all_to_all(tied(send, *after), 'seq', 0, 0, tiled=True)]
    unnamed x327 -> x299, local copies, waits for them, and re-layouts: 38.5 us -> 54.4 us
    ppermute x1, waiting for transfers between devices: 15.4 us -> 0.01 us  [body(): edge = lax.ppermute(normed[:, tokens - EDGE:], 'seq', ahead)]
    dot_general x37 -> x35, matrix products: 190 us -> 184 us  [mm(): return lax.dot_general(a, b, (dims, ((), ())), preferred_element_type=out)]
  transfers between devices with their start and end apart: 25 -> 11, of which waited for: 12 -> 2; matrix products, arithmetic and copies ran while one was open for 28% -> 25% of each run, Pallas kernels for 20% -> 24%
where the time goes in v2:
time: 1310 us
  Pallas kernels  654 us (50%)
  matrix products  261 us (20%)
  local copies, waits for them, and re-layouts  149 us (11%)
  other arithmetic  89.4 us (7%)
  starting transfers between devices  66.6 us (5%)
  waiting for transfers between devices  59 us (5%)
  between operations  16.4 us (1%)
    pallas_call x4, Pallas kernels, cube_reduce(): pl.pallas_call(functools.partial(reduce_kernel, jobs), out_shape=tuple(ou...  262 us
    pallas_call x4, Pallas kernels, cube_gather(): pl.pallas_call(functools.partial(gather_kernel, jobs), out_shape=tuple((j...  188 us
    dot_general x35, matrix products, mm(): return lax.dot_general(a, b, (dims, ((), ())), preferred_element_type=out)  184 us
    pallas_call x2, Pallas kernels, chain(): pl.pallas_call(functools.partial(chain_kernel, way, widths), out_shape=ja...  123 us
    pallas_call x1, Pallas kernels, scan_backward(): pl.pallas_call(backward_kernel, grid=(micro, pairs), out_shape=(jax.Shape...  60.6 us
    unnamed x299, local copies, waits for them, and re-layouts  54.4 us
    all_to_all x2, waiting for transfers between devices, return_expert(): return lax.all_to_all(tied(send, *after), 'seq', 0, 0, tiled=True)  38.8 us
    all_to_all x2, starting transfers between devices, fetch_expert(): lax.all_to_all(tied(send, *after), 'seq', 0, 0, tiled=True)  38.6 us
  transfers between devices with their start and end apart: 11, of which 2 were waited for; matrix products, arithmetic and copies ran while one was open for 25% of the time, Pallas kernels for 24%

profile of v2, /device:TPU:0, one launch (start us, length us, event | category | flops | bytes accessed | tf_op | source)
XLA Modules:
  0.0 1307.8 jit_solution(14347363730635163355)
XLA Ops:
  17.0 50.5 %shard_map.391 = (bf16[2,512,1536]{2,1,0:T(8,128)(2,1)S(1)}, bf16[2,512,1536]{2,1,0:T(8,128)(2,1)S(1)}, f32[1,8,1536]{2,1,0:T(8,128)S(1)}, bf16[1,8,192,1152]{3,2,1,0:T(8,128)(2,1)S(1)}, s32[2,4,8,512]{3,2,1,0:T(8,128)S(1)}) custom-call(bf16[2,512,384]{2,1,0:T(8,128)(2,1)S(1)} %copy-done.20, bf16[2,512,384]{2,1,0:T(8,128)(2,1)S(1)} %copy-done.28, ...), custom_call_target="tpu_custom_call" | custom-call | bytes 104857600 | tf_op jit(solution)/shard_map/pallas_call | solution.py:149
  112.1 9.9 fusion.37
  127.2 72.5 %shard_map.393.state_ref = f32[2,768,128]{2,1,0:T(8,128)S(1)} custom-call(f32[2,768,128]{2,1,0:T(8,128)S(1)} %fusion.71.state_ref, f32[2,12,128]{2,1,0:T(8,128)S(1)} %broadcast_in_dim.212.pass_ref), custom_call_target="tpu_custom_call" | custom-call | bytes 104857600 | tf_op jit(solution)/shard_map/pallas_call | solution.py:434
  207.5 34.0 %all-to-all-start = ((bf16[8,192,1536]{2,1,0:T(8,128)(2,1)}), bf16[8,192,1536]{2,1,0:T(8,128)(2,1)}, u32[]{:S(2)}, u32[]{:S(2)}) async-start(bf16[8,192,1536]{2,1,0:T(8,128)(2,1)} %bitcast.349), calls=%async_computation | async-start | bytes 9437184 | tf_op jit(solution)/shard_map/all_to_all | solution.py:859
  255.7 19.6 %shard_map.392 = f32[2,512,768]{2,1,0:T(8,128)S(1)} custom-call(f32[2,512,768]{2,1,0:T(8,128)S(1)} %slice.307.x_ref, f32[2,512,256]{2,1,0:T(8,128)S(1)} %slice.308.keys_ref, f32[2,6,512,8]{3,2,1,0:T(8,128)S(1)} %copy.394.cols_ref, f32[2,6,8,512]{3,2,1,0:T(8,128)S(1)} %bitcast.322), custom_call_target="tpu_custom_call" | custom-call | flops 1101004800 | bytes 9437184 | tf_op jit(solution)/shard_map/pallas_call | solution.py:542
  285.0 9.8 multiply_reduce_fusion.3
  308.4 21.8 %shard_map.394 = f32[2,128,1536]{2,1,0:T(8,128)S(1)} custom-call(bf16[2,4,128,1536]{3,2,1,0:T(8,128)(2,1)} %bitcast.363), custom_call_target="tpu_custom_call" | custom-call | bytes 104857600 | tf_op jit(solution)/shard_map/pallas_call | solution.py:281
  333.4 88.1 %shard_map.395 = bf16[2,16,128,1536]{3,2,1,0:T(8,128)(2,1)S(1)} custom-call(bf16[2,128,1536]{2,1,0:T(8,128)(2,1)S(1)} %multiply_convert_fusion.10.refs_0_), custom_call_target="tpu_custom_call" | custom-call | bytes 104857600 | tf_op jit(solution)/shard_map/pallas_call | solution.py:149
  433.1 8.3 fusion.153
  448.3 8.1 fusion.211
  456.5 9.0 fusion.56
  502.2 8.0 convolution_bitcast_fusion.1
  518.2 20.2 %all-to-all-done.1 = bf16[8,192,1536]{2,1,0:T(8,128)(2,1)} async-done(((bf16[8,192,1536]{2,1,0:T(8,128)(2,1)}), bf16[8,192,1536]{2,1,0:T(8,128)(2,1)}, u32[]{:S(2)}, u32[]{:S(2)}) %all-to-all-start.1) | async-done | bytes 4718624 | tf_op jit(solution)/shard_map/all_to_all | solution.py:859
  538.4 7.8 fusion.64
  577.5 8.6 multiply_convert_fusion.4
  587.2 8.8 fusion.62
  617.0 12.3 fusion.7
  634.8 8.6 fusion.54
  643.5 38.8 %all-to-all-done.2 = bf16[8,192,1536]{2,1,0:T(8,128)(2,1)} async-done(((bf16[8,192,1536]{2,1,0:T(8,128)(2,1)}), bf16[8,192,1536]{2,1,0:T(8,128)(2,1)}, u32[]{:S(2)}, u32[]{:S(2)}) %all-to-all-start.2) | async-done | bytes 4718624 | tf_op jit(solution)/shard_map/all_to_all | solution.py:855
  682.2 12.4 fusion.11
  701.3 54.0 %shard_map.396 = f32[2,128,1536]{2,1,0:T(8,128)S(1)} custom-call(bf16[2,16,128,1536]{3,2,1,0:T(8,128)(2,1)} %bitcast.355), custom_call_target="tpu_custom_call" | custom-call | bytes 104857600 | tf_op jit(solution)/shard_map/pallas_call | solution.py:281
  760.8 20.6 %shard_map.397 = (bf16[2,4,128,1536]{3,2,1,0:T(8,128)(2,1)S(1)}, f32[2,4,8,128]{3,2,1,0:T(8,128)S(1)}) custom-call(bf16[2,128,1536]{2,1,0:T(8,128)(2,1)S(1)} %get-tuple-element.261.refs_0_, f32[2,8,128]{2,1,0:T(8,128)S(1)} %broadcast_in_dim.219.refs_1_), custom_call_target="tpu_custom_call" | custom-call | bytes 104857600 | tf_op jit(solution)/shard_map/pallas_call | solution.py:149
  798.8 10.5 copy.421
  809.3 8.0 fusion.66.state_ref
  817.3 129.6 %shard_map.398 = (f32[2,128,1536]{2,1,0:T(8,128)S(1)}, f32[1,192,2304]{2,1,0:T(8,128)}) custom-call(bf16[2,16,128,1536]{3,2,1,0:T(8,128)(2,1)} %bitcast.356, bf16[1,8,192,2304]{3,2,1,0:T(8,128)(2,1)} %bitcast.347), custom_call_target="tpu_custom_call" | custom-call | bytes 104857600 | tf_op jit(solution)/shard_map/pallas_call | solution.py:281
  955.1 9.1 convolution_bitcast_fusion
  988.6 50.7 %shard_map.399.next_ref = f32[2,768,128]{2,1,0:T(8,128)S(1)} custom-call(f32[2,768,128]{2,1,0:T(8,128)S(1)} %copy-done.15, f32[2,12,128]{2,1,0:T(8,128)S(1)} %copy-done.31), custom_call_target="tpu_custom_call" | custom-call | bytes 104857600 | tf_op jit(solution)/shard_map/pallas_call | solution.py:434
  1056.2 60.6 %shard_map.400 = (f32[2,512,768]{2,1,0:T(8,128)S(1)}, f32[2,512,256]{2,1,0:T(8,128)S(1)}, f32[2,6,512,8]{3,2,1,0:T(8,128)S(1)}, f32[2,6,8,512]{3,2,1,0:T(8,128)S(1)}) custom-call(f32[2,512,768]{2,1,0:T(8,128)S(1)} %copy-done.4, f32[2,512,256]{2,1,0:T(8,128)S(1)} %copy-done.11, f32[2,6,512,8]{3,2,1,0:T(8,128)S(1)} %copy-done.2, ...), custom_call_target="tpu_custom_call" | custom-call | tf_op jit(solution)/shard_map/pallas_call | solution.py:649
  1157.1 8.8 fusion.18
  1171.5 7.6 fusion.148
  1202.6 57.0 %shard_map.401 = (f32[2,512,384]{2,1,0:T(8,128)}, f32[1,192,1152]{2,1,0:T(8,128)S(1)}, f32[1,192,128]{2,1,0:T(8,128)S(1)}) custom-call(bf16[2,512,1536]{2,1,0:T(8,128)(2,1)} %get-tuple-element.275.refs_0_, bf16[1,8,192,1152]{3,2,1,0:T(8,128)(2,1)} %bitcast.362, bf16[1,8,192,128]{3,2,1,0:T(8,128)(2,1)S(1)} %bitcast.328), custom_call_target="tpu_custom_call" | custom-call | bytes 104857600 | tf_op jit(solution)/shard_map/pallas_call | solution.py:281
  1263.0 29.1 %shard_map.402 = (f32[1,4,192,384]{3,2,1,0:T(8,128)S(1)}, f32[1,8,40,128]{3,2,1,0:T(8,128)S(1)}, f32[1,32,24,128]{3,2,1,0:T(8,128)S(1)}) custom-call(f32[1,192,384]{2,1,0:T(8,128)S(1)} %fusion.158.refs_0_, f32[1,40,128]{2,1,0:T(8,128)S(1)} %pad_bitcast_fusion.refs_1_, f32[1,24,128]{2,1,0:T(8,128)S(1)} %fusion.168.refs_2_), custom_call_target="tpu_custom_call" | custom-call | bytes 104857600 | tf_op jit(solution)/shard_map/pallas_call | solution.py:149
  (510 shorter events, 388.8 us)
Async XLA Ops:
  7.2 272.3 %all-gather.3.cloned.1.call-start = ((), (), s32[]{:S(2)}) async-start(), calls=%async_computation.7 | async-start | bytes 8404992 | tf_op jit(solution)/shard_map/all_gather | solution.py:846
  74.4 400.8 %all-gather.5.cloned.1.call-start = ((), (), s32[]{:S(2)}) async-start(), calls=%async_computation.8 | async-start | bytes 13369344 | tf_op jit(solution)/shard_map/all_gather | solution.py:929
  74.5 257.8 %copy-start.72 = (f32[1536]{0:T(1024)}, f32[1536]{0:T(1024)S(1)}, u32[]{:S(2)}) copy-start(f32[1536]{0:T(1024)S(1)} %get-tuple-element.245) | copy-start | bytes 18436
  76.7 34.1 %collective-permute-start = (bf16[2,8,1536]{2,1,0:T(8,128)(2,1)}, bf16[2,8,1536]{2,1,0:T(8,128)(2,1)}, u32[]{:S(2)}, u32[]{:S(2)}) collective-permute-start(bf16[2,8,1536]{2,1,0:T(8,128)(2,1)} %slice.293), channel_id=1, source_target_pairs={{0,4},{4,8},{8,12},{12,16},{16,20},{20,24},{24,28},{1,5},{5,9},{9,... | collective-permute-start | bytes 147464 | tf_op jit(solution)/shard_map/ppermute | solution.py:866
  122.0 79.3 %copy-start.55 = (bf16[8,192,1024]{2,1,0:T(8,128)(2,1)S(1)}, bf16[8,192,1024]{2,1,0:T(8,128)(2,1)}, u32[]{:S(2)}) copy-start(bf16[8,192,1024]{2,1,0:T(8,128)(2,1)} %param.44) | copy-start | bytes 9437188
  207.4 34.0 %copy-start.58 = (f32[2,512,12]{2,1,0:T(8,128)S(1)}, f32[2,512,12]{2,1,0:T(8,128)}, u32[]{:S(2)}) copy-start(f32[2,512,12]{2,1,0:T(8,128)} %copy-done.57) | copy-start | bytes 147460
  207.4 34.2 %copy-start.59 = (f32[2,512,12]{2,1,0:T(8,128)S(1)}, f32[2,512,12]{2,1,0:T(8,128)}, u32[]{:S(2)}) copy-start(f32[2,512,12]{2,1,0:T(8,128)} %get-tuple-element.290) | copy-start | bytes 147460
  207.5 34.4 %copy-start.62 = (f32[2,512,12]{2,1,0:T(8,128)S(1)}, f32[2,512,12]{2,1,0:T(8,128)}, u32[]{:S(2)}) copy-start(f32[2,512,12]{2,1,0:T(8,128)} %copy-done.61) | copy-start | bytes 147460
  207.5 34.4 %copy-start.71 = (u8[512,12]{1,0:T(8,128)(4,1)S(1)}, u8[512,12]{1,0:T(8,128)(4,1)}, u32[]{:S(2)}) copy-start(u8[512,12]{1,0:T(8,128)(4,1)} %copy-done.70) | copy-start | bytes 18436
  207.5 218.5 %all-to-all-start = ((bf16[8,192,1536]{2,1,0:T(8,128)(2,1)}), bf16[8,192,1536]{2,1,0:T(8,128)(2,1)}, u32[]{:S(2)}, u32[]{:S(2)}) async-start(bf16[8,192,1536]{2,1,0:T(8,128)(2,1)} %bitcast.349), calls=%async_computation | async-start | bytes 9437184 | tf_op jit(solution)/shard_map/all_to_all | solution.py:859
  250.2 34.7 %copy-start.93 = (f32[768]{0:T(1024)}, f32[768]{0:T(1024)S(1)}, u32[]{:S(2)}) copy-start(f32[768]{0:T(1024)S(1)} %mul.612) | copy-start | bytes 9220
  332.2 89.2 %copy-start.95 = (f32[2,128]{1,0:T(2,128)}, f32[2,128]{1,0:T(2,128)S(1)}, u32[]{:S(2)}) copy-start(f32[2,128]{1,0:T(2,128)S(1)} %get-tuple-element.262) | copy-start | bytes 3076
  332.2 89.2 %copy-start.91 = (f32[2,128]{1,0:T(2,128)}, f32[2,128]{1,0:T(2,128)S(1)}, u32[]{:S(2)}) copy-start(f32[2,128]{1,0:T(2,128)S(1)} %add_rsqrt_fusion.2) | copy-start | bytes 3076
  333.4 133.2 %copy-start.9 = (bf16[2,128,1536]{2,1,0:T(8,128)(2,1)}, bf16[2,128,1536]{2,1,0:T(8,128)(2,1)S(1)}, u32[]{:S(2)}) copy-start(bf16[2,128,1536]{2,1,0:T(8,128)(2,1)S(1)} %multiply_convert_fusion.10.refs_0_) | copy-start | bytes 2359300
  333.4 92.6 %copy-start.47 = (bf16[4,192,1536]{2,1,0:T(8,128)(2,1)S(1)}, bf16[4,192,1536]{2,1,0:T(8,128)(2,1)}, u32[]{:S(2)}) copy-start(bf16[4,192,1536]{2,1,0:T(8,128)(2,1)} %get-tuple-element.277) | copy-start | bytes 7077892
  428.5 109.9 %all-to-all-start.1 = ((bf16[8,192,1536]{2,1,0:T(8,128)(2,1)}), bf16[8,192,1536]{2,1,0:T(8,128)(2,1)}, u32[]{:S(2)}, u32[]{:S(2)}) async-start(bf16[8,192,1536]{2,1,0:T(8,128)(2,1)} %bitcast.350), calls=%async_computation.1 | async-start | bytes 9437184 | tf_op jit(solution)/shard_map/all_to_all | solution.py:859
  561.7 10.5 all-to-all-start.3
  572.2 110.0 %all-to-all-start.2 = ((bf16[8,192,1536]{2,1,0:T(8,128)(2,1)}), bf16[8,192,1536]{2,1,0:T(8,128)(2,1)}, u32[]{:S(2)}, u32[]{:S(2)}) async-start(bf16[8,192,1536]{2,1,0:T(8,128)(2,1)} %bitcast.351), calls=%async_computation.2 | async-start | bytes 9437184 | tf_op jit(solution)/shard_map/all_to_all | solution.py:855
  643.4 51.1 %copy-start.120 = (bf16[2,512,256]{1,2,0:T(8,128)(2,1)S(1)}, bf16[2,512,256]{1,2,0:T(8,128)(2,1)}, u32[]{:S(2)}) copy-start(bf16[2,512,256]{1,2,0:T(8,128)(2,1)} %copy-done.119) | copy-start | bytes 1572868
  701.3 54.0 %copy-start.35 = (f32[2,128,1536]{2,1,0:T(8,128)S(1)}, f32[2,128,1536]{2,1,0:T(8,128)}, u32[]{:S(2)}) copy-start(f32[2,128,1536]{2,1,0:T(8,128)} %copy-done.34) | copy-start | bytes 4718596
  701.3 54.0 %copy-start.73 = (f32[1536]{0:T(1024)S(1)}, f32[1536]{0:T(1024)}, u32[]{:S(2)}) copy-start(f32[1536]{0:T(1024)} %copy-done.72) | copy-start | bytes 18436
  701.3 54.1 %copy-start.92 = (f32[2,128]{1,0:T(2,128)S(1)}, f32[2,128]{1,0:T(2,128)}, u32[]{:S(2)}) copy-start(f32[2,128]{1,0:T(2,128)} %copy-done.91) | copy-start | bytes 3076
  757.8 23.7 %copy-start.105 = (f32[2,512]{1,0:T(2,128)S(1)}, f32[2,512]{1,0:T(2,128)}, u32[]{:S(2)}) copy-start(f32[2,512]{1,0:T(2,128)} %copy-done.104) | copy-start | bytes 12292
  817.3 129.6 %copy-start.36 = (f32[2,128,1536]{2,1,0:T(8,128)S(1)}, f32[2,128,1536]{2,1,0:T(8,128)}, u32[]{:S(2)}) copy-start(f32[2,128,1536]{2,1,0:T(8,128)} %copy-done.34) | copy-start | bytes 4718596
  951.0 16.9 %all-to-all-start.4 = ((bf16[2,1,128,1536]{2,0,1,3:T(2,128)(2,1)}), bf16[2,1,128,1536]{2,0,1,3:T(2,128)(2,1)}, u32[]{:S(2)}, u32[]{:S(2)}) async-start(bf16[2,1,128,1536]{2,0,1,3:T(2,128)(2,1)} %copy.422), calls=%async_computation.4 | async-start | bytes 1572864 | tf_op jit(solution)/shard_map/all_to_all | solution.py:715
  967.9 72.3 %all-to-all-start.6 = ((f32[2,1,128,1536]{2,0,1,3:T(2,128)}), f32[2,1,128,1536]{2,0,1,3:T(2,128)}, u32[]{:S(2)}, u32[]{:S(2)}) async-start(f32[2,1,128,1536]{2,0,1,3:T(2,128)} %copy.434), calls=%async_computation.6 | async-start | bytes 3145728 | tf_op jit(solution)/shard_map/all_to_all | solution.py:715
  1040.2 144.5 %all-to-all-start.5 = ((bf16[8,192,1536]{2,1,0:T(8,128)(2,1)}), bf16[8,192,1536]{2,1,0:T(8,128)(2,1)}, u32[]{:S(2)}, u32[]{:S(2)}) async-start(bf16[8,192,1536]{2,1,0:T(8,128)(2,1)} %bitcast.348), calls=%async_computation.5 | async-start | bytes 9437184 | tf_op jit(solution)/shard_map/all_to_all | solution.py:855
  1056.2 60.7 %copy-start.94 = (f32[768]{0:T(1024)S(1)}, f32[768]{0:T(1024)}, u32[]{:S(2)}) copy-start(f32[768]{0:T(1024)} %copy-done.93) | copy-start | bytes 9220
  1129.1 22.3 %collective-permute-start.1 = (f32[2,8,1024]{2,1,0:T(8,128)}, f32[2,8,1024]{2,1,0:T(8,128)}, u32[]{:S(2)}, u32[]{:S(2)}) collective-permute-start(f32[2,8,1024]{2,1,0:T(8,128)} %slice.325), channel_id=1, source_target_pairs={{4,0},{8,4},{12,8},{16,12},{20,16},{24,20},{28,24},{5,1},{9,5},{13... | collective-permute-start | bytes 196616 | tf_op jit(solution)/shard_map/ppermute | solution.py:1123
  1202.6 57.1 %copy-start.21 = (bf16[2,512,384]{2,1,0:T(8,128)(2,1)S(1)}, bf16[2,512,384]{2,1,0:T(8,128)(2,1)}, u32[]{:S(2)}) copy-start(bf16[2,512,384]{2,1,0:T(8,128)(2,1)} %refs_0_.1) | copy-start | bytes 2359300
  1202.6 57.1 %copy-start.83 = (f32[2,512]{1,0:T(2,128)S(1)}, f32[2,512]{1,0:T(2,128)}, u32[]{:S(2)}) copy-start(f32[2,512]{1,0:T(2,128)} %copy-done.82) | copy-start | bytes 12292
  1202.6 57.1 %copy-start.100 = (f32[384]{0:T(512)S(1)}, f32[384]{0:T(512)}, u32[]{:S(2)}) copy-start(f32[384]{0:T(512)} %param.29) | copy-start | bytes 4612
  (124 other events, 815.5 us)
Sparse Core Ops, SparseCore 0:
  74.5 131.9 all-gather.2
  208.1 199.9 all-gather.4

commit v3 on v2

--- a/solution.py
+++ b/solution.py
@@ -662,6 +662,105 @@
     )(x, keys, cols, rows, dy, state, later)
 
 
+TILE = 256
+
+
+def expert_kernel(first, capacity, lines_ref, cols_ref, rows_ref, grads_ref, weights_ref, *refs):
+    before, refs = ((), refs) if first else (refs[:2], refs[2:])
+    ffn_ref, back_ref, dots_ref, sums_ref, total, picked, given = refs
+    tokens, width = rows_ref.shape[1], rows_ref.shape[2]
+    block = pl.program_id(0)
+
+    @pl.when(block == 0)
+    def _():
+        total[...] = jnp.zeros_like(total)
+
+    slot = lax.broadcasted_iota(jnp.int32, (capacity, tokens), 0).astype(F32)
+    pick = slot == lines_ref[0, 0:1, :]
+    slots = jnp.where(pick, 1.0, 0.0).astype(BF)
+    slot = lax.broadcasted_iota(jnp.int32, (tokens, capacity), 1).astype(F32)
+    places = jnp.where(slot == cols_ref[0, :, 0:1], 1.0, 0.0).astype(BF)
+    share = jnp.sum(jnp.where(pick, lines_ref[0, 1:2, :], 0.0), axis=1, keepdims=True)
+    tiles = [slice(i, i + TILE) for i in range(0, width, TILE)]
+    for tile in tiles:
+        picked[:, tile] = dot(slots, rows_ref[0, :, tile], NN).astype(BF)
+        given[:, tile] = dot(slots, grads_ref[0, :, tile], NN).astype(BF)
+    both = dot(picked[...], weights_ref[:, : 2 * EFF], NN)
+    gate, linear = both[:, :EFF], both[:, EFF:]
+    logistic = jax.nn.sigmoid(gate)
+    silu = gate * logistic
+    act = (silu * linear).astype(BF)
+    act_grad, made_dot = 0.0, 0.0
+    for tile in tiles:
+        down = weights_ref[tile, 2 * EFF :]
+        made = dot(act, down, NT)
+        grad = given[:, tile].astype(F32)
+        made_dot = made_dot + jnp.sum(grad * made, axis=1, keepdims=True)
+        out = dot(places, made * share, NN)
+        if not first:
+            out = out + before[0][0, :, tile].astype(F32)
+        ffn_ref[0, :, tile] = out.astype(BF)
+        grad = (grad * share).astype(BF)
+        act_grad = act_grad + dot(grad, down, NN)
+        total[tile, 2 * EFF :] += dot(grad, act, TN)
+    dots = jnp.sum(jnp.where(pick, made_dot, 0.0), axis=0, keepdims=True)
+    dots_ref[0] = jnp.broadcast_to(dots, dots_ref.shape[1:])
+    both_grad = jnp.concatenate(
+        [act_grad * linear * (logistic * (1.0 + gate * (1.0 - logistic))), act_grad * silu], axis=1
+    ).astype(BF)
+    for tile in tiles:
+        back = dot(both_grad, weights_ref[tile, : 2 * EFF], NT)
+        out = dot(places, back, NN)
+        if not first:
+            out = out + before[1][0, :, tile].astype(F32)
+        back_ref[0, :, tile] = out.astype(BF)
+        total[tile, : 2 * EFF] += dot(picked[:, tile], both_grad, TN)
+
+    @pl.when(block == pl.num_programs(0) - 1)
+    def _():
+        for tile in tiles:
+            sums_ref[tile, :] = total[tile, :].astype(BF)
+
+
+def run_expert(capacity, lines, rows, grads, weights, before):
+    blocks, tokens, width = rows.shape
+    line = pl.BlockSpec((1, 8, tokens), lambda b: (b, 0, 0))
+    wide = pl.BlockSpec((1, tokens, width), lambda b: (b, 0, 0))
+    once = pl.Buffered(1)
+    matrix = pl.BlockSpec(weights.shape, lambda b: (0, 0), pipeline_mode=once)
+    whole = jax.ShapeDtypeStruct(rows.shape, BF)
+    return pl.pallas_call(
+        functools.partial(expert_kernel, not before, capacity),
+        grid=(blocks,),
+        out_shape=(
+            whole,
+            whole,
+            jax.ShapeDtypeStruct(lines.shape, F32),
+            jax.ShapeDtypeStruct(weights.shape, BF),
+        ),
+        in_specs=[
+            line,
+            pl.BlockSpec((1, tokens, 8), lambda b: (b, 0, 0)),
+            wide,
+            wide,
+            matrix,
+            *([wide] * len(before)),
+        ],
+        out_specs=(wide, wide, line, pl.BlockSpec(weights.shape, lambda b: (0, 0))),
+        scratch_shapes=[
+            pltpu.VMEM(weights.shape, F32),
+            pltpu.VMEM((capacity, width), BF),
+            pltpu.VMEM((capacity, width), BF),
+        ],
+        compiler_params=pltpu.CompilerParams(vmem_limit_bytes=58 << 20),
+        cost_estimate=pl.CostEstimate(
+            flops=blocks * capacity * width * (18 * EFF + 8 * tokens),
+            bytes_accessed=blocks * tokens * width * 12,
+            transcendentals=0,
+        ),
+    )(lines, lines.transpose(0, 2, 1), rows, grads, weights, *before)
+
+
 def mm(a, b, dims, out=F32):
     return lax.dot_general(a, b, (dims, ((), ())), preferred_element_type=out)
 
@@ -957,83 +1056,57 @@
 
     named_group, weight_group = dense_weights(route_group[:, :, :TOPK], moe_group)
     first_own = head_rank * experts_local + member * own_experts
-    slot_index = jnp.arange(capacity, dtype=jnp.int32)
-    ffn_parts, back_parts, expert_grads, weight_grads = [], [], [], []
-    block = (((3,), (2,)), ((0, 1), (0, 1)))
-    block_t = (((2,), (2,)), ((0, 1), (0, 1)))
-
-    def flat(a):
-        return a.reshape(-1, a.shape[-1])
-
-    expert_backs, slot_parts = [], []
+    def shared_expert(after):
+        moe_own = lax.dynamic_index_in_dim(tied(moe_group, after), member, 1, False)
+        grad_own = lax.dynamic_index_in_dim(grad_group, member, 1, False)
+        shared_both = mm(moe_own, shared_flat, ((2,), (0,)))
+        shared_gate, shared_linear = shared_both[..., :shared_local], shared_both[..., shared_local:]
+        shared_act = (jax.nn.silu(shared_gate) * shared_linear).astype(BF)
+        shared_out = mm(shared_act, shared_down_t, ((2,), (1,)))
+        shared_grad_act = mm(grad_own, shared_down_t, ((2,), (0,)))
+        shared_grad = jnp.concatenate(
+            [
+                shared_grad_act * shared_linear * squash_slope(shared_gate),
+                shared_grad_act * jax.nn.silu(shared_gate),
+            ],
+            axis=-1,
+        ).astype(BF)
+        shared_back = mm(shared_grad, shared_flat, ((2,), (1,)))
+        grad_shared_up = mm(moe_own, shared_grad, ((0, 1), (0, 1)), BF)
+        grad_shared_down_t = mm(grad_own, shared_act, ((0, 1), (0, 1)), BF)
+        return shared_out, shared_back, grad_shared_up, grad_shared_down_t
+
+    blocks = micro * MEMBERS
+    sums, expert_grads, weight_grads, expert_backs = (), [], [], []
     for own in range(own_experts):
-        weights = tied(experts[own], *((expert_grads[-1],) if own else (moe_group,)))
         chosen = (expert_ids == first_own + own).astype(F32)
         named = jnp.sum(named_group * chosen, axis=-1)
         weight = jnp.sum(weight_group * chosen, axis=-1)
-        rank = mm(named.astype(BF), until.astype(BF), ((2,), (0,))).astype(jnp.int32) - 1
-        pick = (rank[:, :, None, :] == slot_index[:, None]) & (named[:, :, None, :] > 0.0)
-        slots = pick.astype(BF)
-        slot_weight = jnp.sum(pick * weight[:, :, None, :], axis=-1, keepdims=True)
-        slot_rows = lax.dot_general(slots, moe_group, block, preferred_element_type=BF)
-        slot_grads = lax.dot_general(slots, grad_group, block, preferred_element_type=BF)
-        up_own, down_t = weights[:, : 2 * EFF], weights[:, 2 * EFF :]
-        both = mm(slot_rows, up_own, ((3,), (0,)))
-        up_gate, up_linear = both[..., :EFF], both[..., EFF:]
-        hidden_act = (jax.nn.silu(up_gate) * up_linear).astype(BF)
-        made = mm(hidden_act, down_t, ((3,), (1,)))
-        slot_dot = jnp.sum(slot_grads.astype(F32) * made, axis=-1, keepdims=True)
-        weight_grads.append(jnp.sum(pick * slot_dot, axis=2))
-        made_low = (made * slot_weight).astype(BF)
-        slot_parts.append(slots)
-        ffn_parts.append(made_low)
-        grads_low = (slot_grads * slot_weight).astype(BF)
-        act_grad = mm(grads_low, down_t, ((3,), (0,)))
-        both_grad = jnp.concatenate(
-            [act_grad * up_linear * squash_slope(up_gate), act_grad * jax.nn.silu(up_gate)], axis=-1
-        ).astype(BF)
-        back = mm(both_grad, up_own, ((3,), (1,)), BF)
-        back_parts.append(back)
-        expert_grads.append(
-            jnp.concatenate(
-                [
-                    mm(flat(slot_rows), flat(both_grad), ((0,), (0,)), BF),
-                    mm(flat(grads_low), flat(hidden_act), ((0,), (0,)), BF),
-                ],
-                axis=1,
-            )
+        rank = mm(named.astype(BF), until.astype(BF), ((2,), (0,))) - 1.0
+        lines = jnp.stack([jnp.where(named > 0.0, rank, -1.0), weight], axis=2)
+        lines = jnp.pad(lines, ((0, 0), (0, 0), (0, 6), (0, 0))).reshape(blocks, 8, tokens)
+        *sums, dots, grads = run_expert(
+            capacity,
+            lines,
+            moe_group.reshape(blocks, tokens, D),
+            grad_group.reshape(blocks, tokens, D),
+            tied(experts[own], *((shared[1], expert_grads[-1]) if own else (moe_group,))),
+            tuple(sums),
         )
-
-    moe_own = lax.dynamic_index_in_dim(tied(moe_group, back_parts[-1]), member, 1, False)
-    grad_own = lax.dynamic_index_in_dim(grad_group, member, 1, False)
-    shared_both = mm(moe_own, shared_flat, ((2,), (0,)))
-    shared_gate, shared_linear = shared_both[..., :shared_local], shared_both[..., shared_local:]
-    shared_act = (jax.nn.silu(shared_gate) * shared_linear).astype(BF)
-    shared_out = mm(shared_act, shared_down_t, ((2,), (1,)))
-    shared_grad_act = mm(grad_own, shared_down_t, ((2,), (0,)))
-    shared_grad = jnp.concatenate(
-        [
-            shared_grad_act * shared_linear * squash_slope(shared_gate),
-            shared_grad_act * jax.nn.silu(shared_gate),
-        ],
-        axis=-1,
-    ).astype(BF)
-    shared_back = mm(shared_grad, shared_flat, ((2,), (1,)))
-    grad_shared_up = mm(moe_own, shared_grad, ((0, 1), (0, 1)), BF)
-    grad_shared_down_t = mm(grad_own, shared_act, ((0, 1), (0, 1)), BF)
-
-    def group_partial(parts, own_part):
-        total = lax.dot_general(
-            jnp.concatenate(slot_parts, axis=2),
-            jnp.concatenate(parts, axis=2),
-            block_t,
-            preferred_element_type=BF,
-        )
+        weight_grads.append(dots[:, 0].reshape(micro, MEMBERS, tokens))
+        expert_grads.append(grads)
+        if own == 0:
+            shared = shared_expert(sums[1])
+    shared_out, shared_back, grad_shared_up, grad_shared_down_t = shared
+    ffn_sum, back_sum = [s.reshape(micro, MEMBERS, tokens, D) for s in sums]
+
+    def group_partial(total, own_part):
         mine = lax.dynamic_slice_in_dim(total, member, 1, 1).astype(F32) + own_part[:, None]
         return lax.dynamic_update_slice_in_dim(total, mine.astype(BF), member, 1)
 
+    expert_backs = [return_expert(grads) for grads in expert_grads[:-1]]
     weight_grad = lax.all_to_all(
-        jnp.stack(weight_grads, axis=-1)
+        tied(jnp.stack(weight_grads, axis=-1), *expert_backs)
         .reshape(micro, MEMBERS * head_count, row_count, own_experts)
         .transpose(1, 0, 2, 3),
         ("seq", "head"),
@@ -1047,11 +1120,9 @@
         .transpose(2, 3, 1, 0, 4)
         .reshape(micro, row_count, expert_total)
     )
-    expert_backs = [return_expert(grads) for grads in expert_grads[:-1]]
-    back_parts[-1] = tied(back_parts[-1], *expert_backs)
-    back_partial = group_partial(back_parts, shared_back)
+    back_partial = group_partial(back_sum, shared_back)
     back_rows = reduce_group(back_partial, 3)
-    ffn_partial = group_partial(ffn_parts, shared_out)
+    ffn_partial = group_partial(ffn_sum, shared_out)
     route_rows = own_rows(routes).transpose(0, 2, 1)
     named_rows, weight_rows = dense_weights(route_rows, moe_rows)
     weight_grad = jnp.where(named_rows, weight_grad, 0.0)

time: 1310 us -> 1260 us (0.962)
  Pallas kernels: 654 us -> 799 us
  matrix products: 261 us -> 127 us
  waiting for transfers between devices: 59 us -> 32.9 us
  local copies, waits for them, and re-layouts: 149 us -> 128 us
  other arithmetic: 89.4 us -> 70.5 us
    pallas_call x0 -> x2, Pallas kernels: none -> 137 us  [run_expert(): pl.pallas_call(functools.partial(expert_kernel, not before, capacity), gr...]
    dot_general x35 -> x23, matrix products: 184 us -> 99.9 us  [mm(): return lax.dot_general(a, b, (dims, ((), ())), preferred_element_type=out)]
    dot_general x6 -> x0, matrix products: 50.8 us -> none  [the longest x2 24.6 us: group_partial(): lax.dot_general(jnp.concatenate(slot_parts, axis=2), jnp.concatenate(part...]
    all_to_all x2, waiting for transfers between devices: 38.8 us -> 0.01 us  [return_expert(): return lax.all_to_all(tied(send, *after), 'seq', 0, 0, tiled=True)]
    unnamed x299 -> x251, local copies, waits for them, and re-layouts: 54.4 us -> 38.3 us
    concatenate x2 -> x0, local copies, waits for them, and re-layouts: 13.3 us -> none  [body(): jnp.concatenate([mm(flat(slot_rows), flat(both_grad), ((0,), (0,)), BF),...]
  transfers between devices with their start and end apart: 11 -> 11, of which waited for: 2 -> 2; matrix products, arithmetic and copies ran while one was open for 25% -> 17% of each run, Pallas kernels for 24% -> 41%
where the time goes in v3:
time: 1260 us; the launch traced here: 1250 us
  Pallas kernels  799 us (63%)
  local copies, waits for them, and re-layouts  128 us (10%)
  matrix products  127 us (10%)
  other arithmetic  70.5 us (6%)
  starting transfers between devices  67.6 us (5%)
  waiting for transfers between devices  32.9 us (3%)
  between operations  16.2 us (1%)
  blocking collectives  13.2 us (1%)
    pallas_call x4, Pallas kernels, cube_reduce(): pl.pallas_call(functools.partial(reduce_kernel, jobs), out_shape=tuple(ou...  265 us
    pallas_call x4, Pallas kernels, cube_gather(): pl.pallas_call(functools.partial(gather_kernel, jobs), out_shape=tuple((j...  192 us
    pallas_call x2, Pallas kernels, run_expert(): pl.pallas_call(functools.partial(expert_kernel, not before, capacity), gr...  137 us
    pallas_call x2, Pallas kernels, chain(): pl.pallas_call(functools.partial(chain_kernel, way, widths), out_shape=ja...  124 us
    dot_general x23, matrix products, mm(): return lax.dot_general(a, b, (dims, ((), ())), preferred_element_type=out)  99.9 us
    pallas_call x1, Pallas kernels, scan_backward(): pl.pallas_call(backward_kernel, grid=(micro, pairs), out_shape=(jax.Shape...  61 us
    unnamed x251, local copies, waits for them, and re-layouts  38.3 us
    all_to_all x2, starting transfers between devices, fetch_expert(): lax.all_to_all(tied(send, *after), 'seq', 0, 0, tiled=True)  38.3 us
  transfers between devices with their start and end apart: 11, of which 2 were waited for; matrix products, arithmetic and copies ran while one was open for 17% of the time, Pallas kernels for 41%

profile of v3, /device:TPU:0, one launch (start us, length us, event | category | flops | bytes accessed | tf_op | source)
XLA Modules:
  0.0 1254.3 jit_solution(14895018690403867689)
XLA Ops:
  17.0 50.5 %shard_map.391 = (bf16[2,512,1536]{2,1,0:T(8,128)(2,1)S(1)}, bf16[2,512,1536]{2,1,0:T(8,128)(2,1)S(1)}, f32[1,8,1536]{2,1,0:T(8,128)S(1)}, bf16[1,8,192,1152]{3,2,1,0:T(8,128)(2,1)S(1)}, s32[2,4,8,512]{3,2,1,0:T(8,128)S(1)}) custom-call(bf16[2,512,384]{2,1,0:T(8,128)(2,1)S(1)} %copy-done.19, bf16[2,512,384]{2,1,0:T(8,128)(2,1)S(1)} %copy-done.29, ...), custom_call_target="tpu_custom_call" | custom-call | bytes 104857600 | tf_op jit(solution)/shard_map/pallas_call | solution.py:149
  94.2 6.9 fusion.55
  112.2 9.9 fusion.25
  127.3 72.9 %shard_map.393.state_ref = f32[2,768,128]{2,1,0:T(8,128)S(1)} custom-call(f32[2,768,128]{2,1,0:T(8,128)S(1)} %fusion.41.state_ref, f32[2,12,128]{2,1,0:T(8,128)S(1)} %broadcast_in_dim.205.pass_ref), custom_call_target="tpu_custom_call" | custom-call | bytes 104857600 | tf_op jit(solution)/shard_map/pallas_call | solution.py:434
  207.8 33.6 %all-to-all-start.1 = ((bf16[8,192,1536]{2,1,0:T(8,128)(2,1)}), bf16[8,192,1536]{2,1,0:T(8,128)(2,1)}, u32[]{:S(2)}, u32[]{:S(2)}) async-start(bf16[8,192,1536]{2,1,0:T(8,128)(2,1)} %bitcast.308), calls=%async_computation.1 | async-start | bytes 9437184 | tf_op jit(solution)/shard_map/all_to_all | solution.py:958
  253.4 19.6 %shard_map.392 = f32[2,512,768]{2,1,0:T(8,128)S(1)} custom-call(f32[2,512,768]{2,1,0:T(8,128)S(1)} %slice.283.x_ref, f32[2,512,256]{2,1,0:T(8,128)S(1)} %slice.284.keys_ref, f32[2,6,512,8]{3,2,1,0:T(8,128)S(1)} %copy.352.cols_ref, f32[2,6,8,512]{3,2,1,0:T(8,128)S(1)} %bitcast.291), custom_call_target="tpu_custom_call" | custom-call | flops 1101004800 | bytes 9437184 | tf_op jit(solution)/shard_map/pallas_call | solution.py:542
  282.7 9.9 multiply_reduce_fusion.3
  292.6 6.7 psum.14
  299.3 6.9 fusion.61
  306.3 21.8 %shard_map.394 = f32[2,128,1536]{2,1,0:T(8,128)S(1)} custom-call(bf16[2,4,128,1536]{3,2,1,0:T(8,128)(2,1)} %bitcast.322), custom_call_target="tpu_custom_call" | custom-call | bytes 104857600 | tf_op jit(solution)/shard_map/pallas_call | solution.py:281
  330.9 90.5 %shard_map.395 = bf16[2,16,128,1536]{3,2,1,0:T(8,128)(2,1)S(1)} custom-call(bf16[2,128,1536]{2,1,0:T(8,128)(2,1)S(1)} %multiply_convert_fusion.2.refs_0_), custom_call_target="tpu_custom_call" | custom-call | bytes 104857600 | tf_op jit(solution)/shard_map/pallas_call | solution.py:149
  434.0 8.3 fusion.106
  445.7 68.0 %shard_map.396 = (bf16[8,512,1536]{2,1,0:T(8,128)(2,1)}, bf16[8,512,1536]{2,1,0:T(8,128)(2,1)}, f32[8,8,512]{2,1,0:T(8,128)}, bf16[1536,1536]{1,0:T(8,128)(2,1)}) custom-call(f32[8,8,512]{2,1,0:T(8,128)} %bitcast.340, f32[8,512,8]{2,1,0:T(8,128)} %bitcast.324, bf16[8,512,1536]{2,1,0:T(8,128)(2,1)} %bitcast.287, bf16[8,512,1536]{2,1,0:T(8,128)(2,1)} %bitcast.372, ...), custom_call_target="tpu_custom_call" | custom-call | flops 31406948352 | bytes 75497472 | tf_op jit(solution)/shard_map/pallas_call | solution.py:732
  513.8 24.8 %all-to-all-done = bf16[8,192,1536]{2,1,0:T(8,128)(2,1)} async-done(((bf16[8,192,1536]{2,1,0:T(8,128)(2,1)}), bf16[8,192,1536]{2,1,0:T(8,128)(2,1)}, u32[]{:S(2)}, u32[]{:S(2)}) %all-to-all-start) | async-done | bytes 4718624 | tf_op jit(solution)/shard_map/all_to_all | solution.py:958
  557.2 6.8 fusion.70
  564.0 69.2 %shard_map.397 = (bf16[8,512,1536]{2,1,0:T(8,128)(2,1)}, bf16[8,512,1536]{2,1,0:T(8,128)(2,1)}, f32[8,8,512]{2,1,0:T(8,128)}, bf16[1536,1536]{1,0:T(8,128)(2,1)}) custom-call(f32[8,8,512]{2,1,0:T(8,128)} %bitcast.339, f32[8,512,8]{2,1,0:T(8,128)} %bitcast.323, bf16[8,512,1536]{2,1,0:T(8,128)(2,1)} %bitcast.289, bf16[8,512,1536]{2,1,0:T(8,128)(2,1)} %bitcast.374, ...), custom_call_target="tpu_custom_call" | custom-call | flops 31406948352 | bytes 75497472 | tf_op jit(solution)/shard_map/pallas_call | solution.py:732
  661.4 55.6 %shard_map.398 = f32[2,128,1536]{2,1,0:T(8,128)S(1)} custom-call(bf16[2,16,128,1536]{3,2,1,0:T(8,128)(2,1)} %bitcast.65.refs_0_), custom_call_target="tpu_custom_call" | custom-call | bytes 104857600 | tf_op jit(solution)/shard_map/pallas_call | solution.py:281
  723.0 20.7 %shard_map.399 = (bf16[2,4,128,1536]{3,2,1,0:T(8,128)(2,1)S(1)}, f32[2,4,8,128]{3,2,1,0:T(8,128)S(1)}) custom-call(bf16[2,128,1536]{2,1,0:T(8,128)(2,1)S(1)} %get-tuple-element.252.refs_0_, f32[2,8,128]{2,1,0:T(8,128)S(1)} %broadcast_in_dim.212.refs_1_), custom_call_target="tpu_custom_call" | custom-call | bytes 104857600 | tf_op jit(solution)/shard_map/pallas_call | solution.py:149
  747.8 6.6 multiply_reduce_fusion.1
  761.0 10.6 copy.384
  771.5 7.9 fusion.38.state_ref
  779.5 129.5 %shard_map.400 = (f32[2,128,1536]{2,1,0:T(8,128)S(1)}, f32[1,192,2304]{2,1,0:T(8,128)}) custom-call(bf16[2,16,128,1536]{3,2,1,0:T(8,128)(2,1)} %bitcast.61.refs_0_, bf16[1,8,192,2304]{3,2,1,0:T(8,128)(2,1)} %bitcast.306), custom_call_target="tpu_custom_call" | custom-call | bytes 104857600 | tf_op jit(solution)/shard_map/pallas_call | solution.py:281
  920.9 8.1 all-to-all-done.4
  934.5 51.3 %shard_map.401.next_ref = f32[2,768,128]{2,1,0:T(8,128)S(1)} custom-call(f32[2,768,128]{2,1,0:T(8,128)S(1)} %copy-done.16, f32[2,12,128]{2,1,0:T(8,128)S(1)} %copy-done.32), custom_call_target="tpu_custom_call" | custom-call | bytes 104857600 | tf_op jit(solution)/shard_map/pallas_call | solution.py:434
  997.6 61.0 %shard_map.402 = (f32[2,512,768]{2,1,0:T(8,128)S(1)}, f32[2,512,256]{2,1,0:T(8,128)S(1)}, f32[2,6,512,8]{3,2,1,0:T(8,128)S(1)}, f32[2,6,8,512]{3,2,1,0:T(8,128)S(1)}) custom-call(f32[2,512,768]{2,1,0:T(8,128)S(1)} %copy-done.4, f32[2,512,256]{2,1,0:T(8,128)S(1)} %copy-done.10, f32[2,6,512,8]{3,2,1,0:T(8,128)S(1)} %copy-done.2, ...), custom_call_target="tpu_custom_call" | custom-call | tf_op jit(solution)/shard_map/pallas_call | solution.py:649
  1068.8 6.3 select_reduce_fusion.2
  1090.2 6.3 fusion.58
  1102.2 9.4 fusion.6
  1111.6 6.5 psum.15
  1119.4 7.5 fusion.101
  1147.0 57.7 %shard_map.403 = (f32[2,512,384]{2,1,0:T(8,128)}, f32[1,192,1152]{2,1,0:T(8,128)S(1)}, f32[1,192,128]{2,1,0:T(8,128)S(1)}) custom-call(bf16[2,512,1536]{2,1,0:T(8,128)(2,1)} %get-tuple-element.262.refs_0_, bf16[1,8,192,1152]{3,2,1,0:T(8,128)(2,1)} %bitcast.321, bf16[1,8,192,128]{3,2,1,0:T(8,128)(2,1)S(1)} %bitcast.297), custom_call_target="tpu_custom_call" | custom-call | bytes 104857600 | tf_op jit(solution)/shard_map/pallas_call | solution.py:281
  1208.2 30.3 %shard_map.404 = (f32[1,4,192,384]{3,2,1,0:T(8,128)S(1)}, f32[1,8,40,128]{3,2,1,0:T(8,128)S(1)}, f32[1,32,24,128]{3,2,1,0:T(8,128)S(1)}) custom-call(f32[1,192,384]{2,1,0:T(8,128)S(1)} %fusion.111.refs_0_, f32[1,40,128]{2,1,0:T(8,128)S(1)} %pad_bitcast_fusion.refs_1_, f32[1,24,128]{2,1,0:T(8,128)S(1)} %fusion.121.refs_2_), custom_call_target="tpu_custom_call" | custom-call | bytes 104857600 | tf_op jit(solution)/shard_map/pallas_call | solution.py:149
  (440 shorter events, 256.5 us)
Async XLA Ops:
  7.2 270.1 %all-gather.3.cloned.1.call-start = ((), (), s32[]{:S(2)}) async-start(), calls=%async_computation.7 | async-start | bytes 8404992 | tf_op jit(solution)/shard_map/all_gather | solution.py:945
  74.3 371.5 %all-gather.5.cloned.1.call-start = ((), (), s32[]{:S(2)}) async-start(), calls=%async_computation.8 | async-start | bytes 13369344 | tf_op jit(solution)/shard_map/all_gather | solution.py:1028
  74.4 255.2 %copy-start.64 = (f32[1536]{0:T(1024)}, f32[1536]{0:T(1024)S(1)}, u32[]{:S(2)}) copy-start(f32[1536]{0:T(1024)S(1)} %get-tuple-element.240) | copy-start | bytes 18436
  76.6 34.2 %collective-permute-start = (bf16[2,8,1536]{2,1,0:T(8,128)(2,1)}, bf16[2,8,1536]{2,1,0:T(8,128)(2,1)}, u32[]{:S(2)}, u32[]{:S(2)}) collective-permute-start(bf16[2,8,1536]{2,1,0:T(8,128)(2,1)} %slice.269), channel_id=1, source_target_pairs={{0,4},{4,8},{8,12},{12,16},{16,20},{20,24},{24,28},{1,5},{5,9},{9,... | collective-permute-start | bytes 147464 | tf_op jit(solution)/shard_map/ppermute | solution.py:965
  122.1 79.6 %copy-start.50 = (bf16[8,192,1024]{2,1,0:T(8,128)(2,1)S(1)}, bf16[8,192,1024]{2,1,0:T(8,128)(2,1)}, u32[]{:S(2)}) copy-start(bf16[8,192,1024]{2,1,0:T(8,128)(2,1)} %param.44) | copy-start | bytes 9437188
  207.8 33.6 %copy-start.52 = (f32[2,512,12]{2,1,0:T(8,128)S(1)}, f32[2,512,12]{2,1,0:T(8,128)}, u32[]{:S(2)}) copy-start(f32[2,512,12]{2,1,0:T(8,128)} %copy-done.51) | copy-start | bytes 147460
  207.8 33.8 %copy-start.53 = (f32[2,512,12]{2,1,0:T(8,128)S(1)}, f32[2,512,12]{2,1,0:T(8,128)}, u32[]{:S(2)}) copy-start(f32[2,512,12]{2,1,0:T(8,128)} %get-tuple-element.277) | copy-start | bytes 147460
  207.8 34.0 %copy-start.56 = (f32[2,512,12]{2,1,0:T(8,128)S(1)}, f32[2,512,12]{2,1,0:T(8,128)}, u32[]{:S(2)}) copy-start(f32[2,512,12]{2,1,0:T(8,128)} %copy-done.55) | copy-start | bytes 147460
  207.8 34.0 %copy-start.63 = (u8[512,12]{1,0:T(8,128)(4,1)S(1)}, u8[512,12]{1,0:T(8,128)(4,1)}, u32[]{:S(2)}) copy-start(u8[512,12]{1,0:T(8,128)(4,1)} %copy-done.62) | copy-start | bytes 18436
  207.8 220.8 %all-to-all-start.1 = ((bf16[8,192,1536]{2,1,0:T(8,128)(2,1)}), bf16[8,192,1536]{2,1,0:T(8,128)(2,1)}, u32[]{:S(2)}, u32[]{:S(2)}) async-start(bf16[8,192,1536]{2,1,0:T(8,128)(2,1)} %bitcast.308), calls=%async_computation.1 | async-start | bytes 9437184 | tf_op jit(solution)/shard_map/all_to_all | solution.py:958
  249.9 32.7 %copy-start.89 = (f32[768]{0:T(1024)}, f32[768]{0:T(1024)S(1)}, u32[]{:S(2)}) copy-start(f32[768]{0:T(1024)S(1)} %mul.501) | copy-start | bytes 9220
  282.7 16.6 %copy-start.105 = (f32[768]{0:T(1024)S(1)}, f32[768]{0:T(1024)}, u32[]{:S(2)}) copy-start(f32[768]{0:T(1024)} %param.40) | copy-start | bytes 9220
  330.9 216.2 %copy-start.7 = (bf16[2,128,1536]{2,1,0:T(8,128)(2,1)}, bf16[2,128,1536]{2,1,0:T(8,128)(2,1)S(1)}, u32[]{:S(2)}) copy-start(bf16[2,128,1536]{2,1,0:T(8,128)(2,1)S(1)} %multiply_convert_fusion.2.refs_0_) | copy-start | bytes 2359300
  330.9 95.1 %copy-start.46 = (bf16[4,192,1536]{2,1,0:T(8,128)(2,1)S(1)}, bf16[4,192,1536]{2,1,0:T(8,128)(2,1)}, u32[]{:S(2)}) copy-start(bf16[4,192,1536]{2,1,0:T(8,128)(2,1)} %get-tuple-element.264) | copy-start | bytes 7077892
  428.6 110.0 %all-to-all-start = ((bf16[8,192,1536]{2,1,0:T(8,128)(2,1)}), bf16[8,192,1536]{2,1,0:T(8,128)(2,1)}, u32[]{:S(2)}, u32[]{:S(2)}) async-start(bf16[8,192,1536]{2,1,0:T(8,128)(2,1)} %bitcast.307), calls=%async_computation | async-start | bytes 9437184 | tf_op jit(solution)/shard_map/all_to_all | solution.py:958
  538.6 112.9 %all-to-all-start.2 = ((bf16[8,192,1536]{2,1,0:T(8,128)(2,1)}), bf16[8,192,1536]{2,1,0:T(8,128)(2,1)}, u32[]{:S(2)}, u32[]{:S(2)}) async-start(bf16[8,192,1536]{2,1,0:T(8,128)(2,1)} %bitcast.320), calls=%async_computation.2 | async-start | bytes 9437184 | tf_op jit(solution)/shard_map/all_to_all | solution.py:954
  557.2 87.2 %copy-start.108 = (bf16[2,512,256]{1,2,0:T(8,128)(2,1)}, bf16[2,512,256]{1,2,0:T(8,128)(2,1)S(1)}, u32[]{:S(2)}) copy-start(bf16[2,512,256]{1,2,0:T(8,128)(2,1)S(1)} %get-tuple-element.270) | copy-start | bytes 1572868
  652.1 64.8 %all-to-all-start.3 = ((f32[16,2,128,2]{2,3,1,0:T(2,128)}), f32[16,2,128,2]{2,3,1,0:T(2,128)S(1)}, u32[]{:S(2)}, u32[]{:S(2)}) async-start(f32[16,2,128,2]{2,3,1,0:T(2,128)} %copy.376), calls=%async_computation.3 | async-start | bytes 65536 | tf_op jit(solution)/shard_map/all_to_all | solution.py:1108
  661.4 55.7 %copy-start.65 = (f32[1536]{0:T(1024)S(1)}, f32[1536]{0:T(1024)}, u32[]{:S(2)}) copy-start(f32[1536]{0:T(1024)} %copy-done.64) | copy-start | bytes 18436
  720.0 23.7 %copy-start.112 = (f32[2,512,768]{2,1,0:T(8,128)S(1)}, f32[2,512,768]{2,1,0:T(8,128)}, u32[]{:S(2)}) copy-start(f32[2,512,768]{2,1,0:T(8,128)} %get-tuple-element.256) | copy-start | bytes 9437188
  779.5 129.5 %copy-start.37 = (f32[2,128,1536]{2,1,0:T(8,128)S(1)}, f32[2,128,1536]{2,1,0:T(8,128)}, u32[]{:S(2)}) copy-start(f32[2,128,1536]{2,1,0:T(8,128)} %copy-done.35) | copy-start | bytes 4718596
  913.0 15.9 %all-to-all-start.4 = ((bf16[2,1,128,1536]{2,0,1,3:T(2,128)(2,1)}), bf16[2,1,128,1536]{2,0,1,3:T(2,128)(2,1)}, u32[]{:S(2)}, u32[]{:S(2)}) async-start(bf16[2,1,128,1536]{2,0,1,3:T(2,128)(2,1)} %copy.385), calls=%async_computation.4 | async-start | bytes 1572864 | tf_op jit(solution)/shard_map/all_to_all | solution.py:814
  917.2 16.1 %copy-start.32 = (f32[2,12,128]{2,1,0:T(8,128)S(1)}, f32[2,12,128]{2,1,0:T(8,128)}, u32[]{:S(2)}) copy-start(f32[2,12,128]{2,1,0:T(8,128)} %copy-done.31) | copy-start | bytes 36868
  928.9 57.7 %all-to-all-start.6 = ((f32[2,1,128,1536]{2,0,1,3:T(2,128)}), f32[2,1,128,1536]{2,0,1,3:T(2,128)}, u32[]{:S(2)}, u32[]{:S(2)}) async-start(f32[2,1,128,1536]{2,0,1,3:T(2,128)} %copy.396), calls=%async_computation.6 | async-start | bytes 3145728 | tf_op jit(solution)/shard_map/all_to_all | solution.py:814
  986.6 145.9 %all-to-all-start.5 = ((bf16[8,192,1536]{2,1,0:T(8,128)(2,1)}), bf16[8,192,1536]{2,1,0:T(8,128)(2,1)}, u32[]{:S(2)}, u32[]{:S(2)}) async-start(bf16[8,192,1536]{2,1,0:T(8,128)(2,1)} %bitcast.319), calls=%async_computation.5 | async-start | bytes 9437184 | tf_op jit(solution)/shard_map/all_to_all | solution.py:954
  997.6 65.3 %copy-start.8 = (bf16[2,128,1536]{2,1,0:T(8,128)(2,1)S(1)}, bf16[2,128,1536]{2,1,0:T(8,128)(2,1)}, u32[]{:S(2)}) copy-start(bf16[2,128,1536]{2,1,0:T(8,128)(2,1)} %copy-done.7) | copy-start | bytes 2359300
  1077.8 18.7 %collective-permute-start.1 = (f32[2,8,1024]{2,1,0:T(8,128)}, f32[2,8,1024]{2,1,0:T(8,128)}, u32[]{:S(2)}, u32[]{:S(2)}) collective-permute-start(f32[2,8,1024]{2,1,0:T(8,128)} %slice.297), channel_id=1, source_target_pairs={{4,0},{8,4},{12,8},{16,12},{20,16},{24,20},{28,24},{5,1},{9,5},{13... | collective-permute-start | bytes 196616 | tf_op jit(solution)/shard_map/ppermute | solution.py:1194
  1102.2 17.2 %copy-start.49 = (bf16[2,512,1536]{2,1,0:T(8,128)(2,1)S(1)}, bf16[2,512,1536]{2,1,0:T(8,128)(2,1)}, u32[]{:S(2)}) copy-start(bf16[2,512,1536]{2,1,0:T(8,128)(2,1)} %copy-done.47) | copy-start | bytes 9437188
  1147.0 57.9 %copy-start.20 = (bf16[2,512,384]{2,1,0:T(8,128)(2,1)S(1)}, bf16[2,512,384]{2,1,0:T(8,128)(2,1)}, u32[]{:S(2)}) copy-start(bf16[2,512,384]{2,1,0:T(8,128)(2,1)} %refs_0_.1) | copy-start | bytes 2359300
  1147.0 57.9 %copy-start.78 = (f32[2,512]{1,0:T(2,128)S(1)}, f32[2,512]{1,0:T(2,128)}, u32[]{:S(2)}) copy-start(f32[2,512]{1,0:T(2,128)} %copy-done.77) | copy-start | bytes 12292
  1147.0 57.9 %copy-start.90 = (f32[2,512]{1,0:T(2,128)S(1)}, f32[2,512]{1,0:T(2,128)}, u32[]{:S(2)}) copy-start(f32[2,512]{1,0:T(2,128)} %fusion.127) | copy-start | bytes 12292
  1147.0 57.9 %copy-start.95 = (f32[384]{0:T(512)S(1)}, f32[384]{0:T(512)}, u32[]{:S(2)}) copy-start(f32[384]{0:T(512)} %param.29) | copy-start | bytes 4612
  (100 other events, 453.6 us)
Sparse Core Ops, SparseCore 0:
  74.4 131.9 all-gather.2
  207.9 200.1 all-gather.4

commit v4 on v3

--- a/solution.py
+++ b/solution.py
@@ -86,7 +86,7 @@
         return (lead, self.count, rows, columns)
 
 
-def gather_kernel(jobs, *refs):
+def gather_kernel(jobs, in_turns, *refs):
     me = (lax.axis_index("seq"), lax.axis_index("head"))
     number = len(jobs)
     x_refs, o_refs, sems = refs[:number], refs[number : 2 * number], refs[2 * number :]
@@ -99,6 +99,8 @@
     deepest_first = sorted(range(number), key=lambda j: -jobs[j].depth)
     turns = [(0, j) for j in range(number)]
     turns += [(step, j) for j in deepest_first for step in range(1, jobs[j].depth)]
+    if in_turns:
+        turns.sort()
     for step, j in turns:
         job = jobs[j]
         send_sem, recv_sem, own_sem, own_block = sems[4 * j : 4 * j + 4]
@@ -139,7 +141,7 @@
         own.wait()
 
 
-def cube_gather(jobs, arrays, collective_id, weight=100 << 20):
+def cube_gather(jobs, arrays, collective_id, in_turns=False, weight=100 << 20):
     anywhere = pl.BlockSpec(memory_space=pl.ANY)
     scratch = []
     for job, x in zip(jobs, arrays, strict=True):
@@ -147,7 +149,7 @@
             scratch.append(pltpu.SemaphoreType.DMA(shape))
         scratch.append(pltpu.VMEM(x.shape, x.dtype))
     return pl.pallas_call(
-        functools.partial(gather_kernel, jobs),
+        functools.partial(gather_kernel, jobs, in_turns),
         out_shape=tuple(
             jax.ShapeDtypeStruct(job.whole_shape(x.shape), x.dtype)
             for job, x in zip(jobs, arrays, strict=True)
@@ -662,7 +664,7 @@
     )(x, keys, cols, rows, dy, state, later)
 
 
-TILE = 256
+TILE = 512
 
 
 def expert_kernel(first, capacity, lines_ref, cols_ref, rows_ref, grads_ref, weights_ref, *refs):
@@ -932,20 +934,9 @@
     resid_in = own_rows(hidden_full).astype(F32)
     grad_rows = own_rows(grad_full)
 
-    second_shard = jnp.concatenate(
-        [
-            input_proj[0],
-            output_proj.T,
-            router,
-            shared_up.reshape(slice_rows, 2 * shared_local),
-            shared_down.T,
-        ],
-        axis=1,
-    )
+    second_shard = jnp.concatenate([input_proj[0], output_proj.T, router], axis=1)
     second_full = lax.all_gather(tied(second_shard, first_full), "seq", axis=0, tiled=True)
-    cuts = [inner_local, inner_local, expert_total, 2 * shared_local, shared_local]
-    cuts = [sum(cuts[: i + 1]) for i in range(4)]
-    proj_gate, out_t, router_full, shared_flat, shared_down_t = jnp.split(second_full, cuts, axis=1)
+    proj_gate, out_t, router_full = jnp.split(second_full, [inner_local, 2 * inner_local], axis=1)
     expert_shard = jnp.concatenate([expert_up, expert_down.transpose(0, 2, 1)], axis=2)
     expert_shard = expert_shard.reshape(MEMBERS, own_experts, slice_rows, 3 * EFF)
 
@@ -1025,6 +1016,9 @@
     state_in = chain(passing, local_state, 1, 8)
     experts = [fetch_expert(0, state_in)]
     local_out = scan_forward(signal, keys, cols, rows)
+    shared_shard = jnp.concatenate(
+        [shared_up.reshape(slice_rows, 2 * shared_local), shared_down.T], axis=1
+    )
     grad_group = lax.all_gather(
         tied(grad_rows, state_in), ("seq", "head"), axis=1, tiled=True, axis_index_groups=groups
     ).reshape(micro, MEMBERS, tokens, D)
@@ -1045,6 +1039,8 @@
     moe_group = gather_group(moe_rows, 2)
 
     expert_ids = jnp.arange(expert_total, dtype=jnp.int32)
+    shared_full = lax.all_gather(tied(shared_shard, moe_group), "seq", axis=0, tiled=True)
+    shared_flat, shared_down_t = jnp.split(shared_full, [2 * shared_local], axis=1)
     experts += [fetch_expert(own, moe_group) for own in range(1, own_experts)]
 
     def dense_weights(route_lines, rows):
@@ -1289,6 +1285,7 @@
         ],
         [over_heads, own_small, all_small],
         7,
+        True,
     )
     over_heads = jnp.sum(heads_found[0], axis=0)
     state_w, router_w = over_heads[:, : 2 * STATE], over_heads[:, 2 * STATE : 2 * STATE + expert_total]

time: 1260 us -> 1240 us (0.984)
  Pallas kernels: 799 us -> 739 us
  waiting for transfers between devices: 32.9 us -> 82.2 us
    all_to_all x2, waiting for transfers between devices: 24.8 us -> 62.9 us  [fetch_expert(): lax.all_to_all(tied(send, *after), 'seq', 0, 0, tiled=True)]
    pallas_call x2, Pallas kernels: 124 us -> 97.4 us  [chain(): pl.pallas_call(functools.partial(chain_kernel, way, widths), out_shape=ja...]
    pallas_call x2, Pallas kernels: 137 us -> 116 us  [run_expert(): pl.pallas_call(functools.partial(expert_kernel, not before, capacity), gr...]
    unnamed x251 -> x257, local copies, waits for them, and re-layouts: 38.3 us -> 37.8 us
  transfers between devices with their start and end apart: 11 -> 12, of which waited for: 2 -> 3; matrix products, arithmetic and copies ran while one was open for 17% -> 17% of each run, Pallas kernels for 41% -> 37%
where the time goes in v4:
time: 1240 us
  Pallas kernels  739 us (60%)
  local copies, waits for them, and re-layouts  125 us (10%)
  matrix products  123 us (10%)
  waiting for transfers between devices  82.2 us (7%)
  other arithmetic  74.9 us (6%)
  starting transfers between devices  63.4 us (5%)
  between operations  15.9 us (1%)
  blocking collectives  12.7 us (1%)
    pallas_call x4, Pallas kernels, cube_reduce(): pl.pallas_call(functools.partial(reduce_kernel, jobs), out_shape=tuple(ou...  264 us
    pallas_call x4, Pallas kernels, cube_gather(): pl.pallas_call(functools.partial(gather_kernel, jobs, in_turns), out_shap...  182 us
    pallas_call x2, Pallas kernels, run_expert(): pl.pallas_call(functools.partial(expert_kernel, not before, capacity), gr...  116 us
    pallas_call x2, Pallas kernels, chain(): pl.pallas_call(functools.partial(chain_kernel, way, widths), out_shape=ja...  97.4 us
    dot_general x23, matrix products, mm(): return lax.dot_general(a, b, (dims, ((), ())), preferred_element_type=out)  95.9 us
    all_to_all x2, waiting for transfers between devices, fetch_expert(): lax.all_to_all(tied(send, *after), 'seq', 0, 0, tiled=True)  62.9 us
    pallas_call x1, Pallas kernels, scan_backward(): pl.pallas_call(backward_kernel, grid=(micro, pairs), out_shape=(jax.Shape...  61 us
    unnamed x257, local copies, waits for them, and re-layouts  37.8 us
  transfers between devices with their start and end apart: 12, of which 3 were waited for; matrix products, arithmetic and copies ran while one was open for 17% of the time, Pallas kernels for 37%

profile of v4, /device:TPU:0, one launch (start us, length us, event | category | flops | bytes accessed | tf_op | source)
XLA Modules:
  0.0 1236.2 jit_solution(4068687483307164844)
XLA Ops:
  19.0 50.5 %shard_map.391 = (bf16[2,512,1536]{2,1,0:T(8,128)(2,1)S(1)}, bf16[2,512,1536]{2,1,0:T(8,128)(2,1)S(1)}, f32[1,8,1536]{2,1,0:T(8,128)S(1)}, bf16[1,8,192,1152]{3,2,1,0:T(8,128)(2,1)S(1)}, s32[2,4,8,512]{3,2,1,0:T(8,128)S(1)}) custom-call(bf16[2,512,384]{2,1,0:T(8,128)(2,1)S(1)} %copy-done.19, bf16[2,512,384]{2,1,0:T(8,128)(2,1)S(1)} %copy-done.30, ...), custom_call_target="tpu_custom_call" | custom-call | bytes 104857600 | tf_op jit(solution)/shard_map/pallas_call | solution.py:151
  93.5 6.8 fusion.55
  111.5 10.9 fusion.25
  127.6 46.1 %shard_map.393.state_ref = f32[2,768,128]{2,1,0:T(8,128)S(1)} custom-call(f32[2,768,128]{2,1,0:T(8,128)S(1)} %fusion.41.state_ref, f32[2,12,128]{2,1,0:T(8,128)S(1)} %broadcast_in_dim.205.pass_ref), custom_call_target="tpu_custom_call" | custom-call | bytes 104857600 | tf_op jit(solution)/shard_map/pallas_call | solution.py:436
  181.4 30.8 %all-to-all-start.1 = ((bf16[8,192,1536]{2,1,0:T(8,128)(2,1)}), bf16[8,192,1536]{2,1,0:T(8,128)(2,1)}, u32[]{:S(2)}, u32[]{:S(2)}) async-start(bf16[8,192,1536]{2,1,0:T(8,128)(2,1)} %bitcast.312), calls=%async_computation.1 | async-start | bytes 9437184 | tf_op jit(solution)/shard_map/all_to_all | solution.py:949
  224.3 19.6 %shard_map.392 = f32[2,512,768]{2,1,0:T(8,128)S(1)} custom-call(f32[2,512,768]{2,1,0:T(8,128)S(1)} %slice.283.x_ref, f32[2,512,256]{2,1,0:T(8,128)S(1)} %slice.284.keys_ref, f32[2,6,512,8]{3,2,1,0:T(8,128)S(1)} %copy.362.cols_ref, f32[2,6,8,512]{3,2,1,0:T(8,128)S(1)} %bitcast.295), custom_call_target="tpu_custom_call" | custom-call | flops 1101004800 | bytes 9437184 | tf_op jit(solution)/shard_map/pallas_call | solution.py:544
  253.7 9.8 multiply_reduce_fusion.3
  263.5 6.2 psum.14
  269.7 6.9 fusion.61
  276.6 21.9 %shard_map.394 = f32[2,128,1536]{2,1,0:T(8,128)S(1)} custom-call(bf16[2,4,128,1536]{3,2,1,0:T(8,128)(2,1)} %bitcast.326), custom_call_target="tpu_custom_call" | custom-call | bytes 104857600 | tf_op jit(solution)/shard_map/pallas_call | solution.py:283
  301.3 90.7 %shard_map.395 = bf16[2,16,128,1536]{3,2,1,0:T(8,128)(2,1)S(1)} custom-call(bf16[2,128,1536]{2,1,0:T(8,128)(2,1)S(1)} %multiply_convert_fusion.2.refs_0_), custom_call_target="tpu_custom_call" | custom-call | bytes 104857600 | tf_op jit(solution)/shard_map/pallas_call | solution.py:151
  405.5 8.3 fusion.106
  417.4 57.5 %shard_map.396 = (bf16[8,512,1536]{2,1,0:T(8,128)(2,1)}, bf16[8,512,1536]{2,1,0:T(8,128)(2,1)}, f32[8,8,512]{2,1,0:T(8,128)}, bf16[1536,1536]{1,0:T(8,128)(2,1)}) custom-call(f32[8,8,512]{2,1,0:T(8,128)} %bitcast.344, f32[8,512,8]{2,1,0:T(8,128)} %bitcast.328, bf16[8,512,1536]{2,1,0:T(8,128)(2,1)} %bitcast.291, bf16[8,512,1536]{2,1,0:T(8,128)(2,1)} %bitcast.376, ...), custom_call_target="tpu_custom_call" | custom-call | flops 31406948352 | bytes 75497472 | tf_op jit(solution)/shard_map/pallas_call | solution.py:734
  474.9 62.9 %all-to-all-done = bf16[8,192,1536]{2,1,0:T(8,128)(2,1)} async-done(((bf16[8,192,1536]{2,1,0:T(8,128)(2,1)}), bf16[8,192,1536]{2,1,0:T(8,128)(2,1)}, u32[]{:S(2)}, u32[]{:S(2)}) %all-to-all-start) | async-done | bytes 4718624 | tf_op jit(solution)/shard_map/all_to_all | solution.py:949
  561.0 58.6 %shard_map.397 = (bf16[8,512,1536]{2,1,0:T(8,128)(2,1)}, bf16[8,512,1536]{2,1,0:T(8,128)(2,1)}, f32[8,8,512]{2,1,0:T(8,128)}, bf16[1536,1536]{1,0:T(8,128)(2,1)}) custom-call(f32[8,8,512]{2,1,0:T(8,128)} %bitcast.343, f32[8,512,8]{2,1,0:T(8,128)} %bitcast.327, bf16[8,512,1536]{2,1,0:T(8,128)(2,1)} %bitcast.293, bf16[8,512,1536]{2,1,0:T(8,128)(2,1)} %bitcast.378, ...), custom_call_target="tpu_custom_call" | custom-call | flops 31406948352 | bytes 75497472 | tf_op jit(solution)/shard_map/pallas_call | solution.py:734
  636.2 11.1 all-to-all-done.2
  655.5 55.5 %shard_map.398 = f32[2,128,1536]{2,1,0:T(8,128)S(1)} custom-call(bf16[2,16,128,1536]{3,2,1,0:T(8,128)(2,1)} %bitcast.65.refs_0_), custom_call_target="tpu_custom_call" | custom-call | bytes 104857600 | tf_op jit(solution)/shard_map/pallas_call | solution.py:283
  717.0 20.7 %shard_map.399 = (bf16[2,4,128,1536]{3,2,1,0:T(8,128)(2,1)S(1)}, f32[2,4,8,128]{3,2,1,0:T(8,128)S(1)}) custom-call(bf16[2,128,1536]{2,1,0:T(8,128)(2,1)S(1)} %get-tuple-element.254.refs_0_, f32[2,8,128]{2,1,0:T(8,128)S(1)} %broadcast_in_dim.212.refs_1_), custom_call_target="tpu_custom_call" | custom-call | bytes 104857600 | tf_op jit(solution)/shard_map/pallas_call | solution.py:151
  741.8 6.6 multiply_reduce_fusion.1
  755.1 10.2 copy.396
  765.3 7.9 fusion.38.state_ref
  773.2 128.5 %shard_map.400 = (f32[2,128,1536]{2,1,0:T(8,128)S(1)}, f32[1,192,2304]{2,1,0:T(8,128)}) custom-call(bf16[2,16,128,1536]{3,2,1,0:T(8,128)(2,1)} %bitcast.61.refs_0_, bf16[1,8,192,2304]{3,2,1,0:T(8,128)(2,1)} %bitcast.310), custom_call_target="tpu_custom_call" | custom-call | bytes 104857600 | tf_op jit(solution)/shard_map/pallas_call | solution.py:283
  913.7 8.1 all-to-all-done.4
  927.2 51.3 %shard_map.401.next_ref = f32[2,768,128]{2,1,0:T(8,128)S(1)} custom-call(f32[2,768,128]{2,1,0:T(8,128)S(1)} %copy-done.16, f32[2,12,128]{2,1,0:T(8,128)S(1)} %copy-done.33), custom_call_target="tpu_custom_call" | custom-call | bytes 104857600 | tf_op jit(solution)/shard_map/pallas_call | solution.py:436
  990.5 61.0 %shard_map.402 = (f32[2,512,768]{2,1,0:T(8,128)S(1)}, f32[2,512,256]{2,1,0:T(8,128)S(1)}, f32[2,6,512,8]{3,2,1,0:T(8,128)S(1)}, f32[2,6,8,512]{3,2,1,0:T(8,128)S(1)}) custom-call(f32[2,512,768]{2,1,0:T(8,128)S(1)} %copy-done.4, f32[2,512,256]{2,1,0:T(8,128)S(1)} %copy-done.10, f32[2,6,512,8]{3,2,1,0:T(8,128)S(1)} %copy-done.2, ...), custom_call_target="tpu_custom_call" | custom-call | tf_op jit(solution)/shard_map/pallas_call | solution.py:651
  1061.7 6.3 select_reduce_fusion.2
  1083.1 6.3 fusion.58
  1095.1 9.4 fusion.6
  1104.5 6.5 psum.15
  1112.3 7.5 fusion.101
  1139.9 57.7 %shard_map.403 = (f32[2,512,384]{2,1,0:T(8,128)}, f32[1,192,1152]{2,1,0:T(8,128)S(1)}, f32[1,192,128]{2,1,0:T(8,128)S(1)}) custom-call(bf16[2,512,1536]{2,1,0:T(8,128)(2,1)} %get-tuple-element.264.refs_0_, bf16[1,8,192,1152]{3,2,1,0:T(8,128)(2,1)} %bitcast.325, bf16[1,8,192,128]{3,2,1,0:T(8,128)(2,1)S(1)} %bitcast.301), custom_call_target="tpu_custom_call" | custom-call | bytes 104857600 | tf_op jit(solution)/shard_map/pallas_call | solution.py:283
  1201.2 19.7 %shard_map.404 = (f32[1,4,192,384]{3,2,1,0:T(8,128)S(1)}, f32[1,8,40,128]{3,2,1,0:T(8,128)S(1)}, f32[1,32,24,128]{3,2,1,0:T(8,128)S(1)}) custom-call(f32[1,192,384]{2,1,0:T(8,128)S(1)} %fusion.111.refs_0_, f32[1,40,128]{2,1,0:T(8,128)S(1)} %pad_bitcast_fusion.refs_1_, f32[1,24,128]{2,1,0:T(8,128)S(1)} %fusion.121.refs_2_), custom_call_target="tpu_custom_call" | custom-call | bytes 104857600 | tf_op jit(solution)/shard_map/pallas_call | solution.py:151
  (450 shorter events, 258.4 us)
Async XLA Ops:
  7.2 241.0 %all-gather.4.cloned.1.call-start = ((), (), s32[]{:S(2)}) async-start(), calls=%async_computation.7 | async-start | bytes 5750784 | tf_op jit(solution)/shard_map/all_gather | solution.py:938
  73.6 343.8 %all-gather.6.cloned.1.call-start = ((), (), s32[]{:S(2)}) async-start(), calls=%async_computation.8 | async-start | bytes 13369344 | tf_op jit(solution)/shard_map/all_gather | solution.py:1022
  73.7 226.3 %copy-start.66 = (f32[1536]{0:T(1024)}, f32[1536]{0:T(1024)S(1)}, u32[]{:S(2)}) copy-start(f32[1536]{0:T(1024)S(1)} %get-tuple-element.242) | copy-start | bytes 18436
  75.9 34.1 %collective-permute-start = (bf16[2,8,1536]{2,1,0:T(8,128)(2,1)}, bf16[2,8,1536]{2,1,0:T(8,128)(2,1)}, u32[]{:S(2)}, u32[]{:S(2)}) collective-permute-start(bf16[2,8,1536]{2,1,0:T(8,128)(2,1)} %slice.269), channel_id=1, source_target_pairs={{0,4},{4,8},{8,12},{12,16},{16,20},{20,24},{24,28},{1,5},{5,9},{9,... | collective-permute-start | bytes 147464 | tf_op jit(solution)/shard_map/ppermute | solution.py:956
  122.4 52.8 %copy-start.51 = (bf16[8,192,1024]{2,1,0:T(8,128)(2,1)S(1)}, bf16[8,192,1024]{2,1,0:T(8,128)(2,1)}, u32[]{:S(2)}) copy-start(bf16[8,192,1024]{2,1,0:T(8,128)(2,1)} %param.44) | copy-start | bytes 9437188
  181.4 30.8 %copy-start.53 = (f32[2,512,12]{2,1,0:T(8,128)S(1)}, f32[2,512,12]{2,1,0:T(8,128)}, u32[]{:S(2)}) copy-start(f32[2,512,12]{2,1,0:T(8,128)} %copy-done.52) | copy-start | bytes 147460
  181.4 31.0 %copy-start.54 = (f32[2,512,12]{2,1,0:T(8,128)S(1)}, f32[2,512,12]{2,1,0:T(8,128)}, u32[]{:S(2)}) copy-start(f32[2,512,12]{2,1,0:T(8,128)} %get-tuple-element.279) | copy-start | bytes 147460
  181.4 31.2 %copy-start.57 = (f32[2,512,12]{2,1,0:T(8,128)S(1)}, f32[2,512,12]{2,1,0:T(8,128)}, u32[]{:S(2)}) copy-start(f32[2,512,12]{2,1,0:T(8,128)} %copy-done.56) | copy-start | bytes 147460
  181.4 31.2 %copy-start.64 = (u8[512,12]{1,0:T(8,128)(4,1)S(1)}, u8[512,12]{1,0:T(8,128)(4,1)}, u32[]{:S(2)}) copy-start(u8[512,12]{1,0:T(8,128)(4,1)} %copy-done.63) | copy-start | bytes 18436
  181.4 217.9 %all-to-all-start.1 = ((bf16[8,192,1536]{2,1,0:T(8,128)(2,1)}), bf16[8,192,1536]{2,1,0:T(8,128)(2,1)}, u32[]{:S(2)}, u32[]{:S(2)}) async-start(bf16[8,192,1536]{2,1,0:T(8,128)(2,1)} %bitcast.312), calls=%async_computation.1 | async-start | bytes 9437184 | tf_op jit(solution)/shard_map/all_to_all | solution.py:949
  220.9 32.7 %copy-start.92 = (f32[768]{0:T(1024)}, f32[768]{0:T(1024)S(1)}, u32[]{:S(2)}) copy-start(f32[768]{0:T(1024)S(1)} %mul.501) | copy-start | bytes 9220
  253.6 16.1 %copy-start.109 = (f32[768]{0:T(1024)S(1)}, f32[768]{0:T(1024)}, u32[]{:S(2)}) copy-start(f32[768]{0:T(1024)} %param.40) | copy-start | bytes 9220
  301.3 245.2 %copy-start.7 = (bf16[2,128,1536]{2,1,0:T(8,128)(2,1)}, bf16[2,128,1536]{2,1,0:T(8,128)(2,1)S(1)}, u32[]{:S(2)}) copy-start(bf16[2,128,1536]{2,1,0:T(8,128)(2,1)S(1)} %multiply_convert_fusion.2.refs_0_) | copy-start | bytes 2359300
  301.3 95.3 %copy-start.47 = (bf16[4,192,1536]{2,1,0:T(8,128)(2,1)S(1)}, bf16[4,192,1536]{2,1,0:T(8,128)(2,1)}, u32[]{:S(2)}) copy-start(bf16[4,192,1536]{2,1,0:T(8,128)(2,1)} %get-tuple-element.266) | copy-start | bytes 7077892
  399.2 138.6 %all-to-all-start = ((bf16[8,192,1536]{2,1,0:T(8,128)(2,1)}), bf16[8,192,1536]{2,1,0:T(8,128)(2,1)}, u32[]{:S(2)}, u32[]{:S(2)}) async-start(bf16[8,192,1536]{2,1,0:T(8,128)(2,1)} %bitcast.311), calls=%async_computation | async-start | bytes 9437184 | tf_op jit(solution)/shard_map/all_to_all | solution.py:949
  404.0 143.9 %all-gather.8.cloned.1.call-start = ((), (), s32[]{:S(2)}) async-start(), calls=%async_computation.9 | async-start | bytes 2654208 | tf_op jit(solution)/shard_map/all_gather | solution.py:1042
  537.8 109.5 %all-to-all-start.2 = ((bf16[8,192,1536]{2,1,0:T(8,128)(2,1)}), bf16[8,192,1536]{2,1,0:T(8,128)(2,1)}, u32[]{:S(2)}, u32[]{:S(2)}) async-start(bf16[8,192,1536]{2,1,0:T(8,128)(2,1)} %bitcast.324), calls=%async_computation.2 | async-start | bytes 9437184 | tf_op jit(solution)/shard_map/all_to_all | solution.py:945
  648.0 63.1 %all-to-all-start.3 = ((f32[16,2,128,2]{2,3,1,0:T(2,128)}), f32[16,2,128,2]{2,3,1,0:T(2,128)S(1)}, u32[]{:S(2)}, u32[]{:S(2)}) async-start(f32[16,2,128,2]{2,3,1,0:T(2,128)} %copy.388), calls=%async_computation.3 | async-start | bytes 65536 | tf_op jit(solution)/shard_map/all_to_all | solution.py:1104
  655.5 55.6 %copy-start.67 = (f32[1536]{0:T(1024)S(1)}, f32[1536]{0:T(1024)}, u32[]{:S(2)}) copy-start(f32[1536]{0:T(1024)} %copy-done.66) | copy-start | bytes 18436
  714.1 23.7 %copy-start.115 = (f32[2,512,768]{2,1,0:T(8,128)S(1)}, f32[2,512,768]{2,1,0:T(8,128)}, u32[]{:S(2)}) copy-start(f32[2,512,768]{2,1,0:T(8,128)} %get-tuple-element.258) | copy-start | bytes 9437188
  773.2 128.5 %copy-start.38 = (f32[2,128,1536]{2,1,0:T(8,128)S(1)}, f32[2,128,1536]{2,1,0:T(8,128)}, u32[]{:S(2)}) copy-start(f32[2,128,1536]{2,1,0:T(8,128)} %copy-done.36) | copy-start | bytes 4718596
  905.8 15.9 %all-to-all-start.4 = ((bf16[2,1,128,1536]{2,0,1,3:T(2,128)(2,1)}), bf16[2,1,128,1536]{2,0,1,3:T(2,128)(2,1)}, u32[]{:S(2)}, u32[]{:S(2)}) async-start(bf16[2,1,128,1536]{2,0,1,3:T(2,128)(2,1)} %copy.397), calls=%async_computation.4 | async-start | bytes 1572864 | tf_op jit(solution)/shard_map/all_to_all | solution.py:816
  910.0 16.1 %copy-start.33 = (f32[2,12,128]{2,1,0:T(8,128)S(1)}, f32[2,12,128]{2,1,0:T(8,128)}, u32[]{:S(2)}) copy-start(f32[2,12,128]{2,1,0:T(8,128)} %copy-done.32) | copy-start | bytes 36868
  921.7 57.7 %all-to-all-start.6 = ((f32[2,1,128,1536]{2,0,1,3:T(2,128)}), f32[2,1,128,1536]{2,0,1,3:T(2,128)}, u32[]{:S(2)}, u32[]{:S(2)}) async-start(f32[2,1,128,1536]{2,0,1,3:T(2,128)} %copy.408), calls=%async_computation.6 | async-start | bytes 3145728 | tf_op jit(solution)/shard_map/all_to_all | solution.py:816
  979.4 146.0 %all-to-all-start.5 = ((bf16[8,192,1536]{2,1,0:T(8,128)(2,1)}), bf16[8,192,1536]{2,1,0:T(8,128)(2,1)}, u32[]{:S(2)}, u32[]{:S(2)}) async-start(bf16[8,192,1536]{2,1,0:T(8,128)(2,1)} %bitcast.323), calls=%async_computation.5 | async-start | bytes 9437184 | tf_op jit(solution)/shard_map/all_to_all | solution.py:945
  990.5 65.3 %copy-start.8 = (bf16[2,128,1536]{2,1,0:T(8,128)(2,1)S(1)}, bf16[2,128,1536]{2,1,0:T(8,128)(2,1)}, u32[]{:S(2)}) copy-start(bf16[2,128,1536]{2,1,0:T(8,128)(2,1)} %copy-done.7) | copy-start | bytes 2359300
  1070.8 18.7 %collective-permute-start.1 = (f32[2,8,1024]{2,1,0:T(8,128)}, f32[2,8,1024]{2,1,0:T(8,128)}, u32[]{:S(2)}, u32[]{:S(2)}) collective-permute-start(f32[2,8,1024]{2,1,0:T(8,128)} %slice.297), channel_id=1, source_target_pairs={{4,0},{8,4},{12,8},{16,12},{20,16},{24,20},{28,24},{5,1},{9,5},{13... | collective-permute-start | bytes 196616 | tf_op jit(solution)/shard_map/ppermute | solution.py:1190
  1095.1 17.2 %copy-start.50 = (bf16[2,512,1536]{2,1,0:T(8,128)(2,1)S(1)}, bf16[2,512,1536]{2,1,0:T(8,128)(2,1)}, u32[]{:S(2)}) copy-start(bf16[2,512,1536]{2,1,0:T(8,128)(2,1)} %copy-done.48) | copy-start | bytes 9437188
  1139.9 57.9 %copy-start.20 = (bf16[2,512,384]{2,1,0:T(8,128)(2,1)S(1)}, bf16[2,512,384]{2,1,0:T(8,128)(2,1)}, u32[]{:S(2)}) copy-start(bf16[2,512,384]{2,1,0:T(8,128)(2,1)} %refs_0_.1) | copy-start | bytes 2359300
  1139.9 57.9 %copy-start.81 = (f32[2,512]{1,0:T(2,128)S(1)}, f32[2,512]{1,0:T(2,128)}, u32[]{:S(2)}) copy-start(f32[2,512]{1,0:T(2,128)} %copy-done.80) | copy-start | bytes 12292
  1139.9 57.9 %copy-start.93 = (f32[2,512]{1,0:T(2,128)S(1)}, f32[2,512]{1,0:T(2,128)}, u32[]{:S(2)}) copy-start(f32[2,512]{1,0:T(2,128)} %fusion.127) | copy-start | bytes 12292
  1139.9 57.9 %copy-start.98 = (f32[384]{0:T(512)S(1)}, f32[384]{0:T(512)}, u32[]{:S(2)}) copy-start(f32[384]{0:T(512)} %param.29) | copy-start | bytes 4612
  (104 other events, 459.3 us)
Sparse Core Ops, SparseCore 0:
  73.7 92.9 all-gather.3
  175.3 204.7 all-gather.5
  417.5 106.0 all-gather.7
